TPU v7x, 32 devices: a whole 2x2x4 slice. The times are simulated.
32 devices in a mesh: space: 4 (over z), scene: 8 (over y, x, core).
Axes of the slice: x: 2, y: 2, z: 4, core: 2. Of those that a mesh axis runs over, the one named last changes fastest.
Arguments:
- pixels: bfloat16 [16, 64, 64, 384], P('scene', 'space'), may hold values from -6 to 6
- dw_kernel: bfloat16 [7, 7, 384], replicated, may hold values from -0.875 to 0.875
- dw_bias: float32 [384], replicated, may hold values from -3 to 3
- norm_gain: float32 [384], replicated, may hold values from 0.25 to 1.75
- w_expand: bfloat16 [384, 1536], replicated, may hold values from -0.3125 to 0.3125
- w_reduce: bfloat16 [1536, 384], replicated, may hold values from -0.15625 to 0.15625
- layer_scale: float32 [384], replicated, may hold values from 0.3 to 1
- pixel_slot: int32 [16, 64, 64], P('scene', 'space'), may hold values from 0 to 63
- intersection: int32 [32, 64], P(('space', 'scene')), may hold values from 0 to 2047, as said below
- parcel_pos: int32 [2048], replicated, may hold values from 0 to 2047, as said below
- parcel_embed: bfloat16 [2048, 384], P(('space', 'scene')), may hold values from -6 to 6
- attn_gain: float32 [384], replicated, may hold values from 0.25 to 1.75
- w_qkv: bfloat16 [384, 1152], replicated, may hold values from -0.91855865 to 0.91855865
- w_out: bfloat16 [384, 384], replicated, may hold values from -0.3125 to 0.3125
- w_class: bfloat16 [384, 20], replicated, may hold values from -10.7165176 to 10.7165176
- labels: int32 [2048], P(('space', 'scene')), may hold values from 0 to 19
Outputs:
- features: bfloat16 [16, 64, 64, 384], P('scene', 'space')
- parcel_state: bfloat16 [2048, 384], P(('space', 'scene'))
- loss: float32 [2048], P(('space', 'scene'))
Inputs may be any that keep to these rules, and one draw needn't show every extreme that they name: `intersection`: row t lists 64 distinct parcels; each owner (positions o * 64 to o * 64 + 63) holds 1 to 3 of them, and in every tile some owner holds exactly 3. `parcel_pos`: each position occurs once.
All inputs are finite; a program needn't handle non-finite values.
Results may differ from a plain program's by a relative error of at most 0.035.
The roundings to bfloat16 on the way count: a program that leaves them out, or rounds other values in their place, can miss the bound.
Values may be sent and summed in bfloat16 or wider, within the bound.
No kernel may reach another device: no remote copies, remote signals or barrier semaphores. Data moves between devices by JAX's collectives and lax.ppermute only.
A program may use at most 128 MiB of HBM per device.

v0:
```python
import jax
import jax.numpy as jnp
from jax import lax
from jax.sharding import PartitionSpec as P

CAP = 3
PAR_DEV = 64
HEADS = 6
HEAD_DIM = 64


epsilon = 1e-06


def with_halo(x, sides, width):
    for axis, dim in sides:
        count, length = (lax.axis_size(axis), x.shape[dim])
        up = [(i, (i + 1) % count) for i in range(count - 1)]
        down = [(j, i) for i, j in up]
        last = lax.slice_in_dim(x, length - width, length, axis=dim)
        initial = lax.slice_in_dim(x, 0, width, axis=dim)
        before = lax.ppermute(last, axis, up)
        after = lax.ppermute(initial, axis, down)
        x = jnp.concatenate([before, x, after], axis=dim)
    return x


def layer_norm(values):
    average = jnp.mean(values, axis=-1, keepdims=True)
    centered = values - average
    return centered * lax.rsqrt(jnp.mean(centered * centered, axis=-1, keepdims=True) + epsilon)


def convnext_block(padded, center, dw_kernel, dw_bias, norm_gain, w_expand, w_reduce, layer_scale):
    height = center.shape[1]
    breadth = center.shape[2]
    kernel_f32 = dw_kernel.astype(jnp.float32)
    spatial = jnp.zeros(center.shape, jnp.float32)
    for row_off in range(dw_kernel.shape[0]):
        for col_off in range(dw_kernel.shape[1]):
            window = padded[:, row_off : row_off + height, col_off : col_off + breadth, :]
            spatial = spatial + window.astype(jnp.float32) * kernel_f32[row_off, col_off]
    spatial = spatial + dw_bias
    normed = (layer_norm(spatial) * norm_gain).astype(jnp.bfloat16)
    channels = center.shape[-1]
    flattened = normed.reshape(-1, channels)
    hidden = jax.nn.gelu(
        jnp.dot(flattened, w_expand, preferred_element_type=jnp.float32), approximate=False
    ).astype(jnp.bfloat16)
    branch = jnp.dot(hidden, w_reduce, preferred_element_type=jnp.float32).reshape(center.shape)
    return (center.astype(jnp.float32) + layer_scale * branch).astype(jnp.bfloat16)


def local(
    pixels,
    dw_kernel,
    dw_bias,
    norm_gain,
    w_expand,
    w_reduce,
    layer_scale,
    pixel_slot,
    intersection,
    parcel_pos,
    parcel_embed,
    attn_gain,
    w_qkv,
    w_out,
    w_class,
    labels,
):
    channels = pixels.shape[-1]
    highest = lax.Precision.HIGHEST
    extended = with_halo(pixels, (("space", 1),), 3)
    padded = jnp.pad(extended, ((0, 0), (0, 0), (3, 3), (0, 0)))
    features = convnext_block(
        padded, pixels, dw_kernel, dw_bias, norm_gain, w_expand, w_reduce, layer_scale
    )
    slot_total = intersection.shape[1]
    owners = lax.axis_size("space") * lax.axis_size("scene")
    slot_range = jnp.arange(slot_total, dtype=jnp.int32)
    membership = (slot_range[:, None] == pixel_slot.reshape(-1)[None, :]).astype(jnp.bfloat16)
    slot_sums = jnp.dot(
        membership, features.reshape(-1, channels), preferred_element_type=jnp.float32
    )
    slot_counts = jnp.sum(membership, axis=1, dtype=jnp.float32)
    positions = jnp.take(parcel_pos, intersection[0])
    owner_dev = positions // PAR_DEV
    local_row = (positions % PAR_DEV).astype(jnp.float32)
    earlier = (owner_dev[:, None] == owner_dev[None, :]) & (
        slot_range[None, :] < slot_range[:, None]
    )
    slot_rank = jnp.sum(earlier.astype(jnp.int32), axis=1)
    buffer_slot = owner_dev * CAP + slot_rank
    placer = (jnp.arange(owners * CAP, dtype=jnp.int32)[:, None] == buffer_slot[None, :]).astype(
        jnp.float32
    )
    sent_sums = jnp.dot(placer, slot_sums, precision=highest)
    sent_counts = jnp.dot(placer, slot_counts, precision=highest)
    sent_rows = jnp.dot(placer, local_row, precision=highest)
    arrived = (
        lax.all_to_all(
            sent_sums.reshape(owners, CAP, channels),
            ("space", "scene"),
            split_axis=0,
            concat_axis=0,
            tiled=True,
        ),
        lax.all_to_all(
            sent_counts.reshape(owners, CAP),
            ("space", "scene"),
            split_axis=0,
            concat_axis=0,
            tiled=True,
        ),
        lax.all_to_all(
            sent_rows.reshape(owners, CAP),
            ("space", "scene"),
            split_axis=0,
            concat_axis=0,
            tiled=True,
        ),
    )
    recv_sums = arrived[0].reshape(-1, channels)
    recv_counts = arrived[1].reshape(-1)
    recv_rows = arrived[2].reshape(-1)
    gather_table = (jnp.arange(PAR_DEV, dtype=jnp.float32)[:, None] == recv_rows[None, :]).astype(
        jnp.float32
    )
    parcel_sums = jnp.dot(gather_table, recv_sums, precision=highest)
    parcel_counts = jnp.dot(gather_table, recv_counts, precision=highest)
    tokens = parcel_sums / jnp.maximum(parcel_counts, 1.0)[:, None] + parcel_embed.astype(
        jnp.float32
    )
    attn_in = (layer_norm(tokens) * attn_gain).astype(jnp.bfloat16)
    queries = (
        jnp.dot(attn_in, w_qkv[:, :channels], preferred_element_type=jnp.float32)
        * HEAD_DIM ** (-0.5)
    ).astype(jnp.bfloat16)
    queries = queries.reshape(-1, HEADS, HEAD_DIM)
    w_pair = w_qkv[:, channels:]
    parcels_here = tokens.shape[0]
    key_value = jnp.dot(attn_in, w_pair, preferred_element_type=jnp.float32).astype(jnp.bfloat16)
    top_score = jnp.full((HEADS, parcels_here), -1e30, jnp.float32)
    key_heads = lax.all_gather(
        key_value[:, :channels], ("space", "scene"), axis=0, tiled=True
    ).reshape(-1, HEADS, HEAD_DIM)
    value_heads = lax.all_gather(
        key_value[:, channels:], ("space", "scene"), axis=0, tiled=True
    ).reshape(-1, HEADS, HEAD_DIM)
    scores = jnp.einsum("qhd,khd->hqk", queries, key_heads, preferred_element_type=jnp.float32)
    new_top = jnp.maximum(top_score, jnp.max(scores, axis=-1))
    weights = jnp.exp(scores - new_top[:, :, None])
    row_total = jnp.sum(weights, axis=-1)
    update = jnp.einsum(
        "hqk,khd->qhd",
        weights.astype(jnp.bfloat16),
        value_heads,
        preferred_element_type=jnp.float32,
    )
    weighted = update
    folded = (new_top, row_total, weighted)
    row_total = folded[1]
    weighted = folded[2]
    attended = (
        (weighted / jnp.transpose(row_total)[:, :, None])
        .reshape(parcels_here, channels)
        .astype(jnp.bfloat16)
    )
    parcel_out = tokens + jnp.dot(attended, w_out, preferred_element_type=jnp.float32)
    class_in = layer_norm(parcel_out).astype(jnp.bfloat16)
    logits = jnp.dot(class_in, w_class, preferred_element_type=jnp.float32)
    top_logit = jnp.max(logits, axis=-1, keepdims=True)
    log_total = top_logit[:, 0] + jnp.log(jnp.sum(jnp.exp(logits - top_logit), axis=-1))
    picked = jnp.sum(
        jnp.where(
            jnp.arange(logits.shape[1], dtype=jnp.int32)[None, :] == labels[:, None], logits, 0.0
        ),
        axis=-1,
    )
    return (features, parcel_out.astype(jnp.bfloat16), log_total - picked)


def solution(mesh):
    in_specs = (
        P("scene", "space", None, None),
        P(),
        P(),
        P(),
        P(),
        P(),
        P(),
        P("scene", "space", None),
        P(("space", "scene"), None),
        P(),
        P(("space", "scene"), None),
        P(),
        P(),
        P(),
        P(),
        P(("space", "scene")),
    )
    out_specs = (
        P("scene", "space", None, None),
        P(("space", "scene"), None),
        P(("space", "scene")),
    )
    return jax.shard_map(local, mesh=mesh, in_specs=in_specs, out_specs=out_specs, check_vma=False)
```

profile of v0, /device:TPU:1, one launch (start us, length us, event | category | flops | bytes accessed | tf_op | source)
XLA Modules:
  0.0 243.5 jit_solution(15093117531007774549)
XLA Ops:
  7.2 2.1 fusion.125
  9.3 4.0 %collective-permute-start = (bf16[2,3,64,384]{3,2,1,0:T(8,128)(2,1)}, bf16[2,3,64,384]{3,2,1,0:T(8,128)(2,1)S(1)}, u32[]{:S(2)}, u32[]{:S(2)}) collective-permute-start(bf16[2,3,64,384]{3,2,1,0:T(8,128)(2,1)} %get-tuple-element.58), channel_id=1, source_target_pairs={{0,8},{8,16},{16,24},{1,9},{9,17},{17,25},{2,10},{10,18},{18,26},{... | collective-permute-start | bytes 884744 | tf_op jit(solution)/shard_map/ppermute | solution.py:22
  13.3 1.3 collective-permute-start.1
  15.3 1.5 gather_fusion
  18.4 0.8 fusion.78
  20.0 7.6 %all-to-all-start = ((f32[32,1,3]{2,1,0:T(1,128)}), f32[32,1,3]{2,1,0:T(1,128)S(1)}, u32[]{:S(2)}, u32[]{:S(2)}) async-start(f32[32,1,3]{2,1,0:T(1,128)} %copy.34), calls=%async_computation | async-start | bytes 32768 | tf_op jit(solution)/shard_map/all_to_all | solution.py:116
  27.6 0.8 convert_element_type.208
  28.4 0.8 eq.112
  31.3 1.2 fusion.48
  32.6 23.7 %fusion.123 = (f32[2,16,64]{2,1,0:T(8,128)S(1)}, f32[2,16,64,384]{3,2,1,0:T(8,128)S(1)}) fusion(f32[384]{0:T(512)S(1)} %copy-done.7, f32[384]{0:T(512)S(1)} %get-tuple-element.4, bf16[2,22,70,384]{3,2,1,0:T(8,128)(2,1)S(1)} %fusion.48, f32[384]{0:T(512)S(1)} %get-tuple-element.5, f32[384]{0:T(512)S(1)} %get-tuple-element.6, f32[384]{0:T(512)S(1)} %get-tuple-element.7, ...), kind=kLoop, calls=%fused_computation.227 | loop fusion | flops 116389888 | bytes 80301056 | tf_op jit(solution)/shard_map/reduce_sum | solution.py:29
  57.0 1.6 multiply_convert_fusion
  58.6 32.0 %fusion.10 = f32[2048,384]{1,0:T(8,128)} fusion(bf16[1536,384]{1,0:T(8,128)(2,1)S(1)} %copy-done, bf16[2048,384]{1,0:T(8,128)(2,1)} %bitcast.67, bf16[384,1536]{1,0:T(8,128)(2,1)} %param.20), kind=kOutput, calls=%fused_computation.22 | convolution fusion | flops 5036310528 | bytes 7077888 | tf_op jit(solution)/shard_map/dot_general | solution.py:50
  90.7 2.4 fusion.40
  93.1 1.1 copy-done.3
  94.6 5.8 %all-to-all-start.2 = ((f32[32,1,3]{2,1,0:T(1,128)}), f32[32,1,3]{2,1,0:T(1,128)S(1)}, u32[]{:S(2)}, u32[]{:S(2)}) async-start(f32[32,1,3]{2,1,0:T(1,128)} %copy.35), calls=%async_computation.2 | async-start | bytes 32768 | tf_op jit(solution)/shard_map/all_to_all | solution.py:109
  101.4 5.7 %all-to-all-done.2 = f32[32,1,3]{2,1,0:T(1,128)S(1)} async-done(((f32[32,1,3]{2,1,0:T(1,128)}), f32[32,1,3]{2,1,0:T(1,128)S(1)}, u32[]{:S(2)}, u32[]{:S(2)}) %all-to-all-start.2) | async-done | bytes 416 | tf_op jit(solution)/shard_map/all_to_all | solution.py:109
  107.1 2.8 %all-to-all-start.1 = ((f32[32,3,384]{2,1,0:T(4,128)}), f32[32,3,384]{2,1,0:T(4,128)S(1)}, u32[]{:S(2)}, u32[]{:S(2)}) async-start(f32[32,3,384]{2,1,0:T(4,128)} %reshape.238), calls=%async_computation.1 | async-start | bytes 393216 | tf_op jit(solution)/shard_map/all_to_all | solution.py:102
  112.2 7.1 %all-to-all-done.1 = f32[32,3,384]{2,1,0:T(4,128)S(1)} async-done(((f32[32,3,384]{2,1,0:T(4,128)}), f32[32,3,384]{2,1,0:T(4,128)S(1)}, u32[]{:S(2)}, u32[]{:S(2)}) %all-to-all-start.1) | async-done | bytes 147488 | tf_op jit(solution)/shard_map/all_to_all | solution.py:102
  122.0 51.6 %all-gather.5.cloned.1.call-done = bf16[2048,384]{1,0:T(8,128)(2,1)} async-done(((bf16[64,384]{1,0:T(8,128)(2,1)}), bf16[2048,384]{1,0:T(8,128)(2,1)}) %all-gather.5.cloned.1.call-update) | async-done | bytes 1572880 | tf_op jit(solution)/shard_map/all_gather | solution.py:145
  173.7 1.7 copy.37
  176.0 1.7 copy-done.2
  178.2 52.2 %all-gather.3.cloned.1.call-done = bf16[2048,384]{1,0:T(8,128)(2,1)} async-done(((bf16[64,384]{1,0:T(8,128)(2,1)}), bf16[2048,384]{1,0:T(8,128)(2,1)}) %all-gather.3.cloned.1.call-update) | async-done | bytes 1572880 | tf_op jit(solution)/shard_map/all_gather | solution.py:148
  230.4 1.7 copy.36
  232.1 2.6 %fusion.58 = bf16[64,6,64]{0,2,1:T(8,128)(2,1)S(1)} fusion(bf16[2048,6,64]{0,2,1:T(8,128)(2,1)S(1)} %bitcast.65, f32[6,64,2048]{2,1,0:T(8,128)} %copy-done.2, f32[6,64]{1,0:T(8,128)S(1)} %broadcast_maximum_fusion, f32[64,6]{0,1:T(8,128)S(1)} %bitcast.69), kind=kOutput, calls=%fused_computation.68 | convolution fusion | flops 102285312 | bytes 4770816 | tf_op jit(solution)/shard_map/hqk,khd->qhd/dot_general | solution.py:155
  (82 shorter events, 15.1 us)
Async XLA Ops:
  7.2 51.4 %copy-start = (bf16[1536,384]{1,0:T(8,128)(2,1)S(1)}, bf16[1536,384]{1,0:T(8,128)(2,1)}, u32[]{:S(2)}) copy-start(bf16[1536,384]{1,0:T(8,128)(2,1)} %param.21) | copy-start | bytes 3538948
  7.2 23.5 %copy-start.1 = (bf16[2,16,64,384]{3,2,1,0:T(8,128)(2,1)S(1)}, bf16[2,16,64,384]{3,2,1,0:T(8,128)(2,1)}, u32[]{:S(2)}) copy-start(bf16[2,16,64,384]{3,2,1,0:T(8,128)(2,1)} %param.16) | copy-start | bytes 4718596
  9.3 21.3 %collective-permute-start = (bf16[2,3,64,384]{3,2,1,0:T(8,128)(2,1)}, bf16[2,3,64,384]{3,2,1,0:T(8,128)(2,1)S(1)}, u32[]{:S(2)}, u32[]{:S(2)}) collective-permute-start(bf16[2,3,64,384]{3,2,1,0:T(8,128)(2,1)} %get-tuple-element.58), channel_id=1, source_target_pairs={{0,8},{8,16},{16,24},{1,9},{9,17},{17,25},{2,10},{10,18},{18,26},{... | collective-permute-start | bytes 884744 | tf_op jit(solution)/shard_map/ppermute | solution.py:22
  13.3 18.0 %collective-permute-start.1 = (bf16[2,3,64,384]{3,2,1,0:T(8,128)(2,1)}, bf16[2,3,64,384]{3,2,1,0:T(8,128)(2,1)S(1)}, u32[]{:S(2)}, u32[]{:S(2)}) collective-permute-start(bf16[2,3,64,384]{3,2,1,0:T(8,128)(2,1)} %get-tuple-element.59), channel_id=1, source_target_pairs={{8,0},{16,8},{24,16},{9,1},{17,9},{25,17},{10,2},{18,10},{26,18},{... | collective-permute-start | bytes 884744 | tf_op jit(solution)/shard_map/ppermute | solution.py:23
  20.0 74.6 %all-to-all-start = ((f32[32,1,3]{2,1,0:T(1,128)}), f32[32,1,3]{2,1,0:T(1,128)S(1)}, u32[]{:S(2)}, u32[]{:S(2)}) async-start(f32[32,1,3]{2,1,0:T(1,128)} %copy.34), calls=%async_computation | async-start | bytes 32768 | tf_op jit(solution)/shard_map/all_to_all | solution.py:116
  31.3 1.3 copy-start.7
  56.3 0.7 copy-start.8
  58.6 32.1 %copy-start.9 = (f32[384]{0:T(512)S(1)}, f32[384]{0:T(512)}, u32[]{:S(2)}) copy-start(f32[384]{0:T(512)} %param.22) | copy-start | bytes 4612
  93.1 1.1 copy-start.3
  93.1 26.3 %copy-start.12 = (bf16[64,384]{1,0:T(8,128)(2,1)S(1)}, bf16[64,384]{1,0:T(8,128)(2,1)}, u32[]{:S(2)}) copy-start(bf16[64,384]{1,0:T(8,128)(2,1)} %param.26) | copy-start | bytes 147460
  93.1 26.8 %copy-start.4 = (bf16[384,1152]{1,0:T(8,128)(2,1)S(1)}, bf16[384,1152]{1,0:T(8,128)(2,1)}, u32[]{:S(2)}) copy-start(bf16[384,1152]{1,0:T(8,128)(2,1)} %param.28) | copy-start | bytes 2654212
  93.1 26.8 %copy-start.10 = (f32[384]{0:T(512)S(1)}, f32[384]{0:T(512)}, u32[]{:S(2)}) copy-start(f32[384]{0:T(512)} %param.27) | copy-start | bytes 4612
  94.6 12.5 %all-to-all-start.2 = ((f32[32,1,3]{2,1,0:T(1,128)}), f32[32,1,3]{2,1,0:T(1,128)S(1)}, u32[]{:S(2)}, u32[]{:S(2)}) async-start(f32[32,1,3]{2,1,0:T(1,128)} %copy.35), calls=%async_computation.2 | async-start | bytes 32768 | tf_op jit(solution)/shard_map/all_to_all | solution.py:109
  107.1 12.2 %all-to-all-start.1 = ((f32[32,3,384]{2,1,0:T(4,128)}), f32[32,3,384]{2,1,0:T(4,128)S(1)}, u32[]{:S(2)}, u32[]{:S(2)}) async-start(f32[32,3,384]{2,1,0:T(4,128)} %reshape.238), calls=%async_computation.1 | async-start | bytes 393216 | tf_op jit(solution)/shard_map/all_to_all | solution.py:102
  110.0 63.7 %all-gather.5.cloned.1.call-start = ((), (), s32[]{:S(2)}) async-start(), calls=%async_computation.4 | async-start | bytes 1622016 | tf_op jit(solution)/shard_map/all_gather | solution.py:145
  120.9 109.5 %all-gather.3.cloned.1.call-start = ((), (), s32[]{:S(2)}) async-start(), calls=%async_computation.3 | async-start | bytes 1622016 | tf_op jit(solution)/shard_map/all_gather | solution.py:148
  176.0 1.7 copy-start.2
  232.1 2.7 %copy-start.5 = (bf16[384,384]{1,0:T(8,128)(2,1)S(1)}, bf16[384,384]{1,0:T(8,128)(2,1)}, u32[]{:S(2)}) copy-start(bf16[384,384]{1,0:T(8,128)(2,1)} %param.29) | copy-start | bytes 884740
  232.1 3.8 %copy-start.6 = (bf16[384,20]{0,1:T(8,128)(2,1)S(1)}, bf16[384,20]{0,1:T(8,128)(2,1)}, u32[]{:S(2)}) copy-start(bf16[384,20]{0,1:T(8,128)(2,1)} %param.30) | copy-start | bytes 46084
  232.1 4.0 %copy-start.11 = (s32[64]{0:T(128)S(1)}, s32[64]{0:T(128)}, u32[]{:S(2)}) copy-start(s32[64]{0:T(128)} %param.31) | copy-start | bytes 772
Sparse Core Ops, SparseCore 0:
  121.0 52.6 all-gather.4
  176.5 53.8 all-gather.2
where the time goes:
time: 244 us
  waiting for transfers between devices  117 us (48%)
  matrix products  38.3 us (16%)
  other arithmetic  36.2 us (15%)
  starting transfers between devices  21.7 us (9%)
  local copies, waits for them, and re-layouts  15.5 us (6%)
  between operations  14.5 us (6%)
    all_gather x1, waiting for transfers between devices, local(): lax.all_gather(key_value[:, channels:], ('space', 'scene'), axis=0, tiled...  52.2 us
    all_gather x1, waiting for transfers between devices, local(): lax.all_gather(key_value[:, :channels], ('space', 'scene'), axis=0, tiled...  51.6 us
    dot_general x1, matrix products, convnext_block(): jnp.dot(hidden, w_reduce, preferred_element_type=jnp.float32)  32 us
    reduce_sum x1, other arithmetic, layer_norm(): average = jnp.mean(values, axis=-1, keepdims=True)  23.7 us
    all_to_all x1, starting transfers between devices, local(): lax.all_to_all(sent_rows.reshape(owners, CAP), ('space', 'scene'), split_...  7.61 us
    all_to_all x1, waiting for transfers between devices, local(): lax.all_to_all(sent_sums.reshape(owners, CAP, channels), ('space', 'scene...  7.08 us
    all_to_all x1, starting transfers between devices, local(): lax.all_to_all(sent_counts.reshape(owners, CAP), ('space', 'scene'), spli...  5.83 us
    all_to_all x1, waiting for transfers between devices, local(): lax.all_to_all(sent_counts.reshape(owners, CAP), ('space', 'scene'), spli...  5.74 us
  transfers between devices with their start and end apart: 7, of which 4 were waited for; matrix products, arithmetic and copies ran while one was open for 32% of the time, Pallas kernels for 0%

commit v1 on v0

v1 whole, which is shorter than its diff:
```python
import functools

import jax
import jax.numpy as jnp
from jax import lax
from jax.experimental import pallas as pl
from jax.experimental.pallas import tpu as pltpu
from jax.sharding import PartitionSpec as P

CAP = 3
PAR_DEV = 64
HEADS = 6
HEAD_DIM = 64
BLOCK_ROWS = 4
MARGIN = 8
LANES = 128
EPS = 1e-06
VMEM_LIMIT = 56 * 1024 * 1024
AXES = ("space", "scene")
HIGHEST = lax.Precision.HIGHEST

ERF_Q = (
    0.7978842161181501,
    0.03633428350265726,
    -3.312998427216715e-05,
    -5.524016139049459e-05,
    3.969109860672752e-06,
    -1.334464341485976e-07,
    1.8056169652228524e-09,
)
ERF_U = 30.25


def gelu(x):
    u = jnp.minimum(x * x, ERF_U)
    q = jnp.full_like(u, ERF_Q[-1])
    for coef in ERF_Q[-2::-1]:
        q = q * u + coef
    half = 0.5 * x
    return half + half * jnp.tanh(x * q)


def layer_norm(values):
    average = jnp.mean(values, axis=-1, keepdims=True)
    centered = values - average
    return centered * lax.rsqrt(jnp.mean(centered * centered, axis=-1, keepdims=True) + EPS)


def to_column(row, rows):
    n = row.shape[1]
    same = lax.broadcasted_iota(jnp.int32, (n, n), 0) == lax.broadcasted_iota(jnp.int32, (n, n), 1)
    return jnp.sum(jnp.where(same, jnp.broadcast_to(row, (n, n)), 0), axis=1, keepdims=True)


def to_row(column):
    n = column.shape[0]
    same = lax.broadcasted_iota(jnp.int32, (n, n), 0) == lax.broadcasted_iota(jnp.int32, (n, n), 1)
    return jnp.sum(jnp.where(same, jnp.broadcast_to(column, (n, n)), 0), axis=0, keepdims=True)


def conv_block(source, slab, spat, wb, bias_ref, width):
    chans = spat.shape[1]
    blocks = chans // LANES
    ksz = len(source) - BLOCK_ROWS + 1
    reach = ksz // 2
    for i, row in enumerate(source):
        value = row().astype(jnp.float32)
        for cb in range(blocks):
            slab[cb, i, MARGIN : MARGIN + width, :] = value[:, cb * LANES : (cb + 1) * LANES]
    step = 16
    for cb in range(blocks):
        lane = slice(cb * LANES, (cb + 1) * LANES)
        bias = bias_ref[0:1, lane]
        for col in range(0, width, step):
            total = jnp.zeros((BLOCK_ROWS, step, LANES), jnp.float32)
            for b in range(ksz):
                start = MARGIN - reach + b + col
                for a in range(ksz):
                    tap = wb[cb, a * ksz + b]
                    window = slab[cb, a : a + BLOCK_ROWS, start : start + step, :]
                    total = total + window * jnp.concatenate([tap] * (step // 8), axis=0)[None]
            for r in range(BLOCK_ROWS):
                spat[r * width + col : r * width + col + step, lane] = total[r] + bias


def mlp_block(spat, gain_ref, we_ref, wr_ref, scale_ref, center):
    normed = (layer_norm(spat[...]) * gain_ref[...]).astype(jnp.bfloat16)
    hid = we_ref.shape[1]
    chunk = min(512, hid)
    branch = None
    for start in range(0, hid, chunk):
        pre = jnp.dot(normed, we_ref[:, start : start + chunk], preferred_element_type=jnp.float32)
        part = jnp.dot(
            gelu(pre).astype(jnp.bfloat16),
            wr_ref[start : start + chunk, :],
            preferred_element_type=jnp.float32,
        )
        branch = part if branch is None else branch + part
    return (center.astype(jnp.float32) + scale_ref[...] * branch).astype(jnp.bfloat16)


def prepare(slab, wb, dwk_ref, width):
    slab[:, :, 0:MARGIN, :] = jnp.zeros(slab.shape[:2] + (MARGIN, LANES), jnp.float32)
    slab[:, :, MARGIN + width :, :] = jnp.zeros(slab.shape[:2] + (MARGIN, LANES), jnp.float32)
    taps = dwk_ref.shape[0]
    kernel = dwk_ref[...].astype(jnp.float32)
    for cb in range(wb.shape[0]):
        for t in range(taps):
            wb[cb, t] = jnp.broadcast_to(
                kernel[t : t + 1, cb * LANES : (cb + 1) * LANES], (8, LANES)
            )


def pool(member, feats, sums_ref, counts_ref):
    sums_ref[...] += jnp.dot(member, feats, preferred_element_type=jnp.float32)
    ones = jnp.ones((member.shape[1], LANES), jnp.bfloat16)
    counts_ref[...] += jnp.dot(member, ones, preferred_element_type=jnp.float32)


def membership(slot_ref, scene, row0, width, slots):
    pieces = []
    for r in range(BLOCK_ROWS):
        one = slot_ref[scene, pl.ds(row0 + r, 1), :]
        index = lax.broadcasted_iota(jnp.int32, (slots, width), 0)
        pieces.append((index == one).astype(jnp.float32).astype(jnp.bfloat16))
    return jnp.concatenate(pieces, axis=1)


def inner_kernel(
    rows, slots, x_ref, slot_ref, dwk_ref, bias_ref, gain_ref, we_ref, wr_ref, scale_ref,
    feat_ref, sums_ref, counts_ref, slab, spat, wb,
):
    width = x_ref.shape[2]
    scene = pl.program_id(0)
    ksz = slab.shape[1] - BLOCK_ROWS + 1
    reach = ksz // 2

    @pl.when(scene == 0)
    def _():
        prepare(slab, wb, dwk_ref, width)
        sums_ref[...] = jnp.zeros_like(sums_ref)
        counts_ref[...] = jnp.zeros_like(counts_ref)

    for n, row0 in enumerate(range(BLOCK_ROWS, rows - BLOCK_ROWS, BLOCK_ROWS)):
        source = [
            functools.partial(lambda r: x_ref[scene, r], row0 - reach + i)
            for i in range(BLOCK_ROWS + ksz - 1)
        ]
        conv_block(source, slab, spat, wb, bias_ref, width)
        center = x_ref[scene, row0 : row0 + BLOCK_ROWS].reshape(BLOCK_ROWS * width, -1)
        feats = mlp_block(spat, gain_ref, we_ref, wr_ref, scale_ref, center)
        feat_ref[scene, row0 : row0 + BLOCK_ROWS] = feats.reshape(BLOCK_ROWS, width, -1)
        pool(membership(slot_ref, scene, row0, width, slots), feats, sums_ref, counts_ref)


def edge_kernel(
    rows, slots, owners, x_ref, top_ref, bot_ref, slot_ref, dwk_ref, bias_ref, gain_ref, we_ref,
    wr_ref, scale_ref, feat_in, sums_in, counts_in, inter_ref, pos_ref,
    feat_ref, sent_ref, slab, spat, wb, sums_ref, counts_ref,
):
    width = x_ref.shape[2]
    scene = pl.program_id(0)
    ksz = slab.shape[1] - BLOCK_ROWS + 1
    reach = ksz // 2

    @pl.when(scene == 0)
    def _():
        prepare(slab, wb, dwk_ref, width)
        sums_ref[...] = sums_in[...]
        counts_ref[...] = counts_in[...]
        feat_ref[:, BLOCK_ROWS : rows - BLOCK_ROWS] = feat_in[:, BLOCK_ROWS : rows - BLOCK_ROWS]

    for row0 in (0, rows - BLOCK_ROWS):
        source = []
        for i in range(BLOCK_ROWS + ksz - 1):
            r = row0 - reach + i
            if r < 0:
                source.append(functools.partial(lambda r: top_ref[scene, r], r + reach))
            elif r >= rows:
                source.append(functools.partial(lambda r: bot_ref[scene, r], r - rows))
            else:
                source.append(functools.partial(lambda r: x_ref[scene, r], r))
        conv_block(source, slab, spat, wb, bias_ref, width)
        center = x_ref[scene, row0 : row0 + BLOCK_ROWS].reshape(BLOCK_ROWS * width, -1)
        feats = mlp_block(spat, gain_ref, we_ref, wr_ref, scale_ref, center)
        feat_ref[scene, row0 : row0 + BLOCK_ROWS] = feats.reshape(BLOCK_ROWS, width, -1)
        pool(membership(slot_ref, scene, row0, width, slots), feats, sums_ref, counts_ref)

    @pl.when(scene == pl.num_programs(0) - 1)
    def _():
        parcels = pos_ref.shape[1]
        listed = to_column(inter_ref[...], slots)
        number = lax.broadcasted_iota(jnp.int32, (slots, parcels), 1)
        position = jnp.sum(
            jnp.where(number == listed, jnp.broadcast_to(pos_ref[...], (slots, parcels)), 0),
            axis=1, keepdims=True,
        )
        owner = position // PAR_DEV
        owner_row = to_row(owner)
        this = lax.broadcasted_iota(jnp.int32, (slots, slots), 0)
        other = lax.broadcasted_iota(jnp.int32, (slots, slots), 1)
        rank = jnp.sum(
            jnp.where((owner == owner_row) & (other < this), 1, 0), axis=1, keepdims=True
        )
        place = to_row(rank * owners + owner)
        place_index = lax.broadcasted_iota(jnp.int32, (CAP * owners, slots), 0)
        placer = (place_index == place).astype(jnp.float32)
        sent = jnp.dot(placer, sums_ref[...], precision=HIGHEST, preferred_element_type=jnp.float32)
        local_row = (position - owner * PAR_DEV).astype(jnp.float32)
        lane = lax.broadcasted_iota(jnp.int32, (slots, LANES), 1)
        counts_rows = jnp.where(lane < CAP, counts_ref[...], jnp.broadcast_to(local_row, (slots, LANES)))
        meta = jnp.dot(placer, counts_rows, precision=HIGHEST, preferred_element_type=jnp.float32)
        chans = sent.shape[1]
        lane = lax.broadcasted_iota(jnp.int32, (owners, LANES), 1)
        packed = jnp.zeros((owners, LANES), jnp.float32)
        for k in range(CAP):
            sent_ref[:, k * chans : (k + 1) * chans] = sent[k * owners : (k + 1) * owners]
            packed = jnp.where(
                (lane == k) | (lane == CAP + k), meta[k * owners : (k + 1) * owners], packed
            )
        sent_ref[:, CAP * chans :] = packed


def owner_kernel(recv_ref, embed_ref, gain_ref, tokens_ref, attn_ref):
    chans = embed_ref.shape[1]
    meta = recv_ref[:, CAP * chans :]
    tiles = recv_ref.shape[0]
    sums = jnp.zeros(tokens_ref.shape, jnp.float32)
    counts = jnp.zeros((PAR_DEV, LANES), jnp.float32)
    index = lax.broadcasted_iota(jnp.int32, (PAR_DEV, tiles), 0).astype(jnp.float32)
    for k in range(CAP):
        rows = jnp.broadcast_to(meta[:, CAP + k : CAP + k + 1], (tiles, LANES)).T[0:1, :]
        table = (index == rows).astype(jnp.float32)
        sums += jnp.dot(
            table, recv_ref[:, k * chans : (k + 1) * chans],
            precision=HIGHEST, preferred_element_type=jnp.float32,
        )
        many = jnp.broadcast_to(meta[:, k : k + 1], (tiles, LANES))
        counts += jnp.dot(table, many, precision=HIGHEST, preferred_element_type=jnp.float32)
    tokens = sums / jnp.maximum(counts[:, :1], 1.0) + embed_ref[...].astype(jnp.float32)
    tokens_ref[...] = tokens
    attn_ref[...] = (layer_norm(tokens) * gain_ref[...]).astype(jnp.bfloat16)


def attend_kernel(
    tokens_ref, own_ref, all_ref, wqkv_ref, wout_ref, wclass_ref, labels_ref,
    state_ref, loss_ref, keys, values,
):
    chans = own_ref.shape[1]
    parcels = all_ref.shape[0]
    chunk = min(512, parcels)
    for start in range(0, parcels, chunk):
        part = all_ref[start : start + chunk]
        keys[start : start + chunk] = jnp.dot(
            part, wqkv_ref[:, chans : 2 * chans], preferred_element_type=jnp.float32
        ).astype(jnp.bfloat16)
        values[start : start + chunk] = jnp.dot(
            part, wqkv_ref[:, 2 * chans :], preferred_element_type=jnp.float32
        ).astype(jnp.bfloat16)
    queries = (
        jnp.dot(own_ref[...], wqkv_ref[:, :chans], preferred_element_type=jnp.float32)
        * HEAD_DIM ** (-0.5)
    )
    here = queries.shape[0]
    outs = []
    lane = lax.broadcasted_iota(jnp.int32, (here, chans), 1)
    for h in range(HEADS):
        mask = (lane >= h * HEAD_DIM) & (lane < (h + 1) * HEAD_DIM)
        q = jnp.where(mask, queries, 0.0).astype(jnp.bfloat16)
        scores = lax.dot_general(
            q, keys[...], (((1,), (1,)), ((), ())), preferred_element_type=jnp.float32
        )
        top = jnp.max(scores, axis=1, keepdims=True)
        weights = jnp.exp(scores - top)
        total = jnp.sum(weights, axis=1, keepdims=True)
        mixed = jnp.dot(
            weights.astype(jnp.bfloat16), values[...], preferred_element_type=jnp.float32
        )
        outs.append(jnp.where(mask, mixed / total, 0.0))
    attended = functools.reduce(lambda a, b: a + b, outs).astype(jnp.bfloat16)
    state = tokens_ref[...] + jnp.dot(
        attended, wout_ref[...], preferred_element_type=jnp.float32
    )
    state_ref[...] = state.astype(jnp.bfloat16)
    class_in = layer_norm(state).astype(jnp.bfloat16)
    logits = jnp.dot(class_in, wclass_ref[...], preferred_element_type=jnp.float32)
    top = jnp.max(logits, axis=1, keepdims=True)
    log_total = top + jnp.log(jnp.sum(jnp.exp(logits - top), axis=1, keepdims=True))
    number = lax.broadcasted_iota(jnp.int32, logits.shape, 1)
    label = to_column(labels_ref[...], here)
    picked = jnp.sum(jnp.where(number == label, logits, 0.0), axis=1, keepdims=True)
    loss = jnp.broadcast_to(log_total - picked, (here, here))
    same = lax.broadcasted_iota(jnp.int32, (here, here), 0) == lax.broadcasted_iota(
        jnp.int32, (here, here), 1
    )
    loss_ref[...] = jnp.sum(jnp.where(same, loss, 0.0), axis=0, keepdims=True)


VM = pl.BlockSpec(memory_space=pltpu.VMEM)


def params():
    return pltpu.CompilerParams(vmem_limit_bytes=VMEM_LIMIT)


def xor_permute(x, axis, mask, count):
    return lax.ppermute(x, axis, [(i, i ^ mask) for i in range(count)])


def gather_blocks(x):
    for axis in AXES:
        count = lax.axis_size(axis)
        bits = count.bit_length() - 1
        while bits > 0:
            low = max(bits - 2, 0)
            masks = [m << low for m in range(1, 1 << (bits - low))]
            x = jnp.concatenate([x] + [xor_permute(x, axis, m, count) for m in masks], axis=0)
            bits = low
    return x


def local(
    pixels, dw_kernel, dw_bias, norm_gain, w_expand, w_reduce, layer_scale, pixel_slot,
    intersection, parcel_pos, parcel_embed, attn_gain, w_qkv, w_out, w_class, labels,
):
    scenes, rows, width, chans = pixels.shape
    ksz = dw_kernel.shape[0]
    reach = ksz // 2
    slots = intersection.shape[1]
    owners = lax.axis_size("space") * lax.axis_size("scene")
    count = lax.axis_size("space")
    up = [(i, i + 1) for i in range(count - 1)]
    down = [(i + 1, i) for i in range(count - 1)]
    top = lax.ppermute(pixels[:, rows - reach :], "space", up)
    bottom = lax.ppermute(pixels[:, :reach], "space", down)

    taps = dw_kernel.reshape(ksz * ksz, chans)
    bias = dw_bias.reshape(1, chans)
    gain = norm_gain.reshape(1, chans)
    scale = layer_scale.reshape(1, chans)
    slab = pltpu.VMEM((chans // LANES, BLOCK_ROWS + ksz - 1, width + 2 * MARGIN, LANES), jnp.float32)
    spat = pltpu.VMEM((BLOCK_ROWS * width, chans), jnp.float32)
    wb = pltpu.VMEM((chans // LANES, ksz * ksz, 8, LANES), jnp.float32)
    work = 2 * rows * width * chans * (ksz * ksz + 2 * w_expand.shape[1])
    feats, sums, counts = pl.pallas_call(
        functools.partial(inner_kernel, rows, slots),
        grid=(scenes,),
        out_shape=(
            jax.ShapeDtypeStruct(pixels.shape, jnp.bfloat16),
            jax.ShapeDtypeStruct((slots, chans), jnp.float32),
            jax.ShapeDtypeStruct((slots, LANES), jnp.float32),
        ),
        in_specs=[VM] * 8,
        out_specs=(VM, VM, VM),
        scratch_shapes=[slab, spat, wb],
        compiler_params=params(),
        cost_estimate=pl.CostEstimate(flops=work, bytes_accessed=6 << 20, transcendentals=0),
        name="inner_rows",
    )(pixels, pixel_slot, taps, bias, gain, w_expand, w_reduce, scale)
    features, sent = pl.pallas_call(
        functools.partial(edge_kernel, rows, slots, owners),
        grid=(scenes,),
        out_shape=(
            jax.ShapeDtypeStruct(pixels.shape, jnp.bfloat16),
            jax.ShapeDtypeStruct((owners, CAP * chans + LANES), jnp.float32),
        ),
        in_specs=[VM] * 15,
        out_specs=(VM, VM),
        scratch_shapes=[
            slab, spat, wb,
            pltpu.VMEM((slots, chans), jnp.float32),
            pltpu.VMEM((slots, LANES), jnp.float32),
        ],
        compiler_params=params(),
        cost_estimate=pl.CostEstimate(flops=work, bytes_accessed=6 << 20, transcendentals=0),
        name="edge_rows",
    )(
        pixels, top, bottom, pixel_slot, taps, bias, gain, w_expand, w_reduce, scale,
        feats, sums, counts, intersection, parcel_pos.reshape(1, -1),
    )
    wide = sent.shape[1]
    arrived = lax.all_to_all(
        sent.reshape(owners, 1, wide), AXES, split_axis=0, concat_axis=0, tiled=True
    ).reshape(owners, wide)
    tokens, attn_in = pl.pallas_call(
        owner_kernel,
        out_shape=(
            jax.ShapeDtypeStruct((PAR_DEV, chans), jnp.float32),
            jax.ShapeDtypeStruct((PAR_DEV, chans), jnp.bfloat16),
        ),
        in_specs=[VM] * 3,
        out_specs=(VM, VM),
        compiler_params=params(),
        name="own_tokens",
    )(arrived, parcel_embed, attn_gain.reshape(1, chans))
    everyone = gather_blocks(attn_in)
    parcels = everyone.shape[0]
    state, loss = pl.pallas_call(
        attend_kernel,
        out_shape=(
            jax.ShapeDtypeStruct((PAR_DEV, chans), jnp.bfloat16),
            jax.ShapeDtypeStruct((1, PAR_DEV), jnp.float32),
        ),
        in_specs=[VM] * 7,
        out_specs=(VM, VM),
        scratch_shapes=[
            pltpu.VMEM((parcels, chans), jnp.bfloat16),
            pltpu.VMEM((parcels, chans), jnp.bfloat16),
        ],
        compiler_params=params(),
        name="attend",
    )(tokens, attn_in, everyone, w_qkv, w_out, w_class, labels.reshape(1, -1))
    return features, state, loss.reshape(-1)


def solution(mesh):
    in_specs = (
        P("scene", "space", None, None),
        P(), P(), P(), P(), P(), P(),
        P("scene", "space", None),
        P(AXES, None),
        P(),
        P(AXES, None),
        P(), P(), P(), P(),
        P(AXES),
    )
    out_specs = (P("scene", "space", None, None), P(AXES, None), P(AXES))
    return jax.shard_map(local, mesh=mesh, in_specs=in_specs, out_specs=out_specs, check_vma=False)
```

time: 244 us -> 108 us (0.44)
  waiting for transfers between devices: 117 us -> 17.9 us
  Pallas kernels: 0 us -> 52.4 us
  matrix products: 38.3 us -> 0 us
  other arithmetic: 36.2 us -> 0 us
  between operations: 14.5 us -> 0.74 us
    all_gather x2 -> x0, waiting for transfers between devices: 104 us -> none  [the longest x1 52.2 us: local(): lax.all_gather(key_value[:, channels:], ('space', 'scene'), axis=0, tiled...]
    pallas_call x0 -> x4, Pallas kernels: none -> 52.4 us  [the longest x1 20.6 us: local(): pl.pallas_call(functools.partial(edge_kernel, rows, slots, owners), grid=...]
    dot_general x13 -> x0, matrix products: 38.3 us -> none  [the longest x1 32 us: convnext_block(): jnp.dot(hidden, w_reduce, preferred_element_type=jnp.float32)]
    reduce_sum x8 -> x0, other arithmetic: 26.2 us -> none  [the longest x1 23.7 us: layer_norm(): average = jnp.mean(values, axis=-1, keepdims=True)]
    ppermute x2 -> x9, starting transfers between devices: 5.33 us -> 15.4 us  [the longest x7 10 us: xor_permute(): return lax.ppermute(x, axis, [(i, i ^ mask) for i in range(count)])]
    ppermute x2 -> x9, waiting for transfers between devices: 0.01 us -> 9.78 us  [the longest x7 9.77 us: xor_permute(): return lax.ppermute(x, axis, [(i, i ^ mask) for i in range(count)])]
    all_to_all x3 -> x1, starting transfers between devices: 16.3 us -> 7.62 us  [local(): lax.all_to_all(sent.reshape(owners, 1, wide), AXES, split_axis=0, concat_...]
    reshape x4 -> x6, local copies, waits for them, and re-layouts: 1.04 us -> 7.47 us  [the longest x1 1.75 us: local(): sent.reshape(owners, 1, wide)]
  transfers between devices with their start and end apart: 7 -> 10, of which waited for: 4 -> 7; matrix products, arithmetic and copies ran while one was open for 32% -> 7% of each run, Pallas kernels for 0% -> 18%
where the time goes in v1:
time: 108 us; the launch traced here: 107 us
  Pallas kernels  52.4 us (49%)
  starting transfers between devices  23 us (21%)
  waiting for transfers between devices  17.9 us (17%)
  local copies, waits for them, and re-layouts  13.3 us (12%)
    pallas_call x1, Pallas kernels, local(): pl.pallas_call(functools.partial(edge_kernel, rows, slots, owners), grid=...  20.6 us
    pallas_call x1, Pallas kernels, local(): pl.pallas_call(functools.partial(inner_kernel, rows, slots), grid=(scenes...  18.8 us
    pallas_call x1, Pallas kernels, local(): pl.pallas_call(attend_kernel, out_shape=(jax.ShapeDtypeStruct((PAR_DEV, c...  10.5 us
    ppermute x7, starting transfers between devices, xor_permute(): return lax.ppermute(x, axis, [(i, i ^ mask) for i in range(count)])  10 us
    ppermute x7, waiting for transfers between devices, xor_permute(): return lax.ppermute(x, axis, [(i, i ^ mask) for i in range(count)])  9.77 us
    all_to_all x1, waiting for transfers between devices, local(): lax.all_to_all(sent.reshape(owners, 1, wide), AXES, split_axis=0, concat_...  8.11 us
    all_to_all x1, starting transfers between devices, local(): lax.all_to_all(sent.reshape(owners, 1, wide), AXES, split_axis=0, concat_...  7.62 us
    unnamed x18, local copies, waits for them, and re-layouts  4.47 us
  transfers between devices with their start and end apart: 10, of which 7 were waited for; matrix products, arithmetic and copies ran while one was open for 7% of the time, Pallas kernels for 18%

profile of v1, /device:TPU:1, one launch (start us, length us, event | category | flops | bytes accessed | tf_op | source)
XLA Modules:
  0.0 107.3 jit_solution(13247921168542199383)
XLA Ops:
  0.6 1.1 %fusion = (bf16[2,3,64,384]{3,2,1,0:T(8,128)(2,1)S(1)}, bf16[2,3,64,384]{3,2,1,0:T(8,128)(2,1)S(1)}) fusion(bf16[2,16,64,384]{3,2,1,0:T(8,128)(2,1)} %x_ref.3), kind=kLoop, calls=%fused_computation.20 | loop fusion | bytes 1179648 | tf_op jit(solution)/shard_map/slice | solution.py:335
  1.8 4.0 %collective-permute-start = (bf16[2,3,64,384]{3,2,1,0:T(8,128)(2,1)S(1)}, bf16[2,3,64,384]{3,2,1,0:T(8,128)(2,1)S(1)}, u32[]{:S(2)}, u32[]{:S(2)}) collective-permute-start(bf16[2,3,64,384]{3,2,1,0:T(8,128)(2,1)S(1)} %get-tuple-element.22), channel_id=1, source_target_pairs={{0,8},{8,16},{16,24},{1,9},{9,17},{17,25},{2,10},{10,18},{18,26},{... | collective-permute-start | bytes 884744 | tf_op jit(solution)/shard_map/ppermute | solution.py:334
  5.8 1.3 %collective-permute-start.1 = (bf16[2,3,64,384]{3,2,1,0:T(8,128)(2,1)S(1)}, bf16[2,3,64,384]{3,2,1,0:T(8,128)(2,1)S(1)}, u32[]{:S(2)}, u32[]{:S(2)}) collective-permute-start(bf16[2,3,64,384]{3,2,1,0:T(8,128)(2,1)S(1)} %get-tuple-element.21), channel_id=1, source_target_pairs={{8,0},{16,8},{24,16},{9,1},{17,9},{25,17},{10,2},{18,10},{26,18},{... | collective-permute-start | bytes 884744 | tf_op jit(solution)/shard_map/ppermute | solution.py:335
  7.1 1.4 %reshape.36.dwk_ref = bf16[49,384]{1,0:T(8,128)(2,1)} reshape(bf16[7,7,384]{2,1,0:T(8,128)(2,1)} %param.17) | data formatting | bytes 75264 | tf_op jit(solution)/shard_map/reshape | solution.py:337
  8.5 1.2 %reshape.37.bias_ref = f32[1,384]{1,0:T(1,128)} reshape(f32[384]{0:T(512)} %param.18) | data formatting | bytes 3072 | tf_op jit(solution)/shard_map/reshape | solution.py:338
  9.8 1.3 %reshape.38.gain_ref = f32[1,384]{1,0:T(1,128)} reshape(f32[384]{0:T(512)} %param.19) | data formatting | bytes 3072 | tf_op jit(solution)/shard_map/reshape | solution.py:339
  11.0 1.2 %reshape.39.scale_ref = f32[1,384]{1,0:T(1,128)} reshape(f32[384]{0:T(512)} %param.22) | data formatting | bytes 3072 | tf_op jit(solution)/shard_map/reshape | solution.py:340
  12.3 18.8 %inner_rows.1 = (bf16[2,16,64,384]{3,2,1,0:T(8,128)(2,1)}, f32[64,384]{1,0:T(8,128)}, f32[64,128]{1,0:T(8,128)}) custom-call(bf16[2,16,64,384]{3,2,1,0:T(8,128)(2,1)} %x_ref.3, s32[2,16,64]{2,1,0:T(8,128)} %slot_ref.3, bf16[49,384]{1,0:T(8,128)(2,1)} %reshape.36.dwk_ref, f32[1,384]{1,0:T(1,128)} %reshape.37.bias_ref, f32[1,384]{1,0:T(1,128)} %reshape.38.gain_ref, ...), custom_call_target="tpu_custom_call" | custom-call | flops 2454454272 | bytes 6291456 | tf_op jit(solution)/shard_map/inner_rows/pallas_call | solution.py:345
  31.9 20.6 %edge_rows.1 = (bf16[2,16,64,384]{3,2,1,0:T(8,128)(2,1)}, f32[32,1280]{1,0:T(8,128)}) custom-call(bf16[2,16,64,384]{3,2,1,0:T(8,128)(2,1)} %x_ref.3, bf16[2,3,64,384]{3,2,1,0:T(8,128)(2,1)} %copy-done.3, bf16[2,3,64,384]{3,2,1,0:T(8,128)(2,1)} %copy-done.4, s32[2,16,64]{2,1,0:T(8,128)} %slot_ref.3, bf16[49,384]{1,0:T(8,128)(2,1)} %reshape.36.dwk_ref, ...), custom_call_target="tpu_custom_call" | custom-call | flops 2454454272 | bytes 6291456 | tf_op jit(solution)/shard_map/edge_rows/pallas_call | solution.py:360
  52.6 1.7 %copy.20 = f32[32,1,1280]{2,1,0:T(1,128)} copy(f32[32,1,1280]{2,0,1:T(8,128)} %bitcast.8) | data formatting | bytes 327680 | tf_op jit(solution)/shard_map/reshape | solution.py:383
  54.3 7.6 %all-to-all-start = ((f32[32,1,1280]{2,1,0:T(1,128)}), f32[32,1,1280]{2,1,0:T(1,128)S(1)}, u32[]{:S(2)}, u32[]{:S(2)}) async-start(f32[32,1,1280]{2,1,0:T(1,128)} %copy.20), calls=%async_computation | async-start | bytes 327680 | tf_op jit(solution)/shard_map/all_to_all | solution.py:382
  62.5 8.1 %all-to-all-done = f32[32,1,1280]{2,1,0:T(1,128)S(1)} async-done(((f32[32,1,1280]{2,1,0:T(1,128)}), f32[32,1,1280]{2,1,0:T(1,128)S(1)}, u32[]{:S(2)}, u32[]{:S(2)}) %all-to-all-start) | async-done | bytes 163872 | tf_op jit(solution)/shard_map/all_to_all | solution.py:382
  71.3 2.4 %own_tokens.1 = (f32[64,384]{1,0:T(8,128)}, bf16[64,384]{1,0:T(8,128)(2,1)}) custom-call(f32[32,1280]{1,0:T(8,128)} %bitcast.7, bf16[64,384]{1,0:T(8,128)(2,1)} %embed_ref.1, f32[1,384]{1,0:T(1,128)} %reshape.43.gain_ref), custom_call_target="tpu_custom_call" | custom-call | tf_op jit(solution)/shard_map/own_tokens/pallas_call | solution.py:385
  75.3 2.9 %collective-permute-start.4 = (bf16[64,384]{1,0:T(8,128)(2,1)}, bf16[64,384]{1,0:T(8,128)(2,1)S(1)}, u32[]{:S(2)}, u32[]{:S(2)}) collective-permute-start(bf16[64,384]{1,0:T(8,128)(2,1)} %get-tuple-element.18.own_ref), channel_id=1, source_target_pairs={{0,24},{8,16},{16,8},{24,0},{1,25},{9,17},{17,9},{25,1},{2,26},{10... | collective-permute-start | bytes 147464 | tf_op jit(solution)/shard_map/ppermute | solution.py:307
  78.7 2.0 %collective-permute-done.4 = bf16[64,384]{1,0:T(8,128)(2,1)S(1)} collective-permute-done((bf16[64,384]{1,0:T(8,128)(2,1)}, bf16[64,384]{1,0:T(8,128)(2,1)S(1)}, u32[]{:S(2)}, u32[]{:S(2)}) %collective-permute-start.4) | collective-permute-done | bytes 49184 | tf_op jit(solution)/shard_map/ppermute | solution.py:307
  80.7 1.1 collective-permute-start.5
  82.3 1.1 %collective-permute-start.7 = (bf16[256,384]{1,0:T(8,128)(2,1)S(1)}, bf16[256,384]{1,0:T(8,128)(2,1)S(1)}, u32[]{:S(2)}, u32[]{:S(2)}) collective-permute-start(bf16[256,384]{1,0:T(8,128)(2,1)S(1)} %get-tuple-element.31), channel_id=1, source_target_pairs={{0,6},{1,7},{2,4},{3,5},{4,2},{5,3},{6,0},{7,1},{8,14},{9,15},{10,... | collective-permute-start | bytes 589832 | tf_op jit(solution)/shard_map/ppermute | solution.py:307
  83.4 1.9 %collective-permute-done.5 = bf16[256,384]{1,0:T(8,128)(2,1)S(1)} collective-permute-done((bf16[256,384]{1,0:T(8,128)(2,1)S(1)}, bf16[256,384]{1,0:T(8,128)(2,1)S(1)}, u32[]{:S(2)}, u32[]{:S(2)}) %collective-permute-start.5) | collective-permute-done | bytes 196640 | tf_op jit(solution)/shard_map/ppermute | solution.py:307
  85.3 2.4 %collective-permute-done.6 = bf16[256,384]{1,0:T(8,128)(2,1)S(1)} collective-permute-done((bf16[256,384]{1,0:T(8,128)(2,1)S(1)}, bf16[256,384]{1,0:T(8,128)(2,1)S(1)}, u32[]{:S(2)}, u32[]{:S(2)}) %collective-permute-start.6) | collective-permute-done | bytes 196640 | tf_op jit(solution)/shard_map/ppermute | solution.py:307
  87.9 1.9 %collective-permute-done.7 = bf16[256,384]{1,0:T(8,128)(2,1)S(1)} collective-permute-done((bf16[256,384]{1,0:T(8,128)(2,1)S(1)}, bf16[256,384]{1,0:T(8,128)(2,1)S(1)}, u32[]{:S(2)}, u32[]{:S(2)}) %collective-permute-start.7) | collective-permute-done | bytes 196640 | tf_op jit(solution)/shard_map/ppermute | solution.py:307
  89.8 3.7 %collective-permute-start.8 = (bf16[1024,384]{1,0:T(8,128)(2,1)S(1)}, bf16[1024,384]{1,0:T(8,128)(2,1)S(1)}, u32[]{:S(2)}, u32[]{:S(2)}) collective-permute-start(bf16[1024,384]{1,0:T(8,128)(2,1)S(1)} %get-tuple-element.23), channel_id=1, source_target_pairs={{0,1},{1,0},{2,3},{3,2},{4,5},{5,4},{6,7},{7,6},{8,9},{9,8},{10,11... | collective-permute-start | bytes 2359304 | tf_op jit(solution)/shard_map/ppermute | solution.py:307
  94.3 1.1 %collective-permute-done.8 = bf16[1024,384]{1,0:T(8,128)(2,1)S(1)} collective-permute-done((bf16[1024,384]{1,0:T(8,128)(2,1)S(1)}, bf16[1024,384]{1,0:T(8,128)(2,1)S(1)}, u32[]{:S(2)}, u32[]{:S(2)}) %collective-permute-start.8) | collective-permute-done | bytes 786464 | tf_op jit(solution)/shard_map/ppermute | solution.py:307
  95.6 1.2 %copy-done = bf16[2048,384]{1,0:T(8,128)(2,1)} copy-done((bf16[2048,384]{1,0:T(8,128)(2,1)}, bf16[2048,384]{1,0:T(8,128)(2,1)S(1)}, u32[]{:S(2)}) %copy-start) | copy-done | bytes 1572888
  96.8 10.5 %attend.1 = (bf16[64,384]{1,0:T(8,128)(2,1)}, f32[1,64]{1,0:T(1,128)}) custom-call(f32[64,384]{1,0:T(8,128)} %get-tuple-element.17.tokens_ref, bf16[64,384]{1,0:T(8,128)(2,1)} %get-tuple-element.18.own_ref, bf16[2048,384]{1,0:T(8,128)(2,1)} %copy-done, bf16[384,1152]{1,0:T(8,128)(2,1)} %wqkv_ref.1, bf16[384,384]{1,0:T(8,128)(2,1)} %wout_ref.1, ...), custom_call_target="tpu_custom_call" | custom-call | tf_op jit(solution)/shard_map/attend/pallas_call | solution.py:398
  (27 shorter events, 5.9 us)
Async XLA Ops:
  1.8 29.3 %collective-permute-start = (bf16[2,3,64,384]{3,2,1,0:T(8,128)(2,1)S(1)}, bf16[2,3,64,384]{3,2,1,0:T(8,128)(2,1)S(1)}, u32[]{:S(2)}, u32[]{:S(2)}) collective-permute-start(bf16[2,3,64,384]{3,2,1,0:T(8,128)(2,1)S(1)} %get-tuple-element.22), channel_id=1, source_target_pairs={{0,8},{8,16},{16,24},{1,9},{9,17},{17,25},{2,10},{10,18},{18,26},{... | collective-permute-start | bytes 884744 | tf_op jit(solution)/shard_map/ppermute | solution.py:334
  5.8 25.3 %collective-permute-start.1 = (bf16[2,3,64,384]{3,2,1,0:T(8,128)(2,1)S(1)}, bf16[2,3,64,384]{3,2,1,0:T(8,128)(2,1)S(1)}, u32[]{:S(2)}, u32[]{:S(2)}) collective-permute-start(bf16[2,3,64,384]{3,2,1,0:T(8,128)(2,1)S(1)} %get-tuple-element.21), channel_id=1, source_target_pairs={{8,0},{16,8},{24,16},{9,1},{17,9},{25,17},{10,2},{18,10},{26,18},{... | collective-permute-start | bytes 884744 | tf_op jit(solution)/shard_map/ppermute | solution.py:335
  31.1 0.7 copy-start.3
  31.1 0.8 copy-start.4
  31.9 30.0 %copy-start.2 = (f32[384]{0:T(512)S(1)}, f32[384]{0:T(512)}, u32[]{:S(2)}) copy-start(f32[384]{0:T(512)} %param.27) | copy-start | bytes 4612
  54.3 16.3 %all-to-all-start = ((f32[32,1,1280]{2,1,0:T(1,128)}), f32[32,1,1280]{2,1,0:T(1,128)S(1)}, u32[]{:S(2)}, u32[]{:S(2)}) async-start(f32[32,1,1280]{2,1,0:T(1,128)} %copy.20), calls=%async_computation | async-start | bytes 327680 | tf_op jit(solution)/shard_map/all_to_all | solution.py:382
  61.9 31.6 %copy-start.1 = (bf16[384,20]{0,1:T(8,128)(2,1)S(1)}, bf16[384,20]{0,1:T(8,128)(2,1)}, u32[]{:S(2)}) copy-start(bf16[384,20]{0,1:T(8,128)(2,1)} %param.30) | copy-start | bytes 46084
  73.7 4.5 %collective-permute-start.2 = (bf16[64,384]{1,0:T(8,128)(2,1)}, bf16[64,384]{1,0:T(8,128)(2,1)S(1)}, u32[]{:S(2)}, u32[]{:S(2)}) collective-permute-start(bf16[64,384]{1,0:T(8,128)(2,1)} %get-tuple-element.18.own_ref), channel_id=1, source_target_pairs={{0,8},{8,0},{16,24},{24,16},{1,9},{9,1},{17,25},{25,17},{2,10},{10... | collective-permute-start | bytes 147464 | tf_op jit(solution)/shard_map/ppermute | solution.py:307
  74.6 4.1 %collective-permute-start.3 = (bf16[64,384]{1,0:T(8,128)(2,1)}, bf16[64,384]{1,0:T(8,128)(2,1)S(1)}, u32[]{:S(2)}, u32[]{:S(2)}) collective-permute-start(bf16[64,384]{1,0:T(8,128)(2,1)} %get-tuple-element.18.own_ref), channel_id=1, source_target_pairs={{0,16},{8,24},{16,0},{24,8},{1,17},{9,25},{17,1},{25,9},{2,18},{10... | collective-permute-start | bytes 147464 | tf_op jit(solution)/shard_map/ppermute | solution.py:307
  75.3 5.4 %collective-permute-start.4 = (bf16[64,384]{1,0:T(8,128)(2,1)}, bf16[64,384]{1,0:T(8,128)(2,1)S(1)}, u32[]{:S(2)}, u32[]{:S(2)}) collective-permute-start(bf16[64,384]{1,0:T(8,128)(2,1)} %get-tuple-element.18.own_ref), channel_id=1, source_target_pairs={{0,24},{8,16},{16,8},{24,0},{1,25},{9,17},{17,9},{25,1},{2,26},{10... | collective-permute-start | bytes 147464 | tf_op jit(solution)/shard_map/ppermute | solution.py:307
  80.7 4.6 %collective-permute-start.5 = (bf16[256,384]{1,0:T(8,128)(2,1)S(1)}, bf16[256,384]{1,0:T(8,128)(2,1)S(1)}, u32[]{:S(2)}, u32[]{:S(2)}) collective-permute-start(bf16[256,384]{1,0:T(8,128)(2,1)S(1)} %get-tuple-element.31), channel_id=1, source_target_pairs={{0,2},{1,3},{2,0},{3,1},{4,6},{5,7},{6,4},{7,5},{8,10},{9,11},{10,... | collective-permute-start | bytes 589832 | tf_op jit(solution)/shard_map/ppermute | solution.py:307
  81.8 6.0 %collective-permute-start.6 = (bf16[256,384]{1,0:T(8,128)(2,1)S(1)}, bf16[256,384]{1,0:T(8,128)(2,1)S(1)}, u32[]{:S(2)}, u32[]{:S(2)}) collective-permute-start(bf16[256,384]{1,0:T(8,128)(2,1)S(1)} %get-tuple-element.31), channel_id=1, source_target_pairs={{0,4},{1,5},{2,6},{3,7},{4,0},{5,1},{6,2},{7,3},{8,12},{9,13},{10,... | collective-permute-start | bytes 589832 | tf_op jit(solution)/shard_map/ppermute | solution.py:307
  82.3 7.4 %collective-permute-start.7 = (bf16[256,384]{1,0:T(8,128)(2,1)S(1)}, bf16[256,384]{1,0:T(8,128)(2,1)S(1)}, u32[]{:S(2)}, u32[]{:S(2)}) collective-permute-start(bf16[256,384]{1,0:T(8,128)(2,1)S(1)} %get-tuple-element.31), channel_id=1, source_target_pairs={{0,6},{1,7},{2,4},{3,5},{4,2},{5,3},{6,0},{7,1},{8,14},{9,15},{10,... | collective-permute-start | bytes 589832 | tf_op jit(solution)/shard_map/ppermute | solution.py:307
  89.8 5.6 %collective-permute-start.8 = (bf16[1024,384]{1,0:T(8,128)(2,1)S(1)}, bf16[1024,384]{1,0:T(8,128)(2,1)S(1)}, u32[]{:S(2)}, u32[]{:S(2)}) collective-permute-start(bf16[1024,384]{1,0:T(8,128)(2,1)S(1)} %get-tuple-element.23), channel_id=1, source_target_pairs={{0,1},{1,0},{2,3},{3,2},{4,5},{5,4},{6,7},{7,6},{8,9},{9,8},{10,11... | collective-permute-start | bytes 2359304 | tf_op jit(solution)/shard_map/ppermute | solution.py:307
  95.6 1.2 %copy-start = (bf16[2048,384]{1,0:T(8,128)(2,1)}, bf16[2048,384]{1,0:T(8,128)(2,1)S(1)}, u32[]{:S(2)}) copy-start(bf16[2048,384]{1,0:T(8,128)(2,1)S(1)} %constant_dynamic-update-slice_fusion.11.all_ref) | copy-start | bytes 4718596

commit v2 on v1

v2 whole, which is shorter than its diff:
```python
import functools

import jax
import jax.numpy as jnp
from jax import lax
from jax.experimental import pallas as pl
from jax.experimental.pallas import tpu as pltpu
from jax.sharding import PartitionSpec as P

CAP = 3
PAR_DEV = 64
HEADS = 6
HEAD_DIM = 64
BLOCK_ROWS = 4
MARGIN = 8
LANES = 128
EPS = 1e-06
HID_CHUNK = 512
TILE_COLS = 32
TAP_ROWS = 16
ROUTE = 1 << 34
AXES = ("space", "scene")
HIGHEST = lax.Precision.HIGHEST

def gelu(x):
    half = 0.5 * x
    return half + half * lax.erf(x * 0.5**0.5)


def layer_norm(values):
    average = jnp.mean(values, axis=-1, keepdims=True)
    centered = values - average
    return centered * lax.rsqrt(jnp.mean(centered * centered, axis=-1, keepdims=True) + EPS)


def to_column(row, rows):
    n = row.shape[1]
    same = lax.broadcasted_iota(jnp.int32, (n, n), 0) == lax.broadcasted_iota(jnp.int32, (n, n), 1)
    return jnp.sum(jnp.where(same, jnp.broadcast_to(row, (n, n)), 0), axis=1, keepdims=True)


def to_row(column):
    n = column.shape[0]
    same = lax.broadcasted_iota(jnp.int32, (n, n), 0) == lax.broadcasted_iota(jnp.int32, (n, n), 1)
    return jnp.sum(jnp.where(same, jnp.broadcast_to(column, (n, n)), 0), axis=0, keepdims=True)


def conv_rows(source, slab, spat, base, wb, bias_ref, width):
    chans = spat.shape[1]
    ksz = dw_size(wb)
    reach = ksz // 2
    many = len(source) - ksz + 1
    for i, row in enumerate(source):
        value = row().astype(jnp.float32)
        for cb in range(chans // LANES):
            slab[cb, i, MARGIN : MARGIN + width, :] = value[:, cb * LANES : (cb + 1) * LANES]
    for cb in range(chans // LANES):
        lane = slice(cb * LANES, (cb + 1) * LANES)
        bias = bias_ref[...].reshape(1, chans)[:, lane]
        for col in range(0, width, TILE_COLS):
            parts = range(0, TILE_COLS, TAP_ROWS)
            total = [[None for _ in parts] for _ in range(many)]
            for i in range(len(source)):
                start = MARGIN - reach + col
                window = [
                    [
                        slab[cb, i, start + b + p : start + b + p + TAP_ROWS, :].astype(jnp.bfloat16)
                        for b in range(ksz)
                    ]
                    for p in parts
                ]
                for a in range(ksz):
                    r = i - a
                    if not 0 <= r < many:
                        continue
                    taps = [wb[cb, a * ksz + b] for b in range(ksz)]
                    for n in range(len(window)):
                        terms = [v * t for v, t in zip(window[n], taps)]
                        while len(terms) > 1:
                            terms = [sum(terms[k : k + 2][1:], terms[k]) for k in range(0, len(terms), 2)]
                        term = terms[0].astype(jnp.float32)
                        total[r][n] = term if total[r][n] is None else total[r][n] + term
            for r in range(many):
                for n, p in enumerate(parts):
                    at = base + r * width + col + p
                    spat[at : at + TAP_ROWS, lane] = total[r][n] + bias


def dw_size(wb):
    return int(wb.shape[1] ** 0.5 + 0.5)


def mlp_rows(spat, normed, branch, gain_ref, we_ref, wr_ref):
    normed[...] = (layer_norm(spat[...]) * gain_ref[...].reshape(1, -1)).astype(jnp.bfloat16)
    hid = we_ref.shape[1]
    chunk = min(HID_CHUNK, hid)
    for start in range(0, hid, chunk):
        pre = jnp.dot(
            normed[...], we_ref[:, start : start + chunk], preferred_element_type=jnp.float32
        )
        part = jnp.dot(
            gelu(pre).astype(jnp.bfloat16),
            wr_ref[start : start + chunk, :],
            preferred_element_type=jnp.float32,
        )
        if start == 0:
            branch[...] = part
        else:
            branch[...] += part


def prepare(slab, wb, dwk_ref, width):
    edge = jnp.zeros(slab.shape[:2] + (MARGIN, LANES), jnp.float32)
    slab[:, :, 0:MARGIN, :] = edge
    slab[:, :, MARGIN + width :, :] = edge
    ksz = dwk_ref.shape[0]
    for a in range(ksz):
        kernel = dwk_ref[a].astype(jnp.float32)
        for cb in range(wb.shape[0]):
            for b in range(ksz):
                wb[cb, a * ksz + b] = jnp.broadcast_to(
                    kernel[b : b + 1, cb * LANES : (cb + 1) * LANES], (TAP_ROWS, LANES)
                ).astype(jnp.bfloat16)


def pool(member, feats, sums_ref, counts_ref):
    sums_ref[...] += jnp.dot(member, feats, preferred_element_type=jnp.float32)
    ones = jnp.ones((member.shape[1], LANES), jnp.bfloat16)
    counts_ref[...] += jnp.dot(member, ones, preferred_element_type=jnp.float32)


def membership(slot_ref, scene, row0, many, width, slots):
    pieces = []
    for r in range(many):
        one = slot_ref[scene, row0 + r : row0 + r + 1, :]
        index = lax.broadcasted_iota(jnp.int32, (slots, width), 0)
        pieces.append((index == one).astype(jnp.float32).astype(jnp.bfloat16))
    return jnp.concatenate(pieces, axis=1)


def rows_block(
    scenes, blocks, slots, width, x_ref, slot_ref, slab, spat, normed, branch, wb, bias_ref,
    gain_ref, we_ref, wr_ref, scale_ref, feat_ref, sums_ref, counts_ref, before_mlp, after_scene,
):
    for scene in range(scenes):
        base = 0
        for _, many, window in blocks:
            conv_rows(window(scene), slab, spat, base, wb, bias_ref, width)
            base += many * width
        if scene == 0:
            before_mlp()
        mlp_rows(spat, normed, branch, gain_ref, we_ref, wr_ref)
        center = jnp.concatenate(
            [x_ref[scene, r : r + n].reshape(n * width, -1) for r, n, _ in blocks], axis=0
        )
        feats = (
            center.astype(jnp.float32) + scale_ref[...].reshape(1, -1) * branch[...]
        ).astype(jnp.bfloat16)
        feat_ref[scene] = feats
        after_scene(scene)
        member = jnp.concatenate(
            [membership(slot_ref, scene, r, n, width, slots) for r, n, _ in blocks], axis=1
        )
        pool(member, feats, sums_ref, counts_ref)


def route_kernel(owners, inter_ref, pos_ref, placer_ref, rows_ref):
    slots = inter_ref.shape[1]
    parcels = pos_ref.shape[0]
    listed = to_column(inter_ref[...], slots)
    number = lax.broadcasted_iota(jnp.int32, (slots, parcels), 1)
    position = jnp.sum(
        jnp.where(number == listed, jnp.broadcast_to(pos_ref[...].reshape(1, parcels), (slots, parcels)), 0),
        axis=1, keepdims=True,
    )
    owner = position // PAR_DEV
    owner_row = to_row(owner)
    this = lax.broadcasted_iota(jnp.int32, (slots, slots), 0)
    other = lax.broadcasted_iota(jnp.int32, (slots, slots), 1)
    rank = jnp.sum(
        jnp.where((owner == owner_row) & (other < this), 1, 0), axis=1, keepdims=True
    )
    place = to_row(rank * owners + owner)
    place_index = lax.broadcasted_iota(jnp.int32, (CAP * owners, slots), 0)
    placer_ref[...] = (place_index == place).astype(jnp.float32)
    local_row = (position - owner * PAR_DEV).astype(jnp.float32)
    rows_ref[...] = jnp.broadcast_to(local_row, rows_ref.shape)


def inner_kernel(
    rows, slots, x_hbm, slot_hbm, dwk_hbm, bias_hbm, gain_hbm, we_hbm, wr_hbm, scale_hbm,
    feat_hbm, sums_ref, counts_ref, x_ref, slot_ref, dwk_ref, bias_ref, gain_ref, we_ref, wr_ref,
    scale_ref, sems, out_sems, slab, spat, normed, branch, wb, feat_ref,
):
    scenes, _, width, _ = x_ref.shape
    ksz = dw_size(wb)
    reach = ksz // 2
    inside = rows - 2 * BLOCK_ROWS
    first = [(x_hbm, x_ref), (dwk_hbm, dwk_ref), (bias_hbm, bias_ref)]
    later = [
        (slot_hbm, slot_ref), (gain_hbm, gain_ref), (we_hbm, we_ref), (wr_hbm, wr_ref),
        (scale_hbm, scale_ref),
    ]
    copies = [pltpu.make_async_copy(a, b, sems.at[i]) for i, (a, b) in enumerate(first + later)]
    for copy in copies:
        copy.start()
    sums_ref[...] = jnp.zeros_like(sums_ref)
    counts_ref[...] = jnp.zeros_like(counts_ref)
    for copy in copies[: len(first)]:
        copy.wait()
    prepare(slab, wb, dwk_ref, width)

    def window(scene):
        return [
            functools.partial(lambda r: x_ref[scene, r], BLOCK_ROWS - reach + i)
            for i in range(inside + ksz - 1)
        ]

    def arrive():
        for copy in copies[len(first) :]:
            copy.wait()

    writes = [
        pltpu.make_async_copy(
            feat_ref.at[scene, pl.ds(r * width, width)],
            feat_hbm.at[scene, BLOCK_ROWS + r],
            out_sems.at[scene, r],
        )
        for scene in range(scenes)
        for r in range(inside)
    ]

    def leave(scene):
        for write in writes[scene * inside : (scene + 1) * inside]:
            write.start()

    rows_block(
        scenes, [(BLOCK_ROWS, inside, window)], slots, width, x_ref, slot_ref, slab, spat, normed,
        branch, wb, bias_ref, gain_ref, we_ref, wr_ref, scale_ref, feat_ref, sums_ref, counts_ref,
        arrive, leave,
    )
    for write in writes:
        write.wait()


def edge_kernel(
    rows, slots, owners, x_ref, top_ref, bot_ref, slot_ref, dwk_ref, bias_ref, gain_ref, we_ref,
    wr_ref, scale_ref, feat_in, sums_in, counts_in, placer_ref, rows_ref,
    feat_hbm, sent_ref, out_sems, slab, spat, normed, branch, wb, feat_ref, sums_ref, counts_ref,
):
    scenes, _, width, _ = x_ref.shape
    ksz = dw_size(wb)
    reach = ksz // 2
    prepare(slab, wb, dwk_ref, width)
    sums_ref[...] = sums_in[...]
    counts_ref[...] = counts_in[...]

    def window(row0):
        def rows_of(scene):
            source = []
            for i in range(BLOCK_ROWS + ksz - 1):
                r = row0 - reach + i
                if r < 0:
                    source.append(functools.partial(lambda r: top_ref[scene, r], r + reach))
                elif r >= rows:
                    source.append(functools.partial(lambda r: bot_ref[scene, r], r - rows))
                else:
                    source.append(functools.partial(lambda r: x_ref[scene, r], r))
            return source

        return rows_of

    starts = (0, rows - BLOCK_ROWS)
    writes = [
        pltpu.make_async_copy(
            feat_ref.at[scene, pl.ds((n * BLOCK_ROWS + r) * width, width)],
            feat_hbm.at[scene, start + r],
            out_sems.at[scene, n * BLOCK_ROWS + r],
        )
        for scene in range(scenes)
        for n, start in enumerate(starts)
        for r in range(BLOCK_ROWS)
    ]
    each = len(starts) * BLOCK_ROWS

    def leave(scene):
        for write in writes[scene * each : (scene + 1) * each]:
            write.start()

    rows_block(
        scenes, [(start, BLOCK_ROWS, window(start)) for start in starts], slots, width, x_ref,
        slot_ref, slab, spat, normed, branch, wb, bias_ref, gain_ref, we_ref, wr_ref, scale_ref,
        feat_ref, sums_ref, counts_ref, lambda: None, leave,
    )
    placer = placer_ref[...]
    sent = jnp.dot(placer, sums_ref[...], precision=HIGHEST, preferred_element_type=jnp.float32)
    lane = lax.broadcasted_iota(jnp.int32, (slots, LANES), 1)
    counts_rows = jnp.where(lane < CAP, counts_ref[...], rows_ref[...])
    meta = jnp.dot(placer, counts_rows, precision=HIGHEST, preferred_element_type=jnp.float32)
    chans = sent.shape[1]
    lane = lax.broadcasted_iota(jnp.int32, (owners, LANES), 1)
    packed = jnp.zeros((owners, LANES), jnp.float32)
    for k in range(CAP):
        sent_ref[:, 0, k * chans : (k + 1) * chans] = sent[k * owners : (k + 1) * owners]
        packed = jnp.where(
            (lane == k) | (lane == CAP + k), meta[k * owners : (k + 1) * owners], packed
        )
    sent_ref[:, 0, CAP * chans :] = packed
    for write in writes:
        write.wait()


def owner_kernel(recv_ref, embed_ref, gain_ref, tokens_ref, attn_ref):
    chans = embed_ref.shape[1]
    meta = recv_ref[:, 0, CAP * chans :]
    tiles = recv_ref.shape[0]
    sums = jnp.zeros(tokens_ref.shape, jnp.float32)
    counts = jnp.zeros((PAR_DEV, LANES), jnp.float32)
    index = lax.broadcasted_iota(jnp.int32, (PAR_DEV, tiles), 0).astype(jnp.float32)
    for k in range(CAP):
        rows = jnp.broadcast_to(meta[:, CAP + k : CAP + k + 1], (tiles, LANES)).T[0:1, :]
        table = (index == rows).astype(jnp.float32)
        sums += jnp.dot(
            table, recv_ref[:, 0, k * chans : (k + 1) * chans],
            precision=HIGHEST, preferred_element_type=jnp.float32,
        )
        many = jnp.broadcast_to(meta[:, k : k + 1], (tiles, LANES))
        counts += jnp.dot(table, many, precision=HIGHEST, preferred_element_type=jnp.float32)
    tokens = sums / jnp.maximum(counts[:, :1], 1.0) + embed_ref[...].astype(jnp.float32)
    tokens_ref[...] = tokens
    attn_ref[...] = (layer_norm(tokens) * gain_ref[...].reshape(1, chans)).astype(jnp.bfloat16)


def fold_keys(pieces, queries, wqkv_ref, state):
    chans = wqkv_ref.shape[0]
    part = jnp.concatenate([p[...] for p in pieces], axis=0)
    keys = jnp.dot(
        part, wqkv_ref[:, chans : 2 * chans], preferred_element_type=jnp.float32
    ).astype(jnp.bfloat16)
    values = jnp.dot(
        part, wqkv_ref[:, 2 * chans :], preferred_element_type=jnp.float32
    ).astype(jnp.bfloat16)
    scores = lax.dot_general(
        queries, keys, (((1,), (1,)), ((), ())), preferred_element_type=jnp.float32
    )
    top = jnp.max(scores, axis=1, keepdims=True)
    if state is not None:
        top = jnp.maximum(state[0], top)
    weights = jnp.exp(scores - top)
    total = jnp.sum(weights, axis=1, keepdims=True)
    mixed = jnp.dot(weights.astype(jnp.bfloat16), values, preferred_element_type=jnp.float32)
    if state is not None:
        keep = jnp.exp(state[0] - top)
        total = total + keep * state[1]
        mixed = mixed + keep * state[2]
    return top, total, mixed


def split_heads(own_ref, wqkv_ref):
    chans = wqkv_ref.shape[0]
    queries = jnp.dot(
        own_ref[...], wqkv_ref[:, :chans], preferred_element_type=jnp.float32
    ) * HEAD_DIM ** (-0.5)
    lane = lax.broadcasted_iota(jnp.int32, queries.shape, 1)
    return jnp.concatenate(
        [jnp.where(lane // HEAD_DIM == h, queries, 0.0).astype(jnp.bfloat16) for h in range(HEADS)],
        axis=0,
    )


def near_kernel(count, own_ref, wqkv_ref, *refs):
    pieces, (stat_ref, mixed_ref, query_ref) = refs[:count], refs[count:]
    queries = split_heads(own_ref, wqkv_ref)
    query_ref[...] = queries
    top, total, mixed = fold_keys(pieces, queries, wqkv_ref, None)
    lane = lax.broadcasted_iota(jnp.int32, stat_ref.shape, 1)
    stat_ref[...] = jnp.where(lane == 0, top, total)
    mixed_ref[...] = mixed


def far_kernel(
    count, tokens_ref, query_ref, wqkv_ref, wout_ref, wclass_ref, labels_ref, stat_ref, mixed_ref,
    *refs,
):
    pieces, (state_ref, loss_ref) = refs[:count], refs[count:]
    chans = wqkv_ref.shape[0]
    here = tokens_ref.shape[0]
    state = (stat_ref[:, 0:1], stat_ref[:, 1:2], mixed_ref[...])
    _, total, mixed = fold_keys(pieces, query_ref[...], wqkv_ref, state)
    mixed = mixed / total
    lane = lax.broadcasted_iota(jnp.int32, (here, chans), 1)
    attended = jnp.zeros((here, chans), jnp.float32)
    for h in range(HEADS):
        attended = jnp.where(lane // HEAD_DIM == h, mixed[h * here : (h + 1) * here], attended)
    state = tokens_ref[...] + jnp.dot(
        attended.astype(jnp.bfloat16), wout_ref[...], preferred_element_type=jnp.float32
    )
    state_ref[...] = state.astype(jnp.bfloat16)
    class_in = layer_norm(state).astype(jnp.bfloat16)
    logits = lax.dot_general(
        class_in, wclass_ref[...], (((1,), (1,)), ((), ())), preferred_element_type=jnp.float32
    )
    top = jnp.max(logits, axis=1, keepdims=True)
    log_total = top + jnp.log(jnp.sum(jnp.exp(logits - top), axis=1, keepdims=True))
    number = lax.broadcasted_iota(jnp.int32, logits.shape, 1)
    label = to_column(labels_ref[...].reshape(1, here), here)
    picked = jnp.sum(jnp.where(number == label, logits, 0.0), axis=1, keepdims=True)
    loss = jnp.broadcast_to(log_total - picked, (here, here))
    same = lax.broadcasted_iota(jnp.int32, (here, here), 0) == lax.broadcasted_iota(
        jnp.int32, (here, here), 1
    )
    loss_ref[...] = jnp.sum(jnp.where(same, loss, 0.0), axis=0)


VM = pl.BlockSpec(memory_space=pltpu.VMEM)
HBM = pl.BlockSpec(memory_space=pltpu.HBM)


def params(mib=32):
    return pltpu.CompilerParams(vmem_limit_bytes=mib * 1024 * 1024)


def xor_permute(x, axis, mask, count):
    return lax.ppermute(x, axis, [(i, i ^ mask) for i in range(count)])


def exchange(groups, axis, bits, count):
    whole = groups[0] if len(groups) == 1 else jnp.concatenate(groups, axis=0)
    masks = [sum(1 << b for n, b in enumerate(bits) if m >> n & 1) for m in range(1, 1 << len(bits))]
    return [whole], [xor_permute(whole, axis, m, count) for m in masks]


def gather_stages():
    stages = []
    for axis in AXES:
        bits = list(range(lax.axis_size(axis).bit_length() - 1))[::-1]
        last = [bits.pop()] if axis == AXES[-1] else []
        stages += [(axis, bits[i : i + 2]) for i in range(0, len(bits), 2)]
        if last:
            stages.append((axis, last))
    return stages


def local(
    pixels, dw_kernel, dw_bias, norm_gain, w_expand, w_reduce, layer_scale, pixel_slot,
    intersection, parcel_pos, parcel_embed, attn_gain, w_qkv, w_out, w_class, labels,
):
    scenes, rows, width, chans = pixels.shape
    ksz = dw_kernel.shape[0]
    reach = ksz // 2
    slots = intersection.shape[1]
    owners = lax.axis_size("space") * lax.axis_size("scene")
    count = lax.axis_size("space")
    up = [(i, i + 1) for i in range(count - 1)]
    down = [(i + 1, i) for i in range(count - 1)]
    top = lax.ppermute(pixels[:, rows - reach :], "space", up)
    bottom = lax.ppermute(pixels[:, :reach], "space", down)

    inside = rows - 2 * BLOCK_ROWS

    def scratch(many, window):
        return [
            pltpu.SemaphoreType.DMA((scenes, many)),
            pltpu.VMEM((chans // LANES, window, width + 2 * MARGIN, LANES), jnp.float32),
            pltpu.VMEM((many * width, chans), jnp.float32),
            pltpu.VMEM((many * width, chans), jnp.bfloat16),
            pltpu.VMEM((many * width, chans), jnp.float32),
            pltpu.VMEM((chans // LANES, ksz * ksz, TAP_ROWS, LANES), jnp.bfloat16),
            pltpu.VMEM((scenes, many * width, chans), jnp.bfloat16),
        ]

    work = 2 * rows * width * chans * (ksz * ksz + 2 * w_expand.shape[1])
    placer, local_rows = pl.pallas_call(
        functools.partial(route_kernel, owners),
        out_shape=(
            jax.ShapeDtypeStruct((CAP * owners, slots), jnp.float32),
            jax.ShapeDtypeStruct((slots, LANES), jnp.float32),
        ),
        in_specs=[VM] * 2,
        out_specs=(VM, VM),
        compiler_params=params(8),
        cost_estimate=pl.CostEstimate(flops=ROUTE, bytes_accessed=1 << 20, transcendentals=0),
        name="route",
    )(intersection, parcel_pos)
    inputs = (
        pixels, pixel_slot, dw_kernel, dw_bias, norm_gain, w_expand, w_reduce, layer_scale
    )
    feats, sums, counts = pl.pallas_call(
        functools.partial(inner_kernel, rows, slots),
        out_shape=(
            jax.ShapeDtypeStruct(pixels.shape, jnp.bfloat16),
            jax.ShapeDtypeStruct((slots, chans), jnp.float32),
            jax.ShapeDtypeStruct((slots, LANES), jnp.float32),
        ),
        in_specs=[HBM] * len(inputs),
        out_specs=(HBM, VM, VM),
        scratch_shapes=[pltpu.VMEM(v.shape, v.dtype) for v in inputs]
        + [pltpu.SemaphoreType.DMA((len(inputs),))]
        + scratch(inside, inside + ksz - 1),
        compiler_params=params(),
        cost_estimate=pl.CostEstimate(flops=work, bytes_accessed=6 << 20, transcendentals=0),
        name="inner_rows",
    )(*inputs)
    features, sent = pl.pallas_call(
        functools.partial(edge_kernel, rows, slots, owners),
        out_shape=(
            jax.ShapeDtypeStruct(pixels.shape, jnp.bfloat16),
            jax.ShapeDtypeStruct((owners, 1, CAP * chans + LANES), jnp.float32),
        ),
        in_specs=[VM] * 10 + [HBM] + [VM] * 4,
        out_specs=(HBM, VM),
        input_output_aliases={10: 0},
        scratch_shapes=scratch(2 * BLOCK_ROWS, BLOCK_ROWS + ksz - 1)
        + [pltpu.VMEM((slots, chans), jnp.float32), pltpu.VMEM((slots, LANES), jnp.float32)],
        compiler_params=params(),
        cost_estimate=pl.CostEstimate(flops=work, bytes_accessed=6 << 20, transcendentals=0),
        name="edge_rows",
    )(
        pixels, top, bottom, pixel_slot, dw_kernel, dw_bias, norm_gain, w_expand, w_reduce, layer_scale,
        feats, sums, counts, placer, local_rows,
    )
    arrived = lax.all_to_all(sent, AXES, split_axis=0, concat_axis=0, tiled=True)
    tokens, attn_in = pl.pallas_call(
        owner_kernel,
        out_shape=(
            jax.ShapeDtypeStruct((PAR_DEV, chans), jnp.float32),
            jax.ShapeDtypeStruct((PAR_DEV, chans), jnp.bfloat16),
        ),
        in_specs=[VM] * 3,
        out_specs=(VM, VM),
        compiler_params=params(),
        name="own_tokens",
    )(arrived, parcel_embed, attn_gain)
    held = [attn_in]
    stages = gather_stages()
    for axis, bits in stages[:-1]:
        kept, got = exchange(held, axis, bits, lax.axis_size(axis))
        held = kept + got
    axis, bits = stages[-1]
    far = [xor_permute(h, axis, 1 << bits[0], lax.axis_size(axis)) for h in held]
    heads = HEADS * PAR_DEV
    fold = 2 * owners * PAR_DEV * chans * (chans + heads)
    stat, mixed, queries = pl.pallas_call(
        functools.partial(near_kernel, len(held)),
        out_shape=(
            jax.ShapeDtypeStruct((heads, LANES), jnp.float32),
            jax.ShapeDtypeStruct((heads, chans), jnp.float32),
            jax.ShapeDtypeStruct((heads, chans), jnp.bfloat16),
        ),
        in_specs=[VM] * (2 + len(held)),
        out_specs=(VM,) * 3,
        compiler_params=params(),
        cost_estimate=pl.CostEstimate(flops=fold, bytes_accessed=2 << 20, transcendentals=0),
        name="near_keys",
    )(attn_in, w_qkv, *held)
    state, loss = pl.pallas_call(
        functools.partial(far_kernel, len(far)),
        out_shape=(
            jax.ShapeDtypeStruct((PAR_DEV, chans), jnp.bfloat16),
            jax.ShapeDtypeStruct((PAR_DEV,), jnp.float32),
        ),
        in_specs=[VM] * (8 + len(far)),
        out_specs=(VM, VM),
        compiler_params=params(),
        cost_estimate=pl.CostEstimate(flops=fold, bytes_accessed=2 << 20, transcendentals=0),
        name="far_keys",
    )(tokens, queries, w_qkv, w_out, w_class.T, labels, stat, mixed, *far)
    return features, state, loss


def solution(mesh):
    in_specs = (
        P("scene", "space", None, None),
        P(), P(), P(), P(), P(), P(),
        P("scene", "space", None),
        P(AXES, None),
        P(),
        P(AXES, None),
        P(), P(), P(), P(),
        P(AXES),
    )
    out_specs = (P("scene", "space", None, None), P(AXES, None), P(AXES))
    return jax.shard_map(local, mesh=mesh, in_specs=in_specs, out_specs=out_specs, check_vma=False)
```

time: 108 us -> 72.1 us (0.67)
  Pallas kernels: 52.4 us -> 26.9 us
  blocking collectives: 0 us -> 16.1 us
  waiting for transfers between devices: 17.9 us -> 2.39 us
  local copies, waits for them, and re-layouts: 13.3 us -> 2.85 us
    pallas_call x3 -> x5, Pallas kernels: 50 us -> 26 us  [the longest x1 10 us: local(): pl.pallas_call(functools.partial(edge_kernel, rows, slots, owners), out_s...]
    all_to_all x0 -> x1, blocking collectives: none -> 16.1 us  [local(): lax.all_to_all(sent, AXES, split_axis=0, concat_axis=0, tiled=True)]
    all_to_all x1 -> x0, waiting for transfers between devices: 8.11 us -> none  [local(): lax.all_to_all(sent.reshape(owners, 1, wide), AXES, split_axis=0, concat_...]
    all_to_all x1 -> x0, starting transfers between devices: 7.62 us -> none  [local(): lax.all_to_all(sent.reshape(owners, 1, wide), AXES, split_axis=0, concat_...]
    reshape x6 -> x0, local copies, waits for them, and re-layouts: 7.47 us -> none  [the longest x1 1.75 us: local(): sent.reshape(owners, 1, wide)]
    ppermute x7 -> x10, waiting for transfers between devices: 9.77 us -> 2.38 us  [xor_permute(): return lax.ppermute(x, axis, [(i, i ^ mask) for i in range(count)])]
    ppermute x7 -> x10, starting transfers between devices: 10 us -> 17 us  [xor_permute(): return lax.ppermute(x, axis, [(i, i ^ mask) for i in range(count)])]
    unnamed x18 -> x35, local copies, waits for them, and re-layouts: 4.47 us -> 1.72 us
  transfers between devices with their start and end apart: 10 -> 12, of which waited for: 7 -> 2; matrix products, arithmetic and copies ran while one was open for 7% -> 0% of each run, Pallas kernels for 18% -> 17%
where the time goes in v2:
time: 72.1 us; the launch traced here: 71.8 us
  Pallas kernels  26.9 us (37%)
  starting transfers between devices  22.6 us (31%)
  blocking collectives  16.1 us (22%)
  local copies, waits for them, and re-layouts  2.85 us (4%)
  waiting for transfers between devices  2.39 us (3%)
  between operations  0.92 us (1%)
    ppermute x10, starting transfers between devices, xor_permute(): return lax.ppermute(x, axis, [(i, i ^ mask) for i in range(count)])  17 us
    all_to_all x1, blocking collectives, local(): lax.all_to_all(sent, AXES, split_axis=0, concat_axis=0, tiled=True)  16.1 us
    pallas_call x1, Pallas kernels, local(): pl.pallas_call(functools.partial(edge_kernel, rows, slots, owners), out_s...  10 us
    pallas_call x1, Pallas kernels, local(): pl.pallas_call(functools.partial(inner_kernel, rows, slots), out_shape=(j...  9.84 us
    ppermute x1, starting transfers between devices, local(): top = lax.ppermute(pixels[:, rows - reach:], 'space', up)  4.05 us
    pallas_call x1, Pallas kernels, local(): pl.pallas_call(functools.partial(far_kernel, len(far)), out_shape=(jax.Sh...  3.51 us
    ppermute x10, waiting for transfers between devices, xor_permute(): return lax.ppermute(x, axis, [(i, i ^ mask) for i in range(count)])  2.38 us
    pallas_call x1, Pallas kernels, local(): pl.pallas_call(functools.partial(near_kernel, len(held)), out_shape=(jax....  2.21 us
  transfers between devices with their start and end apart: 12, of which 2 were waited for; matrix products, arithmetic and copies ran while one was open for 0% of the time, Pallas kernels for 17%

profile of v2, /device:TPU:1, one launch (start us, length us, event | category | flops | bytes accessed | tf_op | source)
XLA Modules:
  0.0 71.8 jit_solution(9240934777746969735)
XLA Ops:
  0.6 1.1 %fusion = (bf16[2,3,64,384]{3,2,1,0:T(8,128)(2,1)S(1)}, bf16[2,3,64,384]{3,2,1,0:T(8,128)(2,1)S(1)}) fusion(bf16[2,16,64,384]{3,2,1,0:T(8,128)(2,1)} %x_ref.1), kind=kLoop, calls=%fused_computation.4 | loop fusion | bytes 1179648 | tf_op jit(solution)/shard_map/slice | solution.py:457
  1.8 4.0 %collective-permute-start = (bf16[2,3,64,384]{3,2,1,0:T(8,128)(2,1)S(1)}, bf16[2,3,64,384]{3,2,1,0:T(8,128)(2,1)S(1)}, u32[]{:S(2)}, u32[]{:S(2)}) collective-permute-start(bf16[2,3,64,384]{3,2,1,0:T(8,128)(2,1)S(1)} %get-tuple-element.32), channel_id=1, source_target_pairs={{0,8},{8,16},{16,24},{1,9},{9,17},{17,25},{2,10},{10,18},{18,26},{... | collective-permute-start | bytes 884744 | tf_op jit(solution)/shard_map/ppermute | solution.py:456
  5.9 1.6 %collective-permute-start.1 = (bf16[2,3,64,384]{3,2,1,0:T(8,128)(2,1)S(1)}, bf16[2,3,64,384]{3,2,1,0:T(8,128)(2,1)S(1)}, u32[]{:S(2)}, u32[]{:S(2)}) collective-permute-start(bf16[2,3,64,384]{3,2,1,0:T(8,128)(2,1)S(1)} %get-tuple-element.31), channel_id=1, source_target_pairs={{8,0},{16,8},{24,16},{9,1},{17,9},{25,17},{10,2},{18,10},{26,18},{... | collective-permute-start | bytes 884744 | tf_op jit(solution)/shard_map/ppermute | solution.py:457
  7.4 0.7 copy-done.10
  8.1 0.7 copy-done.14
  8.8 0.4 route.1
  9.5 9.8 %inner_rows.1 = (bf16[2,16,64,384]{3,2,1,0:T(8,128)(2,1)}, f32[64,384]{1,0:T(8,128)S(1)}, f32[64,128]{1,0:T(8,128)S(1)}) custom-call(bf16[2,16,64,384]{3,2,1,0:T(8,128)(2,1)S(1)} %copy-done, s32[2,16,64]{2,1,0:T(8,128)S(1)} %copy-done.9, bf16[7,7,384]{2,1,0:T(8,128)(2,1)S(1)} %copy-done.7, f32[384]{0:T(512)S(1)} %copy-done.11, f32[384]{0:T(512)S(1)} %copy-done.12, ...), custom_call_target="tpu_custom_call" | custom-call | flops 2454454272 | bytes 6291456 | tf_op jit(solution)/shard_map/inner_rows/pallas_call | solution.py:488
  19.4 10.0 %edge_rows.1 = (bf16[2,16,64,384]{3,2,1,0:T(8,128)(2,1)}, f32[32,1,1280]{2,1,0:T(1,128)S(1)}) custom-call(bf16[2,16,64,384]{3,2,1,0:T(8,128)(2,1)S(1)} %copy-done, bf16[2,3,64,384]{3,2,1,0:T(8,128)(2,1)S(1)} %collective-permute-done.top_ref, bf16[2,3,64,384]{3,2,1,0:T(8,128)(2,1)S(1)} %collective-permute-done.1.bot_ref, ...), custom_call_target="tpu_custom_call", output_to_operand_aliasing={{0}: (10, {})} | custom-call | flops 2454454272 | bytes 6291456 | tf_op jit(solution)/shard_map/edge_rows/pallas_call | solution.py:504
  29.5 16.1 %all_to_all.5.recv_ref = f32[32,1,1280]{2,1,0:T(1,128)S(1)} all-to-all(f32[32,1,1280]{2,1,0:T(1,128)S(1)} %get-tuple-element.23), channel_id=1, replica_groups=mesh['space'=4,'scene'=8] {'space','scene'}, dimensions={0} | all-to-all | bytes 327680 | tf_op jit(solution)/shard_map/all_to_all | solution.py:522
  45.6 0.9 %own_tokens.1 = (f32[64,384]{1,0:T(8,128)S(1)}, bf16[64,384]{1,0:T(8,128)(2,1)S(1)}) custom-call(f32[32,1,1280]{2,1,0:T(1,128)S(1)} %all_to_all.5.recv_ref, bf16[64,384]{1,0:T(8,128)(2,1)S(1)} %copy-done.1, f32[384]{0:T(512)S(1)} %copy-done.2), custom_call_target="tpu_custom_call" | custom-call | tf_op jit(solution)/shard_map/own_tokens/pallas_call | solution.py:523
  46.5 0.4 collective-permute-start.2
  47.0 0.3 collective-permute-start.3
  47.3 2.9 %collective-permute-start.4 = (bf16[64,384]{1,0:T(8,128)(2,1)S(1)}, bf16[64,384]{1,0:T(8,128)(2,1)S(1)}, u32[]{:S(2)}, u32[]{:S(2)}) collective-permute-start(bf16[64,384]{1,0:T(8,128)(2,1)S(1)} %get-tuple-element.25.own_ref), channel_id=1, source_target_pairs={{0,24},{8,16},{16,8},{24,0},{1,25},{9,17},{17,9},{25,1},{2,26},{10... | collective-permute-start | bytes 147464 | tf_op jit(solution)/shard_map/ppermute | solution.py:424
  50.2 0.3 collective-permute-done.2
  50.5 2.1 %collective-permute-done.4 = bf16[64,384]{1,0:T(8,128)(2,1)S(1)} collective-permute-done((bf16[64,384]{1,0:T(8,128)(2,1)S(1)}, bf16[64,384]{1,0:T(8,128)(2,1)S(1)}, u32[]{:S(2)}, u32[]{:S(2)}) %collective-permute-start.4) | collective-permute-done | bytes 49184 | tf_op jit(solution)/shard_map/ppermute | solution.py:424
  52.6 0.9 %collective-permute-start.6 = (bf16[256,384]{1,0:T(8,128)(2,1)S(1)}, bf16[256,384]{1,0:T(8,128)(2,1)S(1)}, u32[]{:S(2)}, u32[]{:S(2)}) collective-permute-start(bf16[256,384]{1,0:T(8,128)(2,1)S(1)} %constant_dynamic-update-slice_fusion.refs_0_), channel_id=1, source_target_pairs={{0,2},{1,3},{2,0},{3,1},{4,6},{5,7},{6,4},{7,5},{8,10},{9,11},{10,... | collective-permute-start | bytes 589832 | tf_op jit(solution)/shard_map/ppermute | solution.py:424
  53.6 0.9 %collective-permute-start.7 = (bf16[256,384]{1,0:T(8,128)(2,1)S(1)}, bf16[256,384]{1,0:T(8,128)(2,1)S(1)}, u32[]{:S(2)}, u32[]{:S(2)}) collective-permute-start(bf16[256,384]{1,0:T(8,128)(2,1)S(1)} %constant_dynamic-update-slice_fusion.refs_0_), channel_id=1, source_target_pairs={{0,6},{1,7},{2,4},{3,5},{4,2},{5,3},{6,0},{7,1},{8,14},{9,15},{10,... | collective-permute-start | bytes 589832 | tf_op jit(solution)/shard_map/ppermute | solution.py:424
  54.5 0.8 %collective-permute-start.5 = (bf16[256,384]{1,0:T(8,128)(2,1)S(1)}, bf16[256,384]{1,0:T(8,128)(2,1)S(1)}, u32[]{:S(2)}, u32[]{:S(2)}) collective-permute-start(bf16[256,384]{1,0:T(8,128)(2,1)S(1)} %constant_dynamic-update-slice_fusion.refs_0_), channel_id=1, source_target_pairs={{0,4},{1,5},{2,6},{3,7},{4,0},{5,1},{6,2},{7,3},{8,12},{9,13},{10,... | collective-permute-start | bytes 589832 | tf_op jit(solution)/shard_map/ppermute | solution.py:424
  55.3 3.0 %collective-permute-start.8 = (bf16[256,384]{1,0:T(8,128)(2,1)S(1)}, bf16[256,384]{1,0:T(8,128)(2,1)S(1)}, u32[]{:S(2)}, u32[]{:S(2)}) collective-permute-start(bf16[256,384]{1,0:T(8,128)(2,1)S(1)} %constant_dynamic-update-slice_fusion.refs_0_), channel_id=1, source_target_pairs={{0,1},{1,0},{2,3},{3,2},{4,5},{5,4},{6,7},{7,6},{8,9},{9,8},{10,11... | collective-permute-start | bytes 589832 | tf_op jit(solution)/shard_map/ppermute | solution.py:424
  58.4 3.7 %collective-permute-start.10 = (bf16[256,384]{1,0:T(8,128)(2,1)S(1)}, bf16[256,384]{1,0:T(8,128)(2,1)S(1)}, u32[]{:S(2)}, u32[]{:S(2)}) collective-permute-start(bf16[256,384]{1,0:T(8,128)(2,1)S(1)} %collective-permute-done.6.refs_2_), channel_id=1, source_target_pairs={{0,1},{1,0},{2,3},{3,2},{4,5},{5,4},{6,7},{7,6},{8,9},{9,8},{10,11... | collective-permute-start | bytes 589832 | tf_op jit(solution)/shard_map/ppermute | solution.py:424
  62.1 2.5 %collective-permute-start.11 = (bf16[256,384]{1,0:T(8,128)(2,1)S(1)}, bf16[256,384]{1,0:T(8,128)(2,1)S(1)}, u32[]{:S(2)}, u32[]{:S(2)}) collective-permute-start(bf16[256,384]{1,0:T(8,128)(2,1)S(1)} %collective-permute-done.7.refs_3_), channel_id=1, source_target_pairs={{0,1},{1,0},{2,3},{3,2},{4,5},{5,4},{6,7},{7,6},{8,9},{9,8},{10,11... | collective-permute-start | bytes 589832 | tf_op jit(solution)/shard_map/ppermute | solution.py:424
  64.6 1.4 %collective-permute-start.9 = (bf16[256,384]{1,0:T(8,128)(2,1)S(1)}, bf16[256,384]{1,0:T(8,128)(2,1)S(1)}, u32[]{:S(2)}, u32[]{:S(2)}) collective-permute-start(bf16[256,384]{1,0:T(8,128)(2,1)S(1)} %collective-permute-done.5.refs_1_), channel_id=1, source_target_pairs={{0,1},{1,0},{2,3},{3,2},{4,5},{5,4},{6,7},{7,6},{8,9},{9,8},{10,11... | collective-permute-start | bytes 589832 | tf_op jit(solution)/shard_map/ppermute | solution.py:424
  66.0 2.2 %near_keys.1 = (f32[384,128]{1,0:T(8,128)S(1)}, f32[384,384]{1,0:T(8,128)S(1)}, bf16[384,384]{1,0:T(8,128)(2,1)S(1)}) custom-call(bf16[64,384]{1,0:T(8,128)(2,1)S(1)} %get-tuple-element.25.own_ref, bf16[384,1152]{1,0:T(8,128)(2,1)S(1)} %copy-done.5, bf16[256,384]{1,0:T(8,128)(2,1)S(1)} %constant_dynamic-update-slice_fusion.refs_0_, ...), custom_call_target="tpu_custom_call" | custom-call | flops 1207959552 | bytes 2097152 | tf_op jit(solution)/shard_map/near_keys/pallas_call | solution.py:543
  68.3 3.5 %far_keys.1 = (bf16[64,384]{1,0:T(8,128)(2,1)}, f32[64]{0:T(128)}) custom-call(f32[64,384]{1,0:T(8,128)S(1)} %get-tuple-element.24.tokens_ref, bf16[384,384]{1,0:T(8,128)(2,1)S(1)} %get-tuple-element.26.query_ref, bf16[384,1152]{1,0:T(8,128)(2,1)S(1)} %copy-done.5, bf16[384,384]{1,0:T(8,128)(2,1)S(1)} %copy-done.6, bf16[20,384]{1,0:T(8,128)(2,1)S(1)} %bitcast.1, ...), custom_call_target="tpu_custom_call" | custom-call | flops 1207959552 | bytes 2097152 | tf_op jit(solution)/shard_map/far_keys/pallas_call | solution.py:556
  (44 shorter events, 0.4 us)
Async XLA Ops:
  1.8 17.6 %collective-permute-start = (bf16[2,3,64,384]{3,2,1,0:T(8,128)(2,1)S(1)}, bf16[2,3,64,384]{3,2,1,0:T(8,128)(2,1)S(1)}, u32[]{:S(2)}, u32[]{:S(2)}) collective-permute-start(bf16[2,3,64,384]{3,2,1,0:T(8,128)(2,1)S(1)} %get-tuple-element.32), channel_id=1, source_target_pairs={{0,8},{8,16},{16,24},{1,9},{9,17},{17,25},{2,10},{10,18},{18,26},{... | collective-permute-start | bytes 884744 | tf_op jit(solution)/shard_map/ppermute | solution.py:456
  5.8 3.4 %copy-start = (bf16[2,16,64,384]{3,2,1,0:T(8,128)(2,1)S(1)}, bf16[2,16,64,384]{3,2,1,0:T(8,128)(2,1)}, u32[]{:S(2)}) copy-start(bf16[2,16,64,384]{3,2,1,0:T(8,128)(2,1)} %x_ref.1) | copy-start | bytes 4718596
  5.8 3.4 %copy-start.3 = (bf16[384,1536]{1,0:T(8,128)(2,1)S(1)}, bf16[384,1536]{1,0:T(8,128)(2,1)}, u32[]{:S(2)}) copy-start(bf16[384,1536]{1,0:T(8,128)(2,1)} %we_ref.1) | copy-start | bytes 3538948
  5.8 3.4 %copy-start.4 = (bf16[1536,384]{1,0:T(8,128)(2,1)S(1)}, bf16[1536,384]{1,0:T(8,128)(2,1)}, u32[]{:S(2)}) copy-start(bf16[1536,384]{1,0:T(8,128)(2,1)} %wr_ref.1) | copy-start | bytes 3538948
  5.8 3.4 %copy-start.7 = (bf16[7,7,384]{2,1,0:T(8,128)(2,1)S(1)}, bf16[7,7,384]{2,1,0:T(8,128)(2,1)}, u32[]{:S(2)}) copy-start(bf16[7,7,384]{2,1,0:T(8,128)(2,1)} %dwk_ref.1) | copy-start | bytes 112900
  5.9 3.4 %copy-start.9 = (s32[2,16,64]{2,1,0:T(8,128)S(1)}, s32[2,16,64]{2,1,0:T(8,128)}, u32[]{:S(2)}) copy-start(s32[2,16,64]{2,1,0:T(8,128)} %slot_ref.1) | copy-start | bytes 24580
  5.9 13.5 %collective-permute-start.1 = (bf16[2,3,64,384]{3,2,1,0:T(8,128)(2,1)S(1)}, bf16[2,3,64,384]{3,2,1,0:T(8,128)(2,1)S(1)}, u32[]{:S(2)}, u32[]{:S(2)}) collective-permute-start(bf16[2,3,64,384]{3,2,1,0:T(8,128)(2,1)S(1)} %get-tuple-element.31), channel_id=1, source_target_pairs={{8,0},{16,8},{24,16},{9,1},{17,9},{25,17},{10,2},{18,10},{26,18},{... | collective-permute-start | bytes 884744 | tf_op jit(solution)/shard_map/ppermute | solution.py:457
  8.8 0.7 copy-start.13
  19.4 26.2 %copy-start.1 = (bf16[64,384]{1,0:T(8,128)(2,1)S(1)}, bf16[64,384]{1,0:T(8,128)(2,1)}, u32[]{:S(2)}) copy-start(bf16[64,384]{1,0:T(8,128)(2,1)} %embed_ref.1) | copy-start | bytes 147460
  19.4 26.2 %copy-start.2 = (f32[384]{0:T(512)S(1)}, f32[384]{0:T(512)}, u32[]{:S(2)}) copy-start(f32[384]{0:T(512)} %gain_ref.3) | copy-start | bytes 4612
  19.4 46.6 %copy-start.5 = (bf16[384,1152]{1,0:T(8,128)(2,1)S(1)}, bf16[384,1152]{1,0:T(8,128)(2,1)}, u32[]{:S(2)}) copy-start(bf16[384,1152]{1,0:T(8,128)(2,1)} %wqkv_ref.3) | copy-start | bytes 2654212
  46.5 3.9 %collective-permute-start.2 = (bf16[64,384]{1,0:T(8,128)(2,1)S(1)}, bf16[64,384]{1,0:T(8,128)(2,1)S(1)}, u32[]{:S(2)}, u32[]{:S(2)}) collective-permute-start(bf16[64,384]{1,0:T(8,128)(2,1)S(1)} %get-tuple-element.25.own_ref), channel_id=1, source_target_pairs={{0,16},{8,24},{16,0},{24,8},{1,17},{9,25},{17,1},{25,9},{2,18},{10... | collective-permute-start | bytes 147464 | tf_op jit(solution)/shard_map/ppermute | solution.py:424
  47.0 3.5 %collective-permute-start.3 = (bf16[64,384]{1,0:T(8,128)(2,1)S(1)}, bf16[64,384]{1,0:T(8,128)(2,1)S(1)}, u32[]{:S(2)}, u32[]{:S(2)}) collective-permute-start(bf16[64,384]{1,0:T(8,128)(2,1)S(1)} %get-tuple-element.25.own_ref), channel_id=1, source_target_pairs={{0,8},{8,0},{16,24},{24,16},{1,9},{9,1},{17,25},{25,17},{2,10},{10... | collective-permute-start | bytes 147464 | tf_op jit(solution)/shard_map/ppermute | solution.py:424
  47.3 5.3 %collective-permute-start.4 = (bf16[64,384]{1,0:T(8,128)(2,1)S(1)}, bf16[64,384]{1,0:T(8,128)(2,1)S(1)}, u32[]{:S(2)}, u32[]{:S(2)}) collective-permute-start(bf16[64,384]{1,0:T(8,128)(2,1)S(1)} %get-tuple-element.25.own_ref), channel_id=1, source_target_pairs={{0,24},{8,16},{16,8},{24,0},{1,25},{9,17},{17,9},{25,1},{2,26},{10... | collective-permute-start | bytes 147464 | tf_op jit(solution)/shard_map/ppermute | solution.py:424
  52.6 15.7 %copy-start.6 = (bf16[384,384]{1,0:T(8,128)(2,1)S(1)}, bf16[384,384]{1,0:T(8,128)(2,1)}, u32[]{:S(2)}) copy-start(bf16[384,384]{1,0:T(8,128)(2,1)} %wout_ref.1) | copy-start | bytes 884740
  52.6 15.7 %copy-start.8 = (bf16[384,20]{0,1:T(8,128)(2,1)S(1)}, bf16[384,20]{0,1:T(8,128)(2,1)}, u32[]{:S(2)}) copy-start(bf16[384,20]{0,1:T(8,128)(2,1)} %param.30) | copy-start | bytes 46084
  52.6 15.7 %copy-start.15 = (s32[64]{0:T(128)S(1)}, s32[64]{0:T(128)}, u32[]{:S(2)}) copy-start(s32[64]{0:T(128)} %labels_ref.1) | copy-start | bytes 772
  52.6 5.8 %collective-permute-start.6 = (bf16[256,384]{1,0:T(8,128)(2,1)S(1)}, bf16[256,384]{1,0:T(8,128)(2,1)S(1)}, u32[]{:S(2)}, u32[]{:S(2)}) collective-permute-start(bf16[256,384]{1,0:T(8,128)(2,1)S(1)} %constant_dynamic-update-slice_fusion.refs_0_), channel_id=1, source_target_pairs={{0,2},{1,3},{2,0},{3,1},{4,6},{5,7},{6,4},{7,5},{8,10},{9,11},{10,... | collective-permute-start | bytes 589832 | tf_op jit(solution)/shard_map/ppermute | solution.py:424
  53.6 8.5 %collective-permute-start.7 = (bf16[256,384]{1,0:T(8,128)(2,1)S(1)}, bf16[256,384]{1,0:T(8,128)(2,1)S(1)}, u32[]{:S(2)}, u32[]{:S(2)}) collective-permute-start(bf16[256,384]{1,0:T(8,128)(2,1)S(1)} %constant_dynamic-update-slice_fusion.refs_0_), channel_id=1, source_target_pairs={{0,6},{1,7},{2,4},{3,5},{4,2},{5,3},{6,0},{7,1},{8,14},{9,15},{10,... | collective-permute-start | bytes 589832 | tf_op jit(solution)/shard_map/ppermute | solution.py:424
  54.5 10.1 %collective-permute-start.5 = (bf16[256,384]{1,0:T(8,128)(2,1)S(1)}, bf16[256,384]{1,0:T(8,128)(2,1)S(1)}, u32[]{:S(2)}, u32[]{:S(2)}) collective-permute-start(bf16[256,384]{1,0:T(8,128)(2,1)S(1)} %constant_dynamic-update-slice_fusion.refs_0_), channel_id=1, source_target_pairs={{0,4},{1,5},{2,6},{3,7},{4,0},{5,1},{6,2},{7,3},{8,12},{9,13},{10,... | collective-permute-start | bytes 589832 | tf_op jit(solution)/shard_map/ppermute | solution.py:424
  55.3 12.9 %collective-permute-start.8 = (bf16[256,384]{1,0:T(8,128)(2,1)S(1)}, bf16[256,384]{1,0:T(8,128)(2,1)S(1)}, u32[]{:S(2)}, u32[]{:S(2)}) collective-permute-start(bf16[256,384]{1,0:T(8,128)(2,1)S(1)} %constant_dynamic-update-slice_fusion.refs_0_), channel_id=1, source_target_pairs={{0,1},{1,0},{2,3},{3,2},{4,5},{5,4},{6,7},{7,6},{8,9},{9,8},{10,11... | collective-permute-start | bytes 589832 | tf_op jit(solution)/shard_map/ppermute | solution.py:424
  58.4 9.9 %collective-permute-start.10 = (bf16[256,384]{1,0:T(8,128)(2,1)S(1)}, bf16[256,384]{1,0:T(8,128)(2,1)S(1)}, u32[]{:S(2)}, u32[]{:S(2)}) collective-permute-start(bf16[256,384]{1,0:T(8,128)(2,1)S(1)} %collective-permute-done.6.refs_2_), channel_id=1, source_target_pairs={{0,1},{1,0},{2,3},{3,2},{4,5},{5,4},{6,7},{7,6},{8,9},{9,8},{10,11... | collective-permute-start | bytes 589832 | tf_op jit(solution)/shard_map/ppermute | solution.py:424
  62.1 6.2 %collective-permute-start.11 = (bf16[256,384]{1,0:T(8,128)(2,1)S(1)}, bf16[256,384]{1,0:T(8,128)(2,1)S(1)}, u32[]{:S(2)}, u32[]{:S(2)}) collective-permute-start(bf16[256,384]{1,0:T(8,128)(2,1)S(1)} %collective-permute-done.7.refs_3_), channel_id=1, source_target_pairs={{0,1},{1,0},{2,3},{3,2},{4,5},{5,4},{6,7},{7,6},{8,9},{9,8},{10,11... | collective-permute-start | bytes 589832 | tf_op jit(solution)/shard_map/ppermute | solution.py:424
  64.6 3.7 %collective-permute-start.9 = (bf16[256,384]{1,0:T(8,128)(2,1)S(1)}, bf16[256,384]{1,0:T(8,128)(2,1)S(1)}, u32[]{:S(2)}, u32[]{:S(2)}) collective-permute-start(bf16[256,384]{1,0:T(8,128)(2,1)S(1)} %collective-permute-done.5.refs_1_), channel_id=1, source_target_pairs={{0,1},{1,0},{2,3},{3,2},{4,5},{5,4},{6,7},{7,6},{8,9},{9,8},{10,11... | collective-permute-start | bytes 589832 | tf_op jit(solution)/shard_map/ppermute | solution.py:424
  (4 other events, 2.7 us)

commit v3 on v2

--- a/solution.py
+++ b/solution.py
@@ -15,10 +15,10 @@
 MARGIN = 8
 LANES = 128
 EPS = 1e-06
-HID_CHUNK = 512
 TILE_COLS = 32
+PIECE = 512
 TAP_ROWS = 16
-ROUTE = 1 << 34
+START = 1 << 34
 AXES = ("space", "scene")
 HIGHEST = lax.Precision.HIGHEST
 
@@ -45,74 +45,106 @@
     return jnp.sum(jnp.where(same, jnp.broadcast_to(column, (n, n)), 0), axis=0, keepdims=True)
 
 
-def conv_rows(source, slab, spat, base, wb, bias_ref, width):
-    chans = spat.shape[1]
+def fill(windows, slab, width):
+    for n, window in enumerate(windows):
+        for i, row in enumerate(window):
+            value = row().astype(jnp.float32)
+            for cb in range(slab.shape[1]):
+                slab[n, cb, i, MARGIN : MARGIN + width, :] = value[:, cb * LANES : (cb + 1) * LANES]
+
+
+def conv_tile(n, cb, col, slab, spat, wb, bias_ref, width):
     ksz = dw_size(wb)
-    reach = ksz // 2
-    many = len(source) - ksz + 1
-    for i, row in enumerate(source):
-        value = row().astype(jnp.float32)
-        for cb in range(chans // LANES):
-            slab[cb, i, MARGIN : MARGIN + width, :] = value[:, cb * LANES : (cb + 1) * LANES]
-    for cb in range(chans // LANES):
-        lane = slice(cb * LANES, (cb + 1) * LANES)
-        bias = bias_ref[...].reshape(1, chans)[:, lane]
-        for col in range(0, width, TILE_COLS):
-            parts = range(0, TILE_COLS, TAP_ROWS)
-            total = [[None for _ in parts] for _ in range(many)]
-            for i in range(len(source)):
-                start = MARGIN - reach + col
-                window = [
-                    [
-                        slab[cb, i, start + b + p : start + b + p + TAP_ROWS, :].astype(jnp.bfloat16)
-                        for b in range(ksz)
-                    ]
-                    for p in parts
-                ]
-                for a in range(ksz):
-                    r = i - a
-                    if not 0 <= r < many:
-                        continue
-                    taps = [wb[cb, a * ksz + b] for b in range(ksz)]
-                    for n in range(len(window)):
-                        terms = [v * t for v, t in zip(window[n], taps)]
-                        while len(terms) > 1:
-                            terms = [sum(terms[k : k + 2][1:], terms[k]) for k in range(0, len(terms), 2)]
-                        term = terms[0].astype(jnp.float32)
-                        total[r][n] = term if total[r][n] is None else total[r][n] + term
-            for r in range(many):
-                for n, p in enumerate(parts):
-                    at = base + r * width + col + p
-                    spat[at : at + TAP_ROWS, lane] = total[r][n] + bias
+    start = MARGIN - ksz // 2 + col
+    parts = range(0, TILE_COLS, TAP_ROWS)
+    total = [[None for _ in parts] for _ in range(BLOCK_ROWS)]
+    for i in range(slab.shape[2]):
+        window = [
+            [
+                slab[n, cb, i, start + b + p : start + b + p + TAP_ROWS, :].astype(jnp.bfloat16)
+                for b in range(ksz)
+            ]
+            for p in parts
+        ]
+        for a in range(ksz):
+            r = i - a
+            if not 0 <= r < BLOCK_ROWS:
+                continue
+            taps = [wb[cb, a * ksz + b] for b in range(ksz)]
+            for k in range(len(window)):
+                terms = [v * t for v, t in zip(window[k], taps)]
+                while len(terms) > 1:
+                    terms = [sum(terms[j + 1 : j + 2], terms[j]) for j in range(0, len(terms), 2)]
+                term = terms[0].astype(jnp.float32)
+                total[r][k] = term if total[r][k] is None else total[r][k] + term
+    bias = bias_ref[cb, 0:1, :]
+    for r in range(BLOCK_ROWS):
+        for k, p in enumerate(parts):
+            at = (n * BLOCK_ROWS + r) * width + col + p
+            spat[cb, pl.ds(at, TAP_ROWS), :] = total[r][k] + bias
 
 
 def dw_size(wb):
     return int(wb.shape[1] ** 0.5 + 0.5)
 
 
-def mlp_rows(spat, normed, branch, gain_ref, we_ref, wr_ref):
-    normed[...] = (layer_norm(spat[...]) * gain_ref[...].reshape(1, -1)).astype(jnp.bfloat16)
-    hid = we_ref.shape[1]
-    chunk = min(HID_CHUNK, hid)
-    for start in range(0, hid, chunk):
-        pre = jnp.dot(
-            normed[...], we_ref[:, start : start + chunk], preferred_element_type=jnp.float32
-        )
-        part = jnp.dot(
-            gelu(pre).astype(jnp.bfloat16),
-            wr_ref[start : start + chunk, :],
+def norm_rows(spat, normed, gain_ref):
+    values = jnp.concatenate([spat[cb] for cb in range(spat.shape[0])], axis=1)
+    normed[...] = (layer_norm(values) * gain_ref[...].reshape(1, -1)).astype(jnp.bfloat16)
+
+
+def rows_step(
+    convolve, pointwise, slab, spat, normed, branch, ahead, wb, bias_ref, we_ref, wr_ref, width
+):
+    blocks, chan_blocks = slab.shape[:2]
+    steps = blocks * chan_blocks
+    chunk = we_ref.shape[1] // steps
+    many = normed.shape[0]
+    cols = list(range(0, width, TILE_COLS))
+
+    def expand(part, slot, r):
+        at = part * chunk
+        ahead[slot, r : r + PIECE] = jnp.dot(
+            normed[r : r + PIECE], we_ref[:, pl.ds(at, chunk)], preferred_element_type=jnp.float32
+        )
+
+    def reduce(part, slot, r):
+        at = part * chunk
+        branch[r : r + PIECE] += jnp.dot(
+            gelu(ahead[slot, r : r + PIECE]).astype(jnp.bfloat16),
+            wr_ref[pl.ds(at, chunk), :],
             preferred_element_type=jnp.float32,
         )
-        if start == 0:
-            branch[...] = part
-        else:
-            branch[...] += part
-
-
-def prepare(slab, wb, dwk_ref, width):
-    edge = jnp.zeros(slab.shape[:2] + (MARGIN, LANES), jnp.float32)
-    slab[:, :, 0:MARGIN, :] = edge
-    slab[:, :, MARGIN + width :, :] = edge
+
+    def step(cb, carry):
+        for n in range(blocks):
+            part = cb * blocks + n
+            todo = list(cols) if convolve else []
+            for r in range(0, many, PIECE):
+                if pointwise:
+                    expand(min(part + 1, steps - 1), (n + 1) % blocks, r)
+                    reduce(part, n, r)
+                if todo:
+                    conv_tile(n, cb, todo.pop(0), slab, spat, wb, bias_ref, width)
+            for col in todo:
+                conv_tile(n, cb, col, slab, spat, wb, bias_ref, width)
+        return carry
+
+    if pointwise:
+        branch[...] = jnp.zeros_like(branch)
+        for r in range(0, many, PIECE):
+            expand(0, 0, r)
+    for cb in range(chan_blocks):
+        step(cb, 0)
+
+
+def prepare(slab, wb, bias, dwk_ref, bias_ref, width):
+    edge = jnp.zeros(slab.shape[:3] + (MARGIN, LANES), jnp.float32)
+    slab[:, :, :, 0:MARGIN, :] = edge
+    slab[:, :, :, MARGIN + width :, :] = edge
+    values = bias_ref[...].reshape(1, -1)
+    for cb in range(wb.shape[0]):
+        bias[cb] = jnp.broadcast_to(values[:, cb * LANES : (cb + 1) * LANES], (8, LANES))
     ksz = dwk_ref.shape[0]
     for a in range(ksz):
         kernel = dwk_ref[a].astype(jnp.float32)
@@ -138,33 +170,53 @@
     return jnp.concatenate(pieces, axis=1)
 
 
-def rows_block(
-    scenes, blocks, slots, width, x_ref, slot_ref, slab, spat, normed, branch, wb, bias_ref,
-    gain_ref, we_ref, wr_ref, scale_ref, feat_ref, sums_ref, counts_ref, before_mlp, after_scene,
+def finish_rows(
+    scene, starts, n, slots, width, x_ref, slot_ref, branch, scale_ref, feat_ref, sums_ref,
+    counts_ref, feat_hbm, out_sems,
 ):
-    for scene in range(scenes):
-        base = 0
-        for _, many, window in blocks:
-            conv_rows(window(scene), slab, spat, base, wb, bias_ref, width)
-            base += many * width
-        if scene == 0:
-            before_mlp()
-        mlp_rows(spat, normed, branch, gain_ref, we_ref, wr_ref)
-        center = jnp.concatenate(
-            [x_ref[scene, r : r + n].reshape(n * width, -1) for r, n, _ in blocks], axis=0
-        )
-        feats = (
-            center.astype(jnp.float32) + scale_ref[...].reshape(1, -1) * branch[...]
-        ).astype(jnp.bfloat16)
-        feat_ref[scene] = feats
-        after_scene(scene)
-        member = jnp.concatenate(
-            [membership(slot_ref, scene, r, n, width, slots) for r, n, _ in blocks], axis=1
-        )
-        pool(member, feats, sums_ref, counts_ref)
-
-
-def route_kernel(owners, inter_ref, pos_ref, placer_ref, rows_ref):
+    size = BLOCK_ROWS * width
+    center = jnp.concatenate(
+        [x_ref[scene, r : r + BLOCK_ROWS].reshape(size, -1) for r in starts], axis=0
+    )
+    feats = (
+        center.astype(jnp.float32) + scale_ref[...].reshape(1, -1) * branch[...]
+    ).astype(jnp.bfloat16)
+    feat_ref[n] = feats.reshape(len(starts) * BLOCK_ROWS, width, -1)
+    writes = [
+        pltpu.make_async_copy(
+            feat_ref.at[n, pl.ds(k * BLOCK_ROWS, BLOCK_ROWS)],
+            feat_hbm.at[scene, pl.ds(r, BLOCK_ROWS)],
+            out_sems.at[n, k],
+        )
+        for k, r in enumerate(starts)
+    ]
+    for write in writes:
+        write.start()
+    member = jnp.concatenate(
+        [membership(slot_ref, scene, r, BLOCK_ROWS, width, slots) for r in starts], axis=1
+    )
+    pool(member, feats, sums_ref, counts_ref)
+    return writes
+
+
+def window_rows(scene, row0, reach, rows, x_ref, top_ref, bot_ref):
+    source = []
+    for r in range(row0 - reach, row0 + BLOCK_ROWS + reach):
+        if r < 0:
+            source.append(functools.partial(lambda r: top_ref[scene, r], r + reach))
+        elif r >= rows:
+            source.append(functools.partial(lambda r: bot_ref[scene, r], r - rows))
+        else:
+            source.append(functools.partial(lambda r: x_ref[scene, r], r))
+    return source
+
+
+def start_kernel(sums_ref, counts_ref):
+    sums_ref[...] = jnp.zeros_like(sums_ref)
+    counts_ref[...] = jnp.zeros_like(counts_ref)
+
+
+def route(owners, inter_ref, pos_ref, placer_ref, rows_ref):
     slots = inter_ref.shape[1]
     parcels = pos_ref.shape[0]
     listed = to_column(inter_ref[...], slots)
@@ -188,110 +240,66 @@
 
 
 def inner_kernel(
-    rows, slots, x_hbm, slot_hbm, dwk_hbm, bias_hbm, gain_hbm, we_hbm, wr_hbm, scale_hbm,
-    feat_hbm, sums_ref, counts_ref, x_ref, slot_ref, dwk_ref, bias_ref, gain_ref, we_ref, wr_ref,
-    scale_ref, sems, out_sems, slab, spat, normed, branch, wb, feat_ref,
+    rows, slots, owners, x_ref, slot_ref, dwk_ref, bias_ref, gain_ref, we_ref, wr_ref, scale_ref,
+    sums_in, counts_in, inter_ref, pos_ref,
+    feat_hbm, sums_ref, counts_ref, normed, placer_ref, rows_ref, out_sems, slab, spat, branch, ahead, wb, bias, feat_ref,
 ):
     scenes, _, width, _ = x_ref.shape
-    ksz = dw_size(wb)
-    reach = ksz // 2
-    inside = rows - 2 * BLOCK_ROWS
-    first = [(x_hbm, x_ref), (dwk_hbm, dwk_ref), (bias_hbm, bias_ref)]
-    later = [
-        (slot_hbm, slot_ref), (gain_hbm, gain_ref), (we_hbm, we_ref), (wr_hbm, wr_ref),
-        (scale_hbm, scale_ref),
-    ]
-    copies = [pltpu.make_async_copy(a, b, sems.at[i]) for i, (a, b) in enumerate(first + later)]
-    for copy in copies:
-        copy.start()
-    sums_ref[...] = jnp.zeros_like(sums_ref)
-    counts_ref[...] = jnp.zeros_like(counts_ref)
-    for copy in copies[: len(first)]:
-        copy.wait()
-    prepare(slab, wb, dwk_ref, width)
-
-    def window(scene):
-        return [
-            functools.partial(lambda r: x_ref[scene, r], BLOCK_ROWS - reach + i)
-            for i in range(inside + ksz - 1)
-        ]
-
-    def arrive():
-        for copy in copies[len(first) :]:
-            copy.wait()
-
-    writes = [
-        pltpu.make_async_copy(
-            feat_ref.at[scene, pl.ds(r * width, width)],
-            feat_hbm.at[scene, BLOCK_ROWS + r],
-            out_sems.at[scene, r],
-        )
-        for scene in range(scenes)
-        for r in range(inside)
-    ]
-
-    def leave(scene):
-        for write in writes[scene * inside : (scene + 1) * inside]:
-            write.start()
-
-    rows_block(
-        scenes, [(BLOCK_ROWS, inside, window)], slots, width, x_ref, slot_ref, slab, spat, normed,
-        branch, wb, bias_ref, gain_ref, we_ref, wr_ref, scale_ref, feat_ref, sums_ref, counts_ref,
-        arrive, leave,
-    )
+    reach = dw_size(wb) // 2
+    sums_ref[...] = sums_in[...]
+    counts_ref[...] = counts_in[...]
+    route(owners, inter_ref, pos_ref, placer_ref, rows_ref)
+    prepare(slab, wb, bias, dwk_ref, bias_ref, width)
+    starts = range(BLOCK_ROWS, rows - BLOCK_ROWS, BLOCK_ROWS)
+    writes = []
+    for scene in range(scenes):
+        fill(
+            [window_rows(scene, r, reach, rows, x_ref, None, None) for r in starts], slab, width
+        )
+        rows_step(
+            True, scene > 0, slab, spat, normed, branch, ahead, wb, bias, we_ref, wr_ref, width
+        )
+        if scene > 0:
+            writes += finish_rows(
+                scene - 1, starts, scene - 1, slots, width, x_ref, slot_ref, branch, scale_ref,
+                feat_ref, sums_ref, counts_ref, feat_hbm, out_sems,
+            )
+        norm_rows(spat, normed, gain_ref)
     for write in writes:
         write.wait()
 
 
 def edge_kernel(
     rows, slots, owners, x_ref, top_ref, bot_ref, slot_ref, dwk_ref, bias_ref, gain_ref, we_ref,
-    wr_ref, scale_ref, feat_in, sums_in, counts_in, placer_ref, rows_ref,
-    feat_hbm, sent_ref, out_sems, slab, spat, normed, branch, wb, feat_ref, sums_ref, counts_ref,
+    wr_ref, scale_ref, feat_in, sums_in, counts_in, normed_in, placer_ref, rows_ref,
+    feat_hbm, sent_ref, out_sems, slab, spat, branch, ahead, wb, bias, feat_ref, normed, sums_ref,
+    counts_ref,
 ):
     scenes, _, width, _ = x_ref.shape
-    ksz = dw_size(wb)
-    reach = ksz // 2
-    prepare(slab, wb, dwk_ref, width)
+    reach = dw_size(wb) // 2
     sums_ref[...] = sums_in[...]
     counts_ref[...] = counts_in[...]
-
-    def window(row0):
-        def rows_of(scene):
-            source = []
-            for i in range(BLOCK_ROWS + ksz - 1):
-                r = row0 - reach + i
-                if r < 0:
-                    source.append(functools.partial(lambda r: top_ref[scene, r], r + reach))
-                elif r >= rows:
-                    source.append(functools.partial(lambda r: bot_ref[scene, r], r - rows))
-                else:
-                    source.append(functools.partial(lambda r: x_ref[scene, r], r))
-            return source
-
-        return rows_of
-
-    starts = (0, rows - BLOCK_ROWS)
-    writes = [
-        pltpu.make_async_copy(
-            feat_ref.at[scene, pl.ds((n * BLOCK_ROWS + r) * width, width)],
-            feat_hbm.at[scene, start + r],
-            out_sems.at[scene, n * BLOCK_ROWS + r],
-        )
-        for scene in range(scenes)
-        for n, start in enumerate(starts)
-        for r in range(BLOCK_ROWS)
-    ]
-    each = len(starts) * BLOCK_ROWS
-
-    def leave(scene):
-        for write in writes[scene * each : (scene + 1) * each]:
-            write.start()
-
-    rows_block(
-        scenes, [(start, BLOCK_ROWS, window(start)) for start in starts], slots, width, x_ref,
-        slot_ref, slab, spat, normed, branch, wb, bias_ref, gain_ref, we_ref, wr_ref, scale_ref,
-        feat_ref, sums_ref, counts_ref, lambda: None, leave,
-    )
+    normed[...] = normed_in[...]
+    prepare(slab, wb, bias, dwk_ref, bias_ref, width)
+    inside = range(BLOCK_ROWS, rows - BLOCK_ROWS, BLOCK_ROWS)
+    outside = (0, rows - BLOCK_ROWS)
+    writes = []
+    for n in range(scenes + 1):
+        if n < scenes:
+            fill(
+                [window_rows(n, r, reach, rows, x_ref, top_ref, bot_ref) for r in outside],
+                slab, width,
+            )
+        rows_step(
+            n < scenes, True, slab, spat, normed, branch, ahead, wb, bias, we_ref, wr_ref, width
+        )
+        scene, starts = (scenes - 1, inside) if n == 0 else (n - 1, outside)
+        writes += finish_rows(
+            scene, starts, n, slots, width, x_ref, slot_ref, branch, scale_ref, feat_ref,
+            sums_ref, counts_ref, feat_hbm, out_sems,
+        )
+        if n < scenes:
+            norm_rows(spat, normed, gain_ref)
     placer = placer_ref[...]
     sent = jnp.dot(placer, sums_ref[...], precision=HIGHEST, preferred_element_type=jnp.float32)
     lane = lax.broadcasted_iota(jnp.int32, (slots, LANES), 1)
@@ -456,47 +464,55 @@
     top = lax.ppermute(pixels[:, rows - reach :], "space", up)
     bottom = lax.ppermute(pixels[:, :reach], "space", down)
 
-    inside = rows - 2 * BLOCK_ROWS
-
-    def scratch(many, window):
+    part = rows // 2 * width
+
+    def scratch(times):
+        blocks = rows // 2 // BLOCK_ROWS
         return [
-            pltpu.SemaphoreType.DMA((scenes, many)),
-            pltpu.VMEM((chans // LANES, window, width + 2 * MARGIN, LANES), jnp.float32),
-            pltpu.VMEM((many * width, chans), jnp.float32),
-            pltpu.VMEM((many * width, chans), jnp.bfloat16),
-            pltpu.VMEM((many * width, chans), jnp.float32),
+            pltpu.SemaphoreType.DMA((times, blocks)),
+            pltpu.VMEM(
+                (blocks, chans // LANES, BLOCK_ROWS + ksz - 1, width + 2 * MARGIN, LANES),
+                jnp.float32,
+            ),
+            pltpu.VMEM((chans // LANES, part, LANES), jnp.float32),
+            pltpu.VMEM((part, chans), jnp.float32),
+            pltpu.VMEM(
+                (blocks, part, w_expand.shape[1] // (blocks * (chans // LANES))), jnp.float32
+            ),
             pltpu.VMEM((chans // LANES, ksz * ksz, TAP_ROWS, LANES), jnp.bfloat16),
-            pltpu.VMEM((scenes, many * width, chans), jnp.bfloat16),
+            pltpu.VMEM((chans // LANES, 8, LANES), jnp.float32),
+            pltpu.VMEM((times, rows // 2, width, chans), jnp.bfloat16),
         ]
 
     work = 2 * rows * width * chans * (ksz * ksz + 2 * w_expand.shape[1])
-    placer, local_rows = pl.pallas_call(
-        functools.partial(route_kernel, owners),
+    zero_sums, zero_counts = pl.pallas_call(
+        start_kernel,
         out_shape=(
-            jax.ShapeDtypeStruct((CAP * owners, slots), jnp.float32),
+            jax.ShapeDtypeStruct((slots, chans), jnp.float32),
             jax.ShapeDtypeStruct((slots, LANES), jnp.float32),
         ),
-        in_specs=[VM] * 2,
         out_specs=(VM, VM),
         compiler_params=params(8),
-        cost_estimate=pl.CostEstimate(flops=ROUTE, bytes_accessed=1 << 20, transcendentals=0),
-        name="route",
-    )(intersection, parcel_pos)
+        cost_estimate=pl.CostEstimate(flops=START, bytes_accessed=1 << 20, transcendentals=0),
+        name="start_sums",
+    )()
     inputs = (
-        pixels, pixel_slot, dw_kernel, dw_bias, norm_gain, w_expand, w_reduce, layer_scale
-    )
-    feats, sums, counts = pl.pallas_call(
-        functools.partial(inner_kernel, rows, slots),
+        pixels, pixel_slot, dw_kernel, dw_bias, norm_gain, w_expand, w_reduce, layer_scale,
+        zero_sums, zero_counts, intersection, parcel_pos,
+    )
+    feats, sums, counts, normed, placer, local_rows = pl.pallas_call(
+        functools.partial(inner_kernel, rows, slots, owners),
         out_shape=(
             jax.ShapeDtypeStruct(pixels.shape, jnp.bfloat16),
             jax.ShapeDtypeStruct((slots, chans), jnp.float32),
             jax.ShapeDtypeStruct((slots, LANES), jnp.float32),
+            jax.ShapeDtypeStruct((part, chans), jnp.bfloat16),
+            jax.ShapeDtypeStruct((CAP * owners, slots), jnp.float32),
+            jax.ShapeDtypeStruct((slots, LANES), jnp.float32),
         ),
-        in_specs=[HBM] * len(inputs),
-        out_specs=(HBM, VM, VM),
-        scratch_shapes=[pltpu.VMEM(v.shape, v.dtype) for v in inputs]
-        + [pltpu.SemaphoreType.DMA((len(inputs),))]
-        + scratch(inside, inside + ksz - 1),
+        in_specs=[VM] * len(inputs),
+        out_specs=(HBM, VM, VM, VM, VM, VM),
+        scratch_shapes=scratch(scenes),
         compiler_params=params(),
         cost_estimate=pl.CostEstimate(flops=work, bytes_accessed=6 << 20, transcendentals=0),
         name="inner_rows",
@@ -507,17 +523,21 @@
             jax.ShapeDtypeStruct(pixels.shape, jnp.bfloat16),
             jax.ShapeDtypeStruct((owners, 1, CAP * chans + LANES), jnp.float32),
         ),
-        in_specs=[VM] * 10 + [HBM] + [VM] * 4,
+        in_specs=[VM] * 10 + [HBM] + [VM] * 5,
         out_specs=(HBM, VM),
         input_output_aliases={10: 0},
-        scratch_shapes=scratch(2 * BLOCK_ROWS, BLOCK_ROWS + ksz - 1)
-        + [pltpu.VMEM((slots, chans), jnp.float32), pltpu.VMEM((slots, LANES), jnp.float32)],
+        scratch_shapes=scratch(scenes + 1)
+        + [
+            pltpu.VMEM((part, chans), jnp.bfloat16),
+            pltpu.VMEM((slots, chans), jnp.float32),
+            pltpu.VMEM((slots, LANES), jnp.float32),
+        ],
         compiler_params=params(),
         cost_estimate=pl.CostEstimate(flops=work, bytes_accessed=6 << 20, transcendentals=0),
         name="edge_rows",
     )(
-        pixels, top, bottom, pixel_slot, dw_kernel, dw_bias, norm_gain, w_expand, w_reduce, layer_scale,
-        feats, sums, counts, placer, local_rows,
+        pixels, top, bottom, pixel_slot, dw_kernel, dw_bias, norm_gain, w_expand, w_reduce,
+        layer_scale, feats, sums, counts, normed, placer, local_rows,
     )
     arrived = lax.all_to_all(sent, AXES, split_axis=0, concat_axis=0, tiled=True)
     tokens, attn_in = pl.pallas_call(

time: 72.1 us -> 68.6 us (0.951)
  waiting for transfers between devices: 2.39 us -> 6.39 us
  starting transfers between devices: 22.6 us -> 18.8 us
  blocking collectives: 16.1 us -> 14.5 us
  local copies, waits for them, and re-layouts: 2.85 us -> 1.26 us
    ppermute x10, starting transfers between devices: 17 us -> 12.6 us  [xor_permute(): return lax.ppermute(x, axis, [(i, i ^ mask) for i in range(count)])]
    ppermute x10, waiting for transfers between devices: 2.38 us -> 6.39 us  [xor_permute(): return lax.ppermute(x, axis, [(i, i ^ mask) for i in range(count)])]
    pallas_call x2, Pallas kernels: 10.2 us -> 7.77 us  [the longest x1 7.76 us: local(): pl.pallas_call(functools.partial(inner_kernel, rows, slots, owners), out_...]
    pallas_call x1, Pallas kernels: 10 us -> 12 us  [local(): pl.pallas_call(functools.partial(edge_kernel, rows, slots, owners), out_s...]
    all_to_all x1, blocking collectives: 16.1 us -> 14.5 us  [local(): lax.all_to_all(sent, AXES, split_axis=0, concat_axis=0, tiled=True)]
    unnamed x35, local copies, waits for them, and re-layouts: 1.72 us -> 0.13 us
    ppermute x1, starting transfers between devices: 4.05 us -> 4.94 us  [local(): top = lax.ppermute(pixels[:, rows - reach:], 'space', up)]
  transfers between devices with their start and end apart: 12 -> 12, of which waited for: 2 -> 3; matrix products, arithmetic and copies ran while one was open for 0% -> 0% of each run, Pallas kernels for 17% -> 15%
where the time goes in v3:
time: 68.6 us; the launch traced here: 68.4 us
  Pallas kernels  26.5 us (39%)
  starting transfers between devices  18.8 us (27%)
  blocking collectives  14.5 us (21%)
  waiting for transfers between devices  6.39 us (9%)
  local copies, waits for them, and re-layouts  1.26 us (2%)
  between operations  1.01 us (1%)
    all_to_all x1, blocking collectives, local(): lax.all_to_all(sent, AXES, split_axis=0, concat_axis=0, tiled=True)  14.5 us
    ppermute x10, starting transfers between devices, xor_permute(): return lax.ppermute(x, axis, [(i, i ^ mask) for i in range(count)])  12.6 us
    pallas_call x1, Pallas kernels, local(): pl.pallas_call(functools.partial(edge_kernel, rows, slots, owners), out_s...  12 us
    pallas_call x1, Pallas kernels, local(): pl.pallas_call(functools.partial(inner_kernel, rows, slots, owners), out_...  7.76 us
    ppermute x10, waiting for transfers between devices, xor_permute(): return lax.ppermute(x, axis, [(i, i ^ mask) for i in range(count)])  6.39 us
    ppermute x1, starting transfers between devices, local(): top = lax.ppermute(pixels[:, rows - reach:], 'space', up)  4.94 us
    pallas_call x1, Pallas kernels, local(): pl.pallas_call(functools.partial(far_kernel, len(far)), out_shape=(jax.Sh...  3.51 us
    pallas_call x1, Pallas kernels, local(): pl.pallas_call(functools.partial(near_kernel, len(held)), out_shape=(jax....  2.21 us
  transfers between devices with their start and end apart: 12, of which 3 were waited for; matrix products, arithmetic and copies ran while one was open for 0% of the time, Pallas kernels for 15%

profile of v3, /device:TPU:1, one launch (start us, length us, event | category | flops | bytes accessed | tf_op | source)
XLA Modules:
  0.0 68.4 jit_solution(13983528256266333535)
XLA Ops:
  0.6 1.1 %fusion = (bf16[2,3,64,384]{3,2,1,0:T(8,128)(2,1)S(1)}, bf16[2,3,64,384]{3,2,1,0:T(8,128)(2,1)S(1)}) fusion(bf16[2,16,64,384]{3,2,1,0:T(8,128)(2,1)} %x_ref.3), kind=kLoop, calls=%fused_computation.4 | loop fusion | bytes 1179648 | tf_op jit(solution)/shard_map/slice | solution.py:465
  1.8 1.3 %collective-permute-start.1 = (bf16[2,3,64,384]{3,2,1,0:T(8,128)(2,1)S(1)}, bf16[2,3,64,384]{3,2,1,0:T(8,128)(2,1)S(1)}, u32[]{:S(2)}, u32[]{:S(2)}) collective-permute-start(bf16[2,3,64,384]{3,2,1,0:T(8,128)(2,1)S(1)} %get-tuple-element.37), channel_id=1, source_target_pairs={{8,0},{16,8},{24,16},{9,1},{17,9},{25,17},{10,2},{18,10},{26,18},{... | collective-permute-start | bytes 884744 | tf_op jit(solution)/shard_map/ppermute | solution.py:465
  3.1 0.0 copy-start
  3.1 0.0 copy-start.3
  3.2 4.9 %collective-permute-start = (bf16[2,3,64,384]{3,2,1,0:T(8,128)(2,1)S(1)}, bf16[2,3,64,384]{3,2,1,0:T(8,128)(2,1)S(1)}, u32[]{:S(2)}, u32[]{:S(2)}) collective-permute-start(bf16[2,3,64,384]{3,2,1,0:T(8,128)(2,1)S(1)} %get-tuple-element.38), channel_id=1, source_target_pairs={{0,8},{8,16},{16,24},{1,9},{9,17},{17,25},{2,10},{10,18},{18,26},{... | collective-permute-start | bytes 884744 | tf_op jit(solution)/shard_map/ppermute | solution.py:464
  8.2 7.8 %inner_rows.1 = (bf16[2,16,64,384]{3,2,1,0:T(8,128)(2,1)}, f32[64,384]{1,0:T(8,128)S(1)}, f32[64,128]{1,0:T(8,128)S(1)}, bf16[512,384]{1,0:T(8,128)(2,1)S(1)}, f...) custom-call(bf16[2,16,64,384]{3,2,1,0:T(8,128)(2,1)S(1)} %copy-done, s32[2,16,64]{2,1,0:T(8,128)S(1)} %copy-done.9, ...), custom_call_target="tpu_custom_call" | custom-call | flops 2454454272 | bytes 6291456 | tf_op jit(solution)/shard_map/inner_rows/pallas_call | solution.py:503
  16.1 12.0 %edge_rows.1 = (bf16[2,16,64,384]{3,2,1,0:T(8,128)(2,1)}, f32[32,1,1280]{2,1,0:T(1,128)S(1)}) custom-call(bf16[2,16,64,384]{3,2,1,0:T(8,128)(2,1)S(1)} %copy-done, bf16[2,3,64,384]{3,2,1,0:T(8,128)(2,1)S(1)} %collective-permute-done.top_ref, bf16[2,3,64,384]{3,2,1,0:T(8,128)(2,1)S(1)} %collective-permute-done.1.bot_ref, ...), custom_call_target="tpu_custom_call", output_to_operand_aliasing={{0}: (10, {})} | custom-call | flops 2454454272 | bytes 6291456 | tf_op jit(solution)/shard_map/edge_rows/pallas_call | solution.py:520
  28.1 14.5 %all_to_all.5.recv_ref = f32[32,1,1280]{2,1,0:T(1,128)S(1)} all-to-all(f32[32,1,1280]{2,1,0:T(1,128)S(1)} %get-tuple-element.29), channel_id=1, replica_groups=mesh['space'=4,'scene'=8] {'space','scene'}, dimensions={0} | all-to-all | bytes 327680 | tf_op jit(solution)/shard_map/all_to_all | solution.py:542
  42.6 0.9 %own_tokens.1 = (f32[64,384]{1,0:T(8,128)S(1)}, bf16[64,384]{1,0:T(8,128)(2,1)S(1)}) custom-call(f32[32,1,1280]{2,1,0:T(1,128)S(1)} %all_to_all.5.recv_ref, bf16[64,384]{1,0:T(8,128)(2,1)S(1)} %copy-done.1, f32[384]{0:T(512)S(1)} %copy-done.2), custom_call_target="tpu_custom_call" | custom-call | tf_op jit(solution)/shard_map/own_tokens/pallas_call | solution.py:543
  43.6 0.5 collective-permute-start.4
  44.0 0.2 collective-permute-start.3
  44.3 2.9 %collective-permute-start.2 = (bf16[64,384]{1,0:T(8,128)(2,1)S(1)}, bf16[64,384]{1,0:T(8,128)(2,1)S(1)}, u32[]{:S(2)}, u32[]{:S(2)}) collective-permute-start(bf16[64,384]{1,0:T(8,128)(2,1)S(1)} %get-tuple-element.31.own_ref), channel_id=1, source_target_pairs={{0,16},{8,24},{16,0},{24,8},{1,17},{9,25},{17,1},{25,9},{2,18},{10... | collective-permute-start | bytes 147464 | tf_op jit(solution)/shard_map/ppermute | solution.py:432
  47.2 2.9 %collective-permute-done.2 = bf16[64,384]{1,0:T(8,128)(2,1)S(1)} collective-permute-done((bf16[64,384]{1,0:T(8,128)(2,1)S(1)}, bf16[64,384]{1,0:T(8,128)(2,1)S(1)}, u32[]{:S(2)}, u32[]{:S(2)}) %collective-permute-start.2) | collective-permute-done | bytes 49184 | tf_op jit(solution)/shard_map/ppermute | solution.py:432
  50.2 0.1 collective-permute-start.7
  50.2 0.1 collective-permute-start.6
  50.3 2.6 %collective-permute-start.5 = (bf16[256,384]{1,0:T(8,128)(2,1)S(1)}, bf16[256,384]{1,0:T(8,128)(2,1)S(1)}, u32[]{:S(2)}, u32[]{:S(2)}) collective-permute-start(bf16[256,384]{1,0:T(8,128)(2,1)S(1)} %constant_dynamic-update-slice_fusion.refs_0_), channel_id=1, source_target_pairs={{0,4},{1,5},{2,6},{3,7},{4,0},{5,1},{6,2},{7,3},{8,12},{9,13},{10,... | collective-permute-start | bytes 589832 | tf_op jit(solution)/shard_map/ppermute | solution.py:432
  52.9 2.0 %collective-permute-start.8 = (bf16[256,384]{1,0:T(8,128)(2,1)S(1)}, bf16[256,384]{1,0:T(8,128)(2,1)S(1)}, u32[]{:S(2)}, u32[]{:S(2)}) collective-permute-start(bf16[256,384]{1,0:T(8,128)(2,1)S(1)} %constant_dynamic-update-slice_fusion.refs_0_), channel_id=1, source_target_pairs={{0,1},{1,0},{2,3},{3,2},{4,5},{5,4},{6,7},{7,6},{8,9},{9,8},{10,11... | collective-permute-start | bytes 589832 | tf_op jit(solution)/shard_map/ppermute | solution.py:432
  54.8 1.6 %collective-permute-done.7.refs_3_ = bf16[256,384]{1,0:T(8,128)(2,1)S(1)} collective-permute-done((bf16[256,384]{1,0:T(8,128)(2,1)S(1)}, bf16[256,384]{1,0:T(8,128)(2,1)S(1)}, u32[]{:S(2)}, u32[]{:S(2)}) %collective-permute-start.7) | collective-permute-done | bytes 196640 | tf_op jit(solution)/shard_map/ppermute | solution.py:432
  56.4 3.7 %collective-permute-start.11 = (bf16[256,384]{1,0:T(8,128)(2,1)S(1)}, bf16[256,384]{1,0:T(8,128)(2,1)S(1)}, u32[]{:S(2)}, u32[]{:S(2)}) collective-permute-start(bf16[256,384]{1,0:T(8,128)(2,1)S(1)} %collective-permute-done.7.refs_3_), channel_id=1, source_target_pairs={{0,1},{1,0},{2,3},{3,2},{4,5},{5,4},{6,7},{7,6},{8,9},{9,8},{10,11... | collective-permute-start | bytes 589832 | tf_op jit(solution)/shard_map/ppermute | solution.py:432
  60.1 0.1 collective-permute-start.10
  60.3 1.9 %collective-permute-done.5.refs_1_ = bf16[256,384]{1,0:T(8,128)(2,1)S(1)} collective-permute-done((bf16[256,384]{1,0:T(8,128)(2,1)S(1)}, bf16[256,384]{1,0:T(8,128)(2,1)S(1)}, u32[]{:S(2)}, u32[]{:S(2)}) %collective-permute-start.5) | collective-permute-done | bytes 196640 | tf_op jit(solution)/shard_map/ppermute | solution.py:432
  62.2 0.5 collective-permute-start.9
  62.7 2.2 %near_keys.1 = (f32[384,128]{1,0:T(8,128)S(1)}, f32[384,384]{1,0:T(8,128)S(1)}, bf16[384,384]{1,0:T(8,128)(2,1)S(1)}) custom-call(bf16[64,384]{1,0:T(8,128)(2,1)S(1)} %get-tuple-element.31.own_ref, bf16[384,1152]{1,0:T(8,128)(2,1)S(1)} %copy-done.5, bf16[256,384]{1,0:T(8,128)(2,1)S(1)} %constant_dynamic-update-slice_fusion.refs_0_, ...), custom_call_target="tpu_custom_call" | custom-call | flops 1207959552 | bytes 2097152 | tf_op jit(solution)/shard_map/near_keys/pallas_call | solution.py:563
  64.9 3.5 %far_keys.1 = (bf16[64,384]{1,0:T(8,128)(2,1)}, f32[64]{0:T(128)}) custom-call(f32[64,384]{1,0:T(8,128)S(1)} %get-tuple-element.30.tokens_ref, bf16[384,384]{1,0:T(8,128)(2,1)S(1)} %get-tuple-element.32.query_ref, bf16[384,1152]{1,0:T(8,128)(2,1)S(1)} %copy-done.5, bf16[384,384]{1,0:T(8,128)(2,1)S(1)} %copy-done.6, bf16[20,384]{1,0:T(8,128)(2,1)S(1)} %bitcast.1, ...), custom_call_target="tpu_custom_call" | custom-call | flops 1207959552 | bytes 2097152 | tf_op jit(solution)/shard_map/far_keys/pallas_call | solution.py:576
  (44 shorter events, 0.2 us)
Async XLA Ops:
  1.8 14.3 %collective-permute-start.1 = (bf16[2,3,64,384]{3,2,1,0:T(8,128)(2,1)S(1)}, bf16[2,3,64,384]{3,2,1,0:T(8,128)(2,1)S(1)}, u32[]{:S(2)}, u32[]{:S(2)}) collective-permute-start(bf16[2,3,64,384]{3,2,1,0:T(8,128)(2,1)S(1)} %get-tuple-element.37), channel_id=1, source_target_pairs={{8,0},{16,8},{24,16},{9,1},{17,9},{25,17},{10,2},{18,10},{26,18},{... | collective-permute-start | bytes 884744 | tf_op jit(solution)/shard_map/ppermute | solution.py:465
  3.1 5.1 %copy-start = (bf16[2,16,64,384]{3,2,1,0:T(8,128)(2,1)S(1)}, bf16[2,16,64,384]{3,2,1,0:T(8,128)(2,1)}, u32[]{:S(2)}) copy-start(bf16[2,16,64,384]{3,2,1,0:T(8,128)(2,1)} %x_ref.3) | copy-start | bytes 4718596
  3.1 5.1 %copy-start.3 = (bf16[384,1536]{1,0:T(8,128)(2,1)S(1)}, bf16[384,1536]{1,0:T(8,128)(2,1)}, u32[]{:S(2)}) copy-start(bf16[384,1536]{1,0:T(8,128)(2,1)} %we_ref.3) | copy-start | bytes 3538948
  3.1 5.1 %copy-start.4 = (bf16[1536,384]{1,0:T(8,128)(2,1)S(1)}, bf16[1536,384]{1,0:T(8,128)(2,1)}, u32[]{:S(2)}) copy-start(bf16[1536,384]{1,0:T(8,128)(2,1)} %wr_ref.3) | copy-start | bytes 3538948
  3.1 5.1 %copy-start.7 = (bf16[7,7,384]{2,1,0:T(8,128)(2,1)S(1)}, bf16[7,7,384]{2,1,0:T(8,128)(2,1)}, u32[]{:S(2)}) copy-start(bf16[7,7,384]{2,1,0:T(8,128)(2,1)} %dwk_ref.3) | copy-start | bytes 112900
  3.1 5.1 %copy-start.9 = (s32[2,16,64]{2,1,0:T(8,128)S(1)}, s32[2,16,64]{2,1,0:T(8,128)}, u32[]{:S(2)}) copy-start(s32[2,16,64]{2,1,0:T(8,128)} %slot_ref.3) | copy-start | bytes 24580
  3.1 5.1 %copy-start.10 = (s32[2048]{0:T(1024)S(1)}, s32[2048]{0:T(1024)}, u32[]{:S(2)}) copy-start(s32[2048]{0:T(1024)} %pos_ref.1) | copy-start | bytes 24580
  3.2 12.8 %collective-permute-start = (bf16[2,3,64,384]{3,2,1,0:T(8,128)(2,1)S(1)}, bf16[2,3,64,384]{3,2,1,0:T(8,128)(2,1)S(1)}, u32[]{:S(2)}, u32[]{:S(2)}) collective-permute-start(bf16[2,3,64,384]{3,2,1,0:T(8,128)(2,1)S(1)} %get-tuple-element.38), channel_id=1, source_target_pairs={{0,8},{8,16},{16,24},{1,9},{9,17},{17,25},{2,10},{10,18},{18,26},{... | collective-permute-start | bytes 884744 | tf_op jit(solution)/shard_map/ppermute | solution.py:464
  16.0 26.6 %copy-start.1 = (bf16[64,384]{1,0:T(8,128)(2,1)S(1)}, bf16[64,384]{1,0:T(8,128)(2,1)}, u32[]{:S(2)}) copy-start(bf16[64,384]{1,0:T(8,128)(2,1)} %embed_ref.1) | copy-start | bytes 147460
  16.0 26.6 %copy-start.2 = (f32[384]{0:T(512)S(1)}, f32[384]{0:T(512)}, u32[]{:S(2)}) copy-start(f32[384]{0:T(512)} %gain_ref.5) | copy-start | bytes 4612
  16.0 46.6 %copy-start.5 = (bf16[384,1152]{1,0:T(8,128)(2,1)S(1)}, bf16[384,1152]{1,0:T(8,128)(2,1)}, u32[]{:S(2)}) copy-start(bf16[384,1152]{1,0:T(8,128)(2,1)} %wqkv_ref.3) | copy-start | bytes 2654212
  43.6 6.5 %collective-permute-start.4 = (bf16[64,384]{1,0:T(8,128)(2,1)S(1)}, bf16[64,384]{1,0:T(8,128)(2,1)S(1)}, u32[]{:S(2)}, u32[]{:S(2)}) collective-permute-start(bf16[64,384]{1,0:T(8,128)(2,1)S(1)} %get-tuple-element.31.own_ref), channel_id=1, source_target_pairs={{0,24},{8,16},{16,8},{24,0},{1,25},{9,17},{17,9},{25,1},{2,26},{10... | collective-permute-start | bytes 147464 | tf_op jit(solution)/shard_map/ppermute | solution.py:432
  44.0 6.0 %collective-permute-start.3 = (bf16[64,384]{1,0:T(8,128)(2,1)S(1)}, bf16[64,384]{1,0:T(8,128)(2,1)S(1)}, u32[]{:S(2)}, u32[]{:S(2)}) collective-permute-start(bf16[64,384]{1,0:T(8,128)(2,1)S(1)} %get-tuple-element.31.own_ref), channel_id=1, source_target_pairs={{0,8},{8,0},{16,24},{24,16},{1,9},{9,1},{17,25},{25,17},{2,10},{10... | collective-permute-start | bytes 147464 | tf_op jit(solution)/shard_map/ppermute | solution.py:432
  44.3 5.8 %collective-permute-start.2 = (bf16[64,384]{1,0:T(8,128)(2,1)S(1)}, bf16[64,384]{1,0:T(8,128)(2,1)S(1)}, u32[]{:S(2)}, u32[]{:S(2)}) collective-permute-start(bf16[64,384]{1,0:T(8,128)(2,1)S(1)} %get-tuple-element.31.own_ref), channel_id=1, source_target_pairs={{0,16},{8,24},{16,0},{24,8},{1,17},{9,25},{17,1},{25,9},{2,18},{10... | collective-permute-start | bytes 147464 | tf_op jit(solution)/shard_map/ppermute | solution.py:432
  50.1 14.8 %copy-start.6 = (bf16[384,384]{1,0:T(8,128)(2,1)S(1)}, bf16[384,384]{1,0:T(8,128)(2,1)}, u32[]{:S(2)}) copy-start(bf16[384,384]{1,0:T(8,128)(2,1)} %wout_ref.1) | copy-start | bytes 884740
  50.1 14.8 %copy-start.8 = (bf16[384,20]{0,1:T(8,128)(2,1)S(1)}, bf16[384,20]{0,1:T(8,128)(2,1)}, u32[]{:S(2)}) copy-start(bf16[384,20]{0,1:T(8,128)(2,1)} %param.30) | copy-start | bytes 46084
  50.1 14.8 %copy-start.15 = (s32[64]{0:T(128)S(1)}, s32[64]{0:T(128)}, u32[]{:S(2)}) copy-start(s32[64]{0:T(128)} %labels_ref.1) | copy-start | bytes 772
  50.2 6.3 %collective-permute-start.7 = (bf16[256,384]{1,0:T(8,128)(2,1)S(1)}, bf16[256,384]{1,0:T(8,128)(2,1)S(1)}, u32[]{:S(2)}, u32[]{:S(2)}) collective-permute-start(bf16[256,384]{1,0:T(8,128)(2,1)S(1)} %constant_dynamic-update-slice_fusion.refs_0_), channel_id=1, source_target_pairs={{0,6},{1,7},{2,4},{3,5},{4,2},{5,3},{6,0},{7,1},{8,14},{9,15},{10,... | collective-permute-start | bytes 589832 | tf_op jit(solution)/shard_map/ppermute | solution.py:432
  50.2 9.9 %collective-permute-start.6 = (bf16[256,384]{1,0:T(8,128)(2,1)S(1)}, bf16[256,384]{1,0:T(8,128)(2,1)S(1)}, u32[]{:S(2)}, u32[]{:S(2)}) collective-permute-start(bf16[256,384]{1,0:T(8,128)(2,1)S(1)} %constant_dynamic-update-slice_fusion.refs_0_), channel_id=1, source_target_pairs={{0,2},{1,3},{2,0},{3,1},{4,6},{5,7},{6,4},{7,5},{8,10},{9,11},{10,... | collective-permute-start | bytes 589832 | tf_op jit(solution)/shard_map/ppermute | solution.py:432
  50.3 11.8 %collective-permute-start.5 = (bf16[256,384]{1,0:T(8,128)(2,1)S(1)}, bf16[256,384]{1,0:T(8,128)(2,1)S(1)}, u32[]{:S(2)}, u32[]{:S(2)}) collective-permute-start(bf16[256,384]{1,0:T(8,128)(2,1)S(1)} %constant_dynamic-update-slice_fusion.refs_0_), channel_id=1, source_target_pairs={{0,4},{1,5},{2,6},{3,7},{4,0},{5,1},{6,2},{7,3},{8,12},{9,13},{10,... | collective-permute-start | bytes 589832 | tf_op jit(solution)/shard_map/ppermute | solution.py:432
  52.9 12.0 %collective-permute-start.8 = (bf16[256,384]{1,0:T(8,128)(2,1)S(1)}, bf16[256,384]{1,0:T(8,128)(2,1)S(1)}, u32[]{:S(2)}, u32[]{:S(2)}) collective-permute-start(bf16[256,384]{1,0:T(8,128)(2,1)S(1)} %constant_dynamic-update-slice_fusion.refs_0_), channel_id=1, source_target_pairs={{0,1},{1,0},{2,3},{3,2},{4,5},{5,4},{6,7},{7,6},{8,9},{9,8},{10,11... | collective-permute-start | bytes 589832 | tf_op jit(solution)/shard_map/ppermute | solution.py:432
  56.4 8.4 %collective-permute-start.11 = (bf16[256,384]{1,0:T(8,128)(2,1)S(1)}, bf16[256,384]{1,0:T(8,128)(2,1)S(1)}, u32[]{:S(2)}, u32[]{:S(2)}) collective-permute-start(bf16[256,384]{1,0:T(8,128)(2,1)S(1)} %collective-permute-done.7.refs_3_), channel_id=1, source_target_pairs={{0,1},{1,0},{2,3},{3,2},{4,5},{5,4},{6,7},{7,6},{8,9},{9,8},{10,11... | collective-permute-start | bytes 589832 | tf_op jit(solution)/shard_map/ppermute | solution.py:432
  60.1 4.8 %collective-permute-start.10 = (bf16[256,384]{1,0:T(8,128)(2,1)S(1)}, bf16[256,384]{1,0:T(8,128)(2,1)S(1)}, u32[]{:S(2)}, u32[]{:S(2)}) collective-permute-start(bf16[256,384]{1,0:T(8,128)(2,1)S(1)} %collective-permute-done.6.refs_2_), channel_id=1, source_target_pairs={{0,1},{1,0},{2,3},{3,2},{4,5},{5,4},{6,7},{7,6},{8,9},{9,8},{10,11... | collective-permute-start | bytes 589832 | tf_op jit(solution)/shard_map/ppermute | solution.py:432
  62.2 2.7 %collective-permute-start.9 = (bf16[256,384]{1,0:T(8,128)(2,1)S(1)}, bf16[256,384]{1,0:T(8,128)(2,1)S(1)}, u32[]{:S(2)}, u32[]{:S(2)}) collective-permute-start(bf16[256,384]{1,0:T(8,128)(2,1)S(1)} %collective-permute-done.5.refs_1_), channel_id=1, source_target_pairs={{0,1},{1,0},{2,3},{3,2},{4,5},{5,4},{6,7},{7,6},{8,9},{9,8},{10,11... | collective-permute-start | bytes 589832 | tf_op jit(solution)/shard_map/ppermute | solution.py:432
  (4 other events, 20.3 us)

commit v4 on v3

--- a/solution.py
+++ b/solution.py
@@ -199,13 +199,13 @@
     return writes
 
 
-def window_rows(scene, row0, reach, rows, x_ref, top_ref, bot_ref):
+def window_rows(scene, row0, reach, rows, x_ref, top, bottom):
     source = []
     for r in range(row0 - reach, row0 + BLOCK_ROWS + reach):
         if r < 0:
-            source.append(functools.partial(lambda r: top_ref[scene, r], r + reach))
+            source.append(functools.partial(top, scene, r + reach))
         elif r >= rows:
-            source.append(functools.partial(lambda r: bot_ref[scene, r], r - rows))
+            source.append(functools.partial(bottom, scene, r - rows))
         else:
             source.append(functools.partial(lambda r: x_ref[scene, r], r))
     return source
@@ -270,7 +270,7 @@
 
 
 def edge_kernel(
-    rows, slots, owners, x_ref, top_ref, bot_ref, slot_ref, dwk_ref, bias_ref, gain_ref, we_ref,
+    rows, slots, owners, x_ref, pair_ref, next_ref, slot_ref, dwk_ref, bias_ref, gain_ref, we_ref,
     wr_ref, scale_ref, feat_in, sums_in, counts_in, normed_in, placer_ref, rows_ref,
     feat_hbm, sent_ref, out_sems, slab, spat, branch, ahead, wb, bias, feat_ref, normed, sums_ref,
     counts_ref,
@@ -283,11 +283,20 @@
     prepare(slab, wb, bias, dwk_ref, bias_ref, width)
     inside = range(BLOCK_ROWS, rows - BLOCK_ROWS, BLOCK_ROWS)
     outside = (0, rows - BLOCK_ROWS)
+    even = lax.rem(lax.axis_index("space"), 2) == 0
+
+    def halo(of_even, of_odd, scene, r):
+        return jnp.where(
+            even, of_even[scene, r].astype(jnp.float32), of_odd[scene, r].astype(jnp.float32)
+        )
+
+    top = functools.partial(halo, next_ref, pair_ref)
+    bottom = functools.partial(halo, pair_ref, next_ref)
     writes = []
     for n in range(scenes + 1):
         if n < scenes:
             fill(
-                [window_rows(n, r, reach, rows, x_ref, top_ref, bot_ref) for r in outside],
+                [window_rows(n, r, reach, rows, x_ref, top, bottom) for r in outside],
                 slab, width,
             )
         rows_step(
@@ -459,10 +468,13 @@
     slots = intersection.shape[1]
     owners = lax.axis_size("space") * lax.axis_size("scene")
     count = lax.axis_size("space")
-    up = [(i, i + 1) for i in range(count - 1)]
-    down = [(i + 1, i) for i in range(count - 1)]
-    top = lax.ppermute(pixels[:, rows - reach :], "space", up)
-    bottom = lax.ppermute(pixels[:, :reach], "space", down)
+    even = lax.rem(lax.axis_index("space"), 2) == 0
+    head, tail = pixels[:, :reach], pixels[:, rows - reach :]
+    pairs = [(i, i ^ 1) for i in range(count)]
+    nexts = [(i, i + 1) for i in range(1, count - 1, 2)]
+    nexts += [(j, i) for i, j in nexts]
+    pair_halo = lax.ppermute(jnp.where(even, tail, head), "space", pairs)
+    next_halo = lax.ppermute(jnp.where(even, head, tail), "space", nexts)
 
     part = rows // 2 * width
 
@@ -536,7 +548,7 @@
         cost_estimate=pl.CostEstimate(flops=work, bytes_accessed=6 << 20, transcendentals=0),
         name="edge_rows",
     )(
-        pixels, top, bottom, pixel_slot, dw_kernel, dw_bias, norm_gain, w_expand, w_reduce,
+        pixels, pair_halo, next_halo, pixel_slot, dw_kernel, dw_bias, norm_gain, w_expand, w_reduce,
         layer_scale, feats, sums, counts, normed, placer, local_rows,
     )
     arrived = lax.all_to_all(sent, AXES, split_axis=0, concat_axis=0, tiled=True)

time: 68.6 us -> 66.9 us (0.975)
  other arithmetic: 0 us -> 1.12 us
  local copies, waits for them, and re-layouts: 1.26 us -> 0.14 us
  blocking collectives: 14.5 us -> 13.6 us
  starting transfers between devices: 18.8 us -> 18 us
    slice x1 -> x0, local copies, waits for them, and re-layouts: 1.12 us -> none  [local(): bottom = lax.ppermute(pixels[:, :reach], 'space', down)]
    select_n x0 -> x1, other arithmetic: none -> 1.12 us  [local(): next_halo = lax.ppermute(jnp.where(even, head, tail), 'space', nexts)]
    all_to_all x1, blocking collectives: 14.5 us -> 13.6 us  [local(): lax.all_to_all(sent, AXES, split_axis=0, concat_axis=0, tiled=True)]
    ppermute x2, starting transfers between devices: 6.23 us -> 5.4 us  [the longest x1 4.72 us: local(): pair_halo = lax.ppermute(jnp.where(even, tail, head), 'space', pairs)]
where the time goes in v4:
time: 66.9 us; the launch traced here: 66.7 us
  Pallas kernels  26.5 us (40%)
  starting transfers between devices  18 us (27%)
  blocking collectives  13.6 us (20%)
  waiting for transfers between devices  6.39 us (10%)
  other arithmetic  1.12 us (2%)
  between operations  1.01 us (2%)
    all_to_all x1, blocking collectives, local(): lax.all_to_all(sent, AXES, split_axis=0, concat_axis=0, tiled=True)  13.6 us
    ppermute x10, starting transfers between devices, xor_permute(): return lax.ppermute(x, axis, [(i, i ^ mask) for i in range(count)])  12.6 us
    pallas_call x1, Pallas kernels, local(): pl.pallas_call(functools.partial(edge_kernel, rows, slots, owners), out_s...  12.1 us
    pallas_call x1, Pallas kernels, local(): pl.pallas_call(functools.partial(inner_kernel, rows, slots, owners), out_...  7.76 us
    ppermute x10, waiting for transfers between devices, xor_permute(): return lax.ppermute(x, axis, [(i, i ^ mask) for i in range(count)])  6.39 us
    ppermute x1, starting transfers between devices, local(): pair_halo = lax.ppermute(jnp.where(even, tail, head), 'space', pairs)  4.72 us
    pallas_call x1, Pallas kernels, local(): pl.pallas_call(functools.partial(far_kernel, len(far)), out_shape=(jax.Sh...  3.51 us
    pallas_call x1, Pallas kernels, local(): pl.pallas_call(functools.partial(near_kernel, len(held)), out_shape=(jax....  2.21 us
  transfers between devices with their start and end apart: 12, of which 3 were waited for; matrix products, arithmetic and copies ran while one was open for 0% of the time, Pallas kernels for 15%

profile of v4, /device:TPU:1, one launch (start us, length us, event | category | flops | bytes accessed | tf_op | source)
XLA Modules:
  0.0 66.7 jit_solution(15493414831752363441)
XLA Ops:
  0.6 1.1 %broadcast_select_fusion = (bf16[2,3,64,384]{3,2,1,0:T(8,128)(2,1)S(1)}, bf16[2,3,64,384]{3,2,1,0:T(8,128)(2,1)S(1)}) fusion(pred[]{:T(512)S(6)} %eq.3, bf16[2,16,64,384]{3,2,1,0:T(8,128)(2,1)} %x_ref.3), kind=kLoop, calls=%fused_computation | loop fusion | flops 294912 | bytes 1179649 | tf_op jit(solution)/shard_map/jit(_where)/select_n | solution.py:477
  1.8 0.7 %collective-permute-start.1 = (bf16[2,3,64,384]{3,2,1,0:T(8,128)(2,1)S(1)}, bf16[2,3,64,384]{3,2,1,0:T(8,128)(2,1)S(1)}, u32[]{:S(2)}, u32[]{:S(2)}) collective-permute-start(bf16[2,3,64,384]{3,2,1,0:T(8,128)(2,1)S(1)} %get-tuple-element.37), channel_id=1, source_target_pairs={{8,16},{16,8},{9,17},{17,9},{10,18},{18,10},{11,19},{19,11},{12,20... | collective-permute-start | bytes 884744 | tf_op jit(solution)/shard_map/ppermute | solution.py:477
  2.5 0.0 copy-start.3
  2.5 0.0 copy-start.4
  2.6 4.7 %collective-permute-start = (bf16[2,3,64,384]{3,2,1,0:T(8,128)(2,1)S(1)}, bf16[2,3,64,384]{3,2,1,0:T(8,128)(2,1)S(1)}, u32[]{:S(2)}, u32[]{:S(2)}) collective-permute-start(bf16[2,3,64,384]{3,2,1,0:T(8,128)(2,1)S(1)} %get-tuple-element.38), channel_id=1, source_target_pairs={{0,8},{8,0},{16,24},{24,16},{1,9},{9,1},{17,25},{25,17},{2,10},{10... | collective-permute-start | bytes 884744 | tf_op jit(solution)/shard_map/ppermute | solution.py:476
  7.4 7.8 %inner_rows.1 = (bf16[2,16,64,384]{3,2,1,0:T(8,128)(2,1)}, f32[64,384]{1,0:T(8,128)S(1)}, f32[64,128]{1,0:T(8,128)S(1)}, bf16[512,384]{1,0:T(8,128)(2,1)S(1)}, f...) custom-call(bf16[2,16,64,384]{3,2,1,0:T(8,128)(2,1)S(1)} %copy-done, s32[2,16,64]{2,1,0:T(8,128)S(1)} %copy-done.9, ...), custom_call_target="tpu_custom_call" | custom-call | flops 2454454272 | bytes 6291456 | tf_op jit(solution)/shard_map/inner_rows/pallas_call | solution.py:515
  15.2 12.1 %edge_rows.1 = (bf16[2,16,64,384]{3,2,1,0:T(8,128)(2,1)}, f32[32,1,1280]{2,1,0:T(1,128)S(1)}) custom-call(bf16[2,16,64,384]{3,2,1,0:T(8,128)(2,1)S(1)} %copy-done, bf16[2,3,64,384]{3,2,1,0:T(8,128)(2,1)S(1)} %collective-permute-done.pair_ref, bf16[2,3,64,384]{3,2,1,0:T(8,128)(2,1)S(1)} %collective-permute-done.1.next_ref, ...), custom_call_target="tpu_custom_call", output_to_operand_aliasing={{0}: (10, {})} | custom-call | flops 2454454272 | bytes 6291456 | tf_op jit(solution)/shard_map/edge_rows/pallas_call | solution.py:532
  27.3 13.6 %all_to_all.5.recv_ref = f32[32,1,1280]{2,1,0:T(1,128)S(1)} all-to-all(f32[32,1,1280]{2,1,0:T(1,128)S(1)} %get-tuple-element.29), channel_id=1, replica_groups=mesh['space'=4,'scene'=8] {'space','scene'}, dimensions={0} | all-to-all | bytes 327680 | tf_op jit(solution)/shard_map/all_to_all | solution.py:554
  40.9 0.9 %own_tokens.1 = (f32[64,384]{1,0:T(8,128)S(1)}, bf16[64,384]{1,0:T(8,128)(2,1)S(1)}) custom-call(f32[32,1,1280]{2,1,0:T(1,128)S(1)} %all_to_all.5.recv_ref, bf16[64,384]{1,0:T(8,128)(2,1)S(1)} %copy-done.1, f32[384]{0:T(512)S(1)} %copy-done.2), custom_call_target="tpu_custom_call" | custom-call | tf_op jit(solution)/shard_map/own_tokens/pallas_call | solution.py:555
  41.8 0.5 collective-permute-start.4
  42.3 0.2 collective-permute-start.3
  42.5 2.9 %collective-permute-start.2 = (bf16[64,384]{1,0:T(8,128)(2,1)S(1)}, bf16[64,384]{1,0:T(8,128)(2,1)S(1)}, u32[]{:S(2)}, u32[]{:S(2)}) collective-permute-start(bf16[64,384]{1,0:T(8,128)(2,1)S(1)} %get-tuple-element.31.own_ref), channel_id=1, source_target_pairs={{0,16},{8,24},{16,0},{24,8},{1,17},{9,25},{17,1},{25,9},{2,18},{10... | collective-permute-start | bytes 147464 | tf_op jit(solution)/shard_map/ppermute | solution.py:441
  45.5 2.9 %collective-permute-done.2 = bf16[64,384]{1,0:T(8,128)(2,1)S(1)} collective-permute-done((bf16[64,384]{1,0:T(8,128)(2,1)S(1)}, bf16[64,384]{1,0:T(8,128)(2,1)S(1)}, u32[]{:S(2)}, u32[]{:S(2)}) %collective-permute-start.2) | collective-permute-done | bytes 49184 | tf_op jit(solution)/shard_map/ppermute | solution.py:441
  48.4 0.1 collective-permute-start.7
  48.5 0.1 collective-permute-start.6
  48.6 2.6 %collective-permute-start.5 = (bf16[256,384]{1,0:T(8,128)(2,1)S(1)}, bf16[256,384]{1,0:T(8,128)(2,1)S(1)}, u32[]{:S(2)}, u32[]{:S(2)}) collective-permute-start(bf16[256,384]{1,0:T(8,128)(2,1)S(1)} %constant_dynamic-update-slice_fusion.refs_0_), channel_id=1, source_target_pairs={{0,4},{1,5},{2,6},{3,7},{4,0},{5,1},{6,2},{7,3},{8,12},{9,13},{10,... | collective-permute-start | bytes 589832 | tf_op jit(solution)/shard_map/ppermute | solution.py:441
  51.1 2.0 %collective-permute-start.8 = (bf16[256,384]{1,0:T(8,128)(2,1)S(1)}, bf16[256,384]{1,0:T(8,128)(2,1)S(1)}, u32[]{:S(2)}, u32[]{:S(2)}) collective-permute-start(bf16[256,384]{1,0:T(8,128)(2,1)S(1)} %constant_dynamic-update-slice_fusion.refs_0_), channel_id=1, source_target_pairs={{0,1},{1,0},{2,3},{3,2},{4,5},{5,4},{6,7},{7,6},{8,9},{9,8},{10,11... | collective-permute-start | bytes 589832 | tf_op jit(solution)/shard_map/ppermute | solution.py:441
  53.1 1.6 %collective-permute-done.7.refs_3_ = bf16[256,384]{1,0:T(8,128)(2,1)S(1)} collective-permute-done((bf16[256,384]{1,0:T(8,128)(2,1)S(1)}, bf16[256,384]{1,0:T(8,128)(2,1)S(1)}, u32[]{:S(2)}, u32[]{:S(2)}) %collective-permute-start.7) | collective-permute-done | bytes 196640 | tf_op jit(solution)/shard_map/ppermute | solution.py:441
  54.7 3.7 %collective-permute-start.11 = (bf16[256,384]{1,0:T(8,128)(2,1)S(1)}, bf16[256,384]{1,0:T(8,128)(2,1)S(1)}, u32[]{:S(2)}, u32[]{:S(2)}) collective-permute-start(bf16[256,384]{1,0:T(8,128)(2,1)S(1)} %collective-permute-done.7.refs_3_), channel_id=1, source_target_pairs={{0,1},{1,0},{2,3},{3,2},{4,5},{5,4},{6,7},{7,6},{8,9},{9,8},{10,11... | collective-permute-start | bytes 589832 | tf_op jit(solution)/shard_map/ppermute | solution.py:441
  58.4 0.1 collective-permute-start.10
  58.5 1.9 %collective-permute-done.5.refs_1_ = bf16[256,384]{1,0:T(8,128)(2,1)S(1)} collective-permute-done((bf16[256,384]{1,0:T(8,128)(2,1)S(1)}, bf16[256,384]{1,0:T(8,128)(2,1)S(1)}, u32[]{:S(2)}, u32[]{:S(2)}) %collective-permute-start.5) | collective-permute-done | bytes 196640 | tf_op jit(solution)/shard_map/ppermute | solution.py:441
  60.4 0.5 collective-permute-start.9
  60.9 2.2 %near_keys.1 = (f32[384,128]{1,0:T(8,128)S(1)}, f32[384,384]{1,0:T(8,128)S(1)}, bf16[384,384]{1,0:T(8,128)(2,1)S(1)}) custom-call(bf16[64,384]{1,0:T(8,128)(2,1)S(1)} %get-tuple-element.31.own_ref, bf16[384,1152]{1,0:T(8,128)(2,1)S(1)} %copy-done.5, bf16[256,384]{1,0:T(8,128)(2,1)S(1)} %constant_dynamic-update-slice_fusion.refs_0_, ...), custom_call_target="tpu_custom_call" | custom-call | flops 1207959552 | bytes 2097152 | tf_op jit(solution)/shard_map/near_keys/pallas_call | solution.py:575
  63.2 3.5 %far_keys.1 = (bf16[64,384]{1,0:T(8,128)(2,1)}, f32[64]{0:T(128)}) custom-call(f32[64,384]{1,0:T(8,128)S(1)} %get-tuple-element.30.tokens_ref, bf16[384,384]{1,0:T(8,128)(2,1)S(1)} %get-tuple-element.32.query_ref, bf16[384,1152]{1,0:T(8,128)(2,1)S(1)} %copy-done.5, bf16[384,384]{1,0:T(8,128)(2,1)S(1)} %copy-done.6, bf16[20,384]{1,0:T(8,128)(2,1)S(1)} %bitcast.1, ...), custom_call_target="tpu_custom_call" | custom-call | flops 1207959552 | bytes 2097152 | tf_op jit(solution)/shard_map/far_keys/pallas_call | solution.py:588
  (44 shorter events, 0.2 us)
Async XLA Ops:
  1.8 13.4 %collective-permute-start.1 = (bf16[2,3,64,384]{3,2,1,0:T(8,128)(2,1)S(1)}, bf16[2,3,64,384]{3,2,1,0:T(8,128)(2,1)S(1)}, u32[]{:S(2)}, u32[]{:S(2)}) collective-permute-start(bf16[2,3,64,384]{3,2,1,0:T(8,128)(2,1)S(1)} %get-tuple-element.37), channel_id=1, source_target_pairs={{8,16},{16,8},{9,17},{17,9},{10,18},{18,10},{11,19},{19,11},{12,20... | collective-permute-start | bytes 884744 | tf_op jit(solution)/shard_map/ppermute | solution.py:477
  2.4 4.9 %copy-start = (bf16[2,16,64,384]{3,2,1,0:T(8,128)(2,1)S(1)}, bf16[2,16,64,384]{3,2,1,0:T(8,128)(2,1)}, u32[]{:S(2)}) copy-start(bf16[2,16,64,384]{3,2,1,0:T(8,128)(2,1)} %x_ref.3) | copy-start | bytes 4718596
  2.5 4.9 %copy-start.3 = (bf16[384,1536]{1,0:T(8,128)(2,1)S(1)}, bf16[384,1536]{1,0:T(8,128)(2,1)}, u32[]{:S(2)}) copy-start(bf16[384,1536]{1,0:T(8,128)(2,1)} %we_ref.3) | copy-start | bytes 3538948
  2.5 4.8 %copy-start.4 = (bf16[1536,384]{1,0:T(8,128)(2,1)S(1)}, bf16[1536,384]{1,0:T(8,128)(2,1)}, u32[]{:S(2)}) copy-start(bf16[1536,384]{1,0:T(8,128)(2,1)} %wr_ref.3) | copy-start | bytes 3538948
  2.5 4.8 %copy-start.7 = (bf16[7,7,384]{2,1,0:T(8,128)(2,1)S(1)}, bf16[7,7,384]{2,1,0:T(8,128)(2,1)}, u32[]{:S(2)}) copy-start(bf16[7,7,384]{2,1,0:T(8,128)(2,1)} %dwk_ref.3) | copy-start | bytes 112900
  2.5 4.8 %copy-start.9 = (s32[2,16,64]{2,1,0:T(8,128)S(1)}, s32[2,16,64]{2,1,0:T(8,128)}, u32[]{:S(2)}) copy-start(s32[2,16,64]{2,1,0:T(8,128)} %slot_ref.3) | copy-start | bytes 24580
  2.5 4.8 %copy-start.10 = (s32[2048]{0:T(1024)S(1)}, s32[2048]{0:T(1024)}, u32[]{:S(2)}) copy-start(s32[2048]{0:T(1024)} %pos_ref.1) | copy-start | bytes 24580
  2.6 12.6 %collective-permute-start = (bf16[2,3,64,384]{3,2,1,0:T(8,128)(2,1)S(1)}, bf16[2,3,64,384]{3,2,1,0:T(8,128)(2,1)S(1)}, u32[]{:S(2)}, u32[]{:S(2)}) collective-permute-start(bf16[2,3,64,384]{3,2,1,0:T(8,128)(2,1)S(1)} %get-tuple-element.38), channel_id=1, source_target_pairs={{0,8},{8,0},{16,24},{24,16},{1,9},{9,1},{17,25},{25,17},{2,10},{10... | collective-permute-start | bytes 884744 | tf_op jit(solution)/shard_map/ppermute | solution.py:476
  15.2 25.7 %copy-start.1 = (bf16[64,384]{1,0:T(8,128)(2,1)S(1)}, bf16[64,384]{1,0:T(8,128)(2,1)}, u32[]{:S(2)}) copy-start(bf16[64,384]{1,0:T(8,128)(2,1)} %embed_ref.1) | copy-start | bytes 147460
  15.2 25.7 %copy-start.2 = (f32[384]{0:T(512)S(1)}, f32[384]{0:T(512)}, u32[]{:S(2)}) copy-start(f32[384]{0:T(512)} %gain_ref.5) | copy-start | bytes 4612
  15.2 45.7 %copy-start.5 = (bf16[384,1152]{1,0:T(8,128)(2,1)S(1)}, bf16[384,1152]{1,0:T(8,128)(2,1)}, u32[]{:S(2)}) copy-start(bf16[384,1152]{1,0:T(8,128)(2,1)} %wqkv_ref.3) | copy-start | bytes 2654212
  41.8 6.5 %collective-permute-start.4 = (bf16[64,384]{1,0:T(8,128)(2,1)S(1)}, bf16[64,384]{1,0:T(8,128)(2,1)S(1)}, u32[]{:S(2)}, u32[]{:S(2)}) collective-permute-start(bf16[64,384]{1,0:T(8,128)(2,1)S(1)} %get-tuple-element.31.own_ref), channel_id=1, source_target_pairs={{0,24},{8,16},{16,8},{24,0},{1,25},{9,17},{17,9},{25,1},{2,26},{10... | collective-permute-start | bytes 147464 | tf_op jit(solution)/shard_map/ppermute | solution.py:441
  42.3 6.0 %collective-permute-start.3 = (bf16[64,384]{1,0:T(8,128)(2,1)S(1)}, bf16[64,384]{1,0:T(8,128)(2,1)S(1)}, u32[]{:S(2)}, u32[]{:S(2)}) collective-permute-start(bf16[64,384]{1,0:T(8,128)(2,1)S(1)} %get-tuple-element.31.own_ref), channel_id=1, source_target_pairs={{0,8},{8,0},{16,24},{24,16},{1,9},{9,1},{17,25},{25,17},{2,10},{10... | collective-permute-start | bytes 147464 | tf_op jit(solution)/shard_map/ppermute | solution.py:441
  42.5 5.8 %collective-permute-start.2 = (bf16[64,384]{1,0:T(8,128)(2,1)S(1)}, bf16[64,384]{1,0:T(8,128)(2,1)S(1)}, u32[]{:S(2)}, u32[]{:S(2)}) collective-permute-start(bf16[64,384]{1,0:T(8,128)(2,1)S(1)} %get-tuple-element.31.own_ref), channel_id=1, source_target_pairs={{0,16},{8,24},{16,0},{24,8},{1,17},{9,25},{17,1},{25,9},{2,18},{10... | collective-permute-start | bytes 147464 | tf_op jit(solution)/shard_map/ppermute | solution.py:441
  48.4 14.8 %copy-start.6 = (bf16[384,384]{1,0:T(8,128)(2,1)S(1)}, bf16[384,384]{1,0:T(8,128)(2,1)}, u32[]{:S(2)}) copy-start(bf16[384,384]{1,0:T(8,128)(2,1)} %wout_ref.1) | copy-start | bytes 884740
  48.4 14.8 %copy-start.8 = (bf16[384,20]{0,1:T(8,128)(2,1)S(1)}, bf16[384,20]{0,1:T(8,128)(2,1)}, u32[]{:S(2)}) copy-start(bf16[384,20]{0,1:T(8,128)(2,1)} %param.30) | copy-start | bytes 46084
  48.4 14.8 %copy-start.15 = (s32[64]{0:T(128)S(1)}, s32[64]{0:T(128)}, u32[]{:S(2)}) copy-start(s32[64]{0:T(128)} %labels_ref.1) | copy-start | bytes 772
  48.4 6.3 %collective-permute-start.7 = (bf16[256,384]{1,0:T(8,128)(2,1)S(1)}, bf16[256,384]{1,0:T(8,128)(2,1)S(1)}, u32[]{:S(2)}, u32[]{:S(2)}) collective-permute-start(bf16[256,384]{1,0:T(8,128)(2,1)S(1)} %constant_dynamic-update-slice_fusion.refs_0_), channel_id=1, source_target_pairs={{0,6},{1,7},{2,4},{3,5},{4,2},{5,3},{6,0},{7,1},{8,14},{9,15},{10,... | collective-permute-start | bytes 589832 | tf_op jit(solution)/shard_map/ppermute | solution.py:441
  48.5 9.9 %collective-permute-start.6 = (bf16[256,384]{1,0:T(8,128)(2,1)S(1)}, bf16[256,384]{1,0:T(8,128)(2,1)S(1)}, u32[]{:S(2)}, u32[]{:S(2)}) collective-permute-start(bf16[256,384]{1,0:T(8,128)(2,1)S(1)} %constant_dynamic-update-slice_fusion.refs_0_), channel_id=1, source_target_pairs={{0,2},{1,3},{2,0},{3,1},{4,6},{5,7},{6,4},{7,5},{8,10},{9,11},{10,... | collective-permute-start | bytes 589832 | tf_op jit(solution)/shard_map/ppermute | solution.py:441
  48.6 11.8 %collective-permute-start.5 = (bf16[256,384]{1,0:T(8,128)(2,1)S(1)}, bf16[256,384]{1,0:T(8,128)(2,1)S(1)}, u32[]{:S(2)}, u32[]{:S(2)}) collective-permute-start(bf16[256,384]{1,0:T(8,128)(2,1)S(1)} %constant_dynamic-update-slice_fusion.refs_0_), channel_id=1, source_target_pairs={{0,4},{1,5},{2,6},{3,7},{4,0},{5,1},{6,2},{7,3},{8,12},{9,13},{10,... | collective-permute-start | bytes 589832 | tf_op jit(solution)/shard_map/ppermute | solution.py:441
  51.1 12.0 %collective-permute-start.8 = (bf16[256,384]{1,0:T(8,128)(2,1)S(1)}, bf16[256,384]{1,0:T(8,128)(2,1)S(1)}, u32[]{:S(2)}, u32[]{:S(2)}) collective-permute-start(bf16[256,384]{1,0:T(8,128)(2,1)S(1)} %constant_dynamic-update-slice_fusion.refs_0_), channel_id=1, source_target_pairs={{0,1},{1,0},{2,3},{3,2},{4,5},{5,4},{6,7},{7,6},{8,9},{9,8},{10,11... | collective-permute-start | bytes 589832 | tf_op jit(solution)/shard_map/ppermute | solution.py:441
  54.7 8.4 %collective-permute-start.11 = (bf16[256,384]{1,0:T(8,128)(2,1)S(1)}, bf16[256,384]{1,0:T(8,128)(2,1)S(1)}, u32[]{:S(2)}, u32[]{:S(2)}) collective-permute-start(bf16[256,384]{1,0:T(8,128)(2,1)S(1)} %collective-permute-done.7.refs_3_), channel_id=1, source_target_pairs={{0,1},{1,0},{2,3},{3,2},{4,5},{5,4},{6,7},{7,6},{8,9},{9,8},{10,11... | collective-permute-start | bytes 589832 | tf_op jit(solution)/shard_map/ppermute | solution.py:441
  58.4 4.8 %collective-permute-start.10 = (bf16[256,384]{1,0:T(8,128)(2,1)S(1)}, bf16[256,384]{1,0:T(8,128)(2,1)S(1)}, u32[]{:S(2)}, u32[]{:S(2)}) collective-permute-start(bf16[256,384]{1,0:T(8,128)(2,1)S(1)} %collective-permute-done.6.refs_2_), channel_id=1, source_target_pairs={{0,1},{1,0},{2,3},{3,2},{4,5},{5,4},{6,7},{7,6},{8,9},{9,8},{10,11... | collective-permute-start | bytes 589832 | tf_op jit(solution)/shard_map/ppermute | solution.py:441
  60.4 2.7 %collective-permute-start.9 = (bf16[256,384]{1,0:T(8,128)(2,1)S(1)}, bf16[256,384]{1,0:T(8,128)(2,1)S(1)}, u32[]{:S(2)}, u32[]{:S(2)}) collective-permute-start(bf16[256,384]{1,0:T(8,128)(2,1)S(1)} %collective-permute-done.5.refs_1_), channel_id=1, source_target_pairs={{0,1},{1,0},{2,3},{3,2},{4,5},{5,4},{6,7},{7,6},{8,9},{9,8},{10,11... | collective-permute-start | bytes 589832 | tf_op jit(solution)/shard_map/ppermute | solution.py:441
  (4 other events, 19.3 us)

commit v5 on v4

--- a/solution.py
+++ b/solution.py
@@ -121,11 +121,12 @@
             part = cb * blocks + n
             todo = list(cols) if convolve else []
             for r in range(0, many, PIECE):
-                if pointwise:
-                    expand(min(part + 1, steps - 1), (n + 1) % blocks, r)
-                    reduce(part, n, r)
                 if todo:
                     conv_tile(n, cb, todo.pop(0), slab, spat, wb, bias_ref, width)
+                if pointwise and part + 1 < steps:
+                    expand(part + 1, (n + 1) % blocks, r)
+                if pointwise:
+                    reduce(part, n, r)
             for col in todo:
                 conv_tile(n, cb, col, slab, spat, wb, bias_ref, width)
         return carry

time: 66.9 us -> 66.5 us (level)
  no operation moved by 1% of the time
where the time goes in v5:
time: 66.5 us; the launch traced here: 66.3 us
  Pallas kernels  26.1 us (39%)
  starting transfers between devices  18 us (27%)
  blocking collectives  13.6 us (20%)
  waiting for transfers between devices  6.39 us (10%)
  other arithmetic  1.12 us (2%)
  between operations  1.01 us (2%)
    all_to_all x1, blocking collectives, local(): lax.all_to_all(sent, AXES, split_axis=0, concat_axis=0, tiled=True)  13.6 us
    ppermute x10, starting transfers between devices, xor_permute(): return lax.ppermute(x, axis, [(i, i ^ mask) for i in range(count)])  12.6 us
    pallas_call x1, Pallas kernels, local(): pl.pallas_call(functools.partial(edge_kernel, rows, slots, owners), out_s...  11.7 us
    pallas_call x1, Pallas kernels, local(): pl.pallas_call(functools.partial(inner_kernel, rows, slots, owners), out_...  7.65 us
    ppermute x10, waiting for transfers between devices, xor_permute(): return lax.ppermute(x, axis, [(i, i ^ mask) for i in range(count)])  6.39 us
    ppermute x1, starting transfers between devices, local(): pair_halo = lax.ppermute(jnp.where(even, tail, head), 'space', pairs)  4.72 us
    pallas_call x1, Pallas kernels, local(): pl.pallas_call(functools.partial(far_kernel, len(far)), out_shape=(jax.Sh...  3.51 us
    pallas_call x1, Pallas kernels, local(): pl.pallas_call(functools.partial(near_kernel, len(held)), out_shape=(jax....  2.21 us
  transfers between devices with their start and end apart: 12, of which 3 were waited for; matrix products, arithmetic and copies ran while one was open for 0% of the time, Pallas kernels for 15%

profile of v5, /device:TPU:1, one launch (start us, length us, event | category | flops | bytes accessed | tf_op | source)
XLA Modules:
  0.0 66.3 jit_solution(12209674815577604779)
XLA Ops:
  0.6 1.1 %broadcast_select_fusion = (bf16[2,3,64,384]{3,2,1,0:T(8,128)(2,1)S(1)}, bf16[2,3,64,384]{3,2,1,0:T(8,128)(2,1)S(1)}) fusion(pred[]{:T(512)S(6)} %eq.3, bf16[2,16,64,384]{3,2,1,0:T(8,128)(2,1)} %x_ref.3), kind=kLoop, calls=%fused_computation | loop fusion | flops 294912 | bytes 1179649 | tf_op jit(solution)/shard_map/jit(_where)/select_n | solution.py:478
  1.8 0.7 %collective-permute-start.1 = (bf16[2,3,64,384]{3,2,1,0:T(8,128)(2,1)S(1)}, bf16[2,3,64,384]{3,2,1,0:T(8,128)(2,1)S(1)}, u32[]{:S(2)}, u32[]{:S(2)}) collective-permute-start(bf16[2,3,64,384]{3,2,1,0:T(8,128)(2,1)S(1)} %get-tuple-element.37), channel_id=1, source_target_pairs={{8,16},{16,8},{9,17},{17,9},{10,18},{18,10},{11,19},{19,11},{12,20... | collective-permute-start | bytes 884744 | tf_op jit(solution)/shard_map/ppermute | solution.py:478
  2.5 0.0 copy-start.3
  2.5 0.0 copy-start.4
  2.6 4.7 %collective-permute-start = (bf16[2,3,64,384]{3,2,1,0:T(8,128)(2,1)S(1)}, bf16[2,3,64,384]{3,2,1,0:T(8,128)(2,1)S(1)}, u32[]{:S(2)}, u32[]{:S(2)}) collective-permute-start(bf16[2,3,64,384]{3,2,1,0:T(8,128)(2,1)S(1)} %get-tuple-element.38), channel_id=1, source_target_pairs={{0,8},{8,0},{16,24},{24,16},{1,9},{9,1},{17,25},{25,17},{2,10},{10... | collective-permute-start | bytes 884744 | tf_op jit(solution)/shard_map/ppermute | solution.py:477
  7.4 7.7 %inner_rows.1 = (bf16[2,16,64,384]{3,2,1,0:T(8,128)(2,1)}, f32[64,384]{1,0:T(8,128)S(1)}, f32[64,128]{1,0:T(8,128)S(1)}, bf16[512,384]{1,0:T(8,128)(2,1)S(1)}, f...) custom-call(bf16[2,16,64,384]{3,2,1,0:T(8,128)(2,1)S(1)} %copy-done, s32[2,16,64]{2,1,0:T(8,128)S(1)} %copy-done.9, ...), custom_call_target="tpu_custom_call" | custom-call | flops 2454454272 | bytes 6291456 | tf_op jit(solution)/shard_map/inner_rows/pallas_call | solution.py:516
  15.1 11.7 %edge_rows.1 = (bf16[2,16,64,384]{3,2,1,0:T(8,128)(2,1)}, f32[32,1,1280]{2,1,0:T(1,128)S(1)}) custom-call(bf16[2,16,64,384]{3,2,1,0:T(8,128)(2,1)S(1)} %copy-done, bf16[2,3,64,384]{3,2,1,0:T(8,128)(2,1)S(1)} %collective-permute-done.pair_ref, bf16[2,3,64,384]{3,2,1,0:T(8,128)(2,1)S(1)} %collective-permute-done.1.next_ref, ...), custom_call_target="tpu_custom_call", output_to_operand_aliasing={{0}: (10, {})} | custom-call | flops 2454454272 | bytes 6291456 | tf_op jit(solution)/shard_map/edge_rows/pallas_call | solution.py:533
  26.9 13.6 %all_to_all.5.recv_ref = f32[32,1,1280]{2,1,0:T(1,128)S(1)} all-to-all(f32[32,1,1280]{2,1,0:T(1,128)S(1)} %get-tuple-element.29), channel_id=1, replica_groups=mesh['space'=4,'scene'=8] {'space','scene'}, dimensions={0} | all-to-all | bytes 327680 | tf_op jit(solution)/shard_map/all_to_all | solution.py:555
  40.5 0.9 %own_tokens.1 = (f32[64,384]{1,0:T(8,128)S(1)}, bf16[64,384]{1,0:T(8,128)(2,1)S(1)}) custom-call(f32[32,1,1280]{2,1,0:T(1,128)S(1)} %all_to_all.5.recv_ref, bf16[64,384]{1,0:T(8,128)(2,1)S(1)} %copy-done.1, f32[384]{0:T(512)S(1)} %copy-done.2), custom_call_target="tpu_custom_call" | custom-call | tf_op jit(solution)/shard_map/own_tokens/pallas_call | solution.py:556
  41.4 0.5 collective-permute-start.4
  41.9 0.2 collective-permute-start.3
  42.1 2.9 %collective-permute-start.2 = (bf16[64,384]{1,0:T(8,128)(2,1)S(1)}, bf16[64,384]{1,0:T(8,128)(2,1)S(1)}, u32[]{:S(2)}, u32[]{:S(2)}) collective-permute-start(bf16[64,384]{1,0:T(8,128)(2,1)S(1)} %get-tuple-element.31.own_ref), channel_id=1, source_target_pairs={{0,16},{8,24},{16,0},{24,8},{1,17},{9,25},{17,1},{25,9},{2,18},{10... | collective-permute-start | bytes 147464 | tf_op jit(solution)/shard_map/ppermute | solution.py:442
  45.0 2.9 %collective-permute-done.2 = bf16[64,384]{1,0:T(8,128)(2,1)S(1)} collective-permute-done((bf16[64,384]{1,0:T(8,128)(2,1)S(1)}, bf16[64,384]{1,0:T(8,128)(2,1)S(1)}, u32[]{:S(2)}, u32[]{:S(2)}) %collective-permute-start.2) | collective-permute-done | bytes 49184 | tf_op jit(solution)/shard_map/ppermute | solution.py:442
  48.0 0.1 collective-permute-start.7
  48.1 0.1 collective-permute-start.6
  48.2 2.6 %collective-permute-start.5 = (bf16[256,384]{1,0:T(8,128)(2,1)S(1)}, bf16[256,384]{1,0:T(8,128)(2,1)S(1)}, u32[]{:S(2)}, u32[]{:S(2)}) collective-permute-start(bf16[256,384]{1,0:T(8,128)(2,1)S(1)} %constant_dynamic-update-slice_fusion.refs_0_), channel_id=1, source_target_pairs={{0,4},{1,5},{2,6},{3,7},{4,0},{5,1},{6,2},{7,3},{8,12},{9,13},{10,... | collective-permute-start | bytes 589832 | tf_op jit(solution)/shard_map/ppermute | solution.py:442
  50.7 2.0 %collective-permute-start.8 = (bf16[256,384]{1,0:T(8,128)(2,1)S(1)}, bf16[256,384]{1,0:T(8,128)(2,1)S(1)}, u32[]{:S(2)}, u32[]{:S(2)}) collective-permute-start(bf16[256,384]{1,0:T(8,128)(2,1)S(1)} %constant_dynamic-update-slice_fusion.refs_0_), channel_id=1, source_target_pairs={{0,1},{1,0},{2,3},{3,2},{4,5},{5,4},{6,7},{7,6},{8,9},{9,8},{10,11... | collective-permute-start | bytes 589832 | tf_op jit(solution)/shard_map/ppermute | solution.py:442
  52.7 1.6 %collective-permute-done.7.refs_3_ = bf16[256,384]{1,0:T(8,128)(2,1)S(1)} collective-permute-done((bf16[256,384]{1,0:T(8,128)(2,1)S(1)}, bf16[256,384]{1,0:T(8,128)(2,1)S(1)}, u32[]{:S(2)}, u32[]{:S(2)}) %collective-permute-start.7) | collective-permute-done | bytes 196640 | tf_op jit(solution)/shard_map/ppermute | solution.py:442
  54.3 3.7 %collective-permute-start.11 = (bf16[256,384]{1,0:T(8,128)(2,1)S(1)}, bf16[256,384]{1,0:T(8,128)(2,1)S(1)}, u32[]{:S(2)}, u32[]{:S(2)}) collective-permute-start(bf16[256,384]{1,0:T(8,128)(2,1)S(1)} %collective-permute-done.7.refs_3_), channel_id=1, source_target_pairs={{0,1},{1,0},{2,3},{3,2},{4,5},{5,4},{6,7},{7,6},{8,9},{9,8},{10,11... | collective-permute-start | bytes 589832 | tf_op jit(solution)/shard_map/ppermute | solution.py:442
  58.0 0.1 collective-permute-start.10
  58.1 1.9 %collective-permute-done.5.refs_1_ = bf16[256,384]{1,0:T(8,128)(2,1)S(1)} collective-permute-done((bf16[256,384]{1,0:T(8,128)(2,1)S(1)}, bf16[256,384]{1,0:T(8,128)(2,1)S(1)}, u32[]{:S(2)}, u32[]{:S(2)}) %collective-permute-start.5) | collective-permute-done | bytes 196640 | tf_op jit(solution)/shard_map/ppermute | solution.py:442
  60.0 0.5 collective-permute-start.9
  60.5 2.2 %near_keys.1 = (f32[384,128]{1,0:T(8,128)S(1)}, f32[384,384]{1,0:T(8,128)S(1)}, bf16[384,384]{1,0:T(8,128)(2,1)S(1)}) custom-call(bf16[64,384]{1,0:T(8,128)(2,1)S(1)} %get-tuple-element.31.own_ref, bf16[384,1152]{1,0:T(8,128)(2,1)S(1)} %copy-done.5, bf16[256,384]{1,0:T(8,128)(2,1)S(1)} %constant_dynamic-update-slice_fusion.refs_0_, ...), custom_call_target="tpu_custom_call" | custom-call | flops 1207959552 | bytes 2097152 | tf_op jit(solution)/shard_map/near_keys/pallas_call | solution.py:576
  62.8 3.5 %far_keys.1 = (bf16[64,384]{1,0:T(8,128)(2,1)}, f32[64]{0:T(128)}) custom-call(f32[64,384]{1,0:T(8,128)S(1)} %get-tuple-element.30.tokens_ref, bf16[384,384]{1,0:T(8,128)(2,1)S(1)} %get-tuple-element.32.query_ref, bf16[384,1152]{1,0:T(8,128)(2,1)S(1)} %copy-done.5, bf16[384,384]{1,0:T(8,128)(2,1)S(1)} %copy-done.6, bf16[20,384]{1,0:T(8,128)(2,1)S(1)} %bitcast.1, ...), custom_call_target="tpu_custom_call" | custom-call | flops 1207959552 | bytes 2097152 | tf_op jit(solution)/shard_map/far_keys/pallas_call | solution.py:589
  (44 shorter events, 0.2 us)
Async XLA Ops:
  1.8 13.3 %collective-permute-start.1 = (bf16[2,3,64,384]{3,2,1,0:T(8,128)(2,1)S(1)}, bf16[2,3,64,384]{3,2,1,0:T(8,128)(2,1)S(1)}, u32[]{:S(2)}, u32[]{:S(2)}) collective-permute-start(bf16[2,3,64,384]{3,2,1,0:T(8,128)(2,1)S(1)} %get-tuple-element.37), channel_id=1, source_target_pairs={{8,16},{16,8},{9,17},{17,9},{10,18},{18,10},{11,19},{19,11},{12,20... | collective-permute-start | bytes 884744 | tf_op jit(solution)/shard_map/ppermute | solution.py:478
  2.4 4.9 %copy-start = (bf16[2,16,64,384]{3,2,1,0:T(8,128)(2,1)S(1)}, bf16[2,16,64,384]{3,2,1,0:T(8,128)(2,1)}, u32[]{:S(2)}) copy-start(bf16[2,16,64,384]{3,2,1,0:T(8,128)(2,1)} %x_ref.3) | copy-start | bytes 4718596
  2.5 4.9 %copy-start.3 = (bf16[384,1536]{1,0:T(8,128)(2,1)S(1)}, bf16[384,1536]{1,0:T(8,128)(2,1)}, u32[]{:S(2)}) copy-start(bf16[384,1536]{1,0:T(8,128)(2,1)} %we_ref.3) | copy-start | bytes 3538948
  2.5 4.8 %copy-start.4 = (bf16[1536,384]{1,0:T(8,128)(2,1)S(1)}, bf16[1536,384]{1,0:T(8,128)(2,1)}, u32[]{:S(2)}) copy-start(bf16[1536,384]{1,0:T(8,128)(2,1)} %wr_ref.3) | copy-start | bytes 3538948
  2.5 4.8 %copy-start.7 = (bf16[7,7,384]{2,1,0:T(8,128)(2,1)S(1)}, bf16[7,7,384]{2,1,0:T(8,128)(2,1)}, u32[]{:S(2)}) copy-start(bf16[7,7,384]{2,1,0:T(8,128)(2,1)} %dwk_ref.3) | copy-start | bytes 112900
  2.5 4.8 %copy-start.9 = (s32[2,16,64]{2,1,0:T(8,128)S(1)}, s32[2,16,64]{2,1,0:T(8,128)}, u32[]{:S(2)}) copy-start(s32[2,16,64]{2,1,0:T(8,128)} %slot_ref.3) | copy-start | bytes 24580
  2.5 4.8 %copy-start.10 = (s32[2048]{0:T(1024)S(1)}, s32[2048]{0:T(1024)}, u32[]{:S(2)}) copy-start(s32[2048]{0:T(1024)} %pos_ref.1) | copy-start | bytes 24580
  2.6 12.5 %collective-permute-start = (bf16[2,3,64,384]{3,2,1,0:T(8,128)(2,1)S(1)}, bf16[2,3,64,384]{3,2,1,0:T(8,128)(2,1)S(1)}, u32[]{:S(2)}, u32[]{:S(2)}) collective-permute-start(bf16[2,3,64,384]{3,2,1,0:T(8,128)(2,1)S(1)} %get-tuple-element.38), channel_id=1, source_target_pairs={{0,8},{8,0},{16,24},{24,16},{1,9},{9,1},{17,25},{25,17},{2,10},{10... | collective-permute-start | bytes 884744 | tf_op jit(solution)/shard_map/ppermute | solution.py:477
  15.1 25.4 %copy-start.1 = (bf16[64,384]{1,0:T(8,128)(2,1)S(1)}, bf16[64,384]{1,0:T(8,128)(2,1)}, u32[]{:S(2)}) copy-start(bf16[64,384]{1,0:T(8,128)(2,1)} %embed_ref.1) | copy-start | bytes 147460
  15.1 25.4 %copy-start.2 = (f32[384]{0:T(512)S(1)}, f32[384]{0:T(512)}, u32[]{:S(2)}) copy-start(f32[384]{0:T(512)} %gain_ref.5) | copy-start | bytes 4612
  15.1 45.4 %copy-start.5 = (bf16[384,1152]{1,0:T(8,128)(2,1)S(1)}, bf16[384,1152]{1,0:T(8,128)(2,1)}, u32[]{:S(2)}) copy-start(bf16[384,1152]{1,0:T(8,128)(2,1)} %wqkv_ref.3) | copy-start | bytes 2654212
  41.4 6.5 %collective-permute-start.4 = (bf16[64,384]{1,0:T(8,128)(2,1)S(1)}, bf16[64,384]{1,0:T(8,128)(2,1)S(1)}, u32[]{:S(2)}, u32[]{:S(2)}) collective-permute-start(bf16[64,384]{1,0:T(8,128)(2,1)S(1)} %get-tuple-element.31.own_ref), channel_id=1, source_target_pairs={{0,24},{8,16},{16,8},{24,0},{1,25},{9,17},{17,9},{25,1},{2,26},{10... | collective-permute-start | bytes 147464 | tf_op jit(solution)/shard_map/ppermute | solution.py:442
  41.9 6.0 %collective-permute-start.3 = (bf16[64,384]{1,0:T(8,128)(2,1)S(1)}, bf16[64,384]{1,0:T(8,128)(2,1)S(1)}, u32[]{:S(2)}, u32[]{:S(2)}) collective-permute-start(bf16[64,384]{1,0:T(8,128)(2,1)S(1)} %get-tuple-element.31.own_ref), channel_id=1, source_target_pairs={{0,8},{8,0},{16,24},{24,16},{1,9},{9,1},{17,25},{25,17},{2,10},{10... | collective-permute-start | bytes 147464 | tf_op jit(solution)/shard_map/ppermute | solution.py:442
  42.1 5.8 %collective-permute-start.2 = (bf16[64,384]{1,0:T(8,128)(2,1)S(1)}, bf16[64,384]{1,0:T(8,128)(2,1)S(1)}, u32[]{:S(2)}, u32[]{:S(2)}) collective-permute-start(bf16[64,384]{1,0:T(8,128)(2,1)S(1)} %get-tuple-element.31.own_ref), channel_id=1, source_target_pairs={{0,16},{8,24},{16,0},{24,8},{1,17},{9,25},{17,1},{25,9},{2,18},{10... | collective-permute-start | bytes 147464 | tf_op jit(solution)/shard_map/ppermute | solution.py:442
  48.0 14.8 %copy-start.6 = (bf16[384,384]{1,0:T(8,128)(2,1)S(1)}, bf16[384,384]{1,0:T(8,128)(2,1)}, u32[]{:S(2)}) copy-start(bf16[384,384]{1,0:T(8,128)(2,1)} %wout_ref.1) | copy-start | bytes 884740
  48.0 14.8 %copy-start.8 = (bf16[384,20]{0,1:T(8,128)(2,1)S(1)}, bf16[384,20]{0,1:T(8,128)(2,1)}, u32[]{:S(2)}) copy-start(bf16[384,20]{0,1:T(8,128)(2,1)} %param.30) | copy-start | bytes 46084
  48.0 14.8 %copy-start.15 = (s32[64]{0:T(128)S(1)}, s32[64]{0:T(128)}, u32[]{:S(2)}) copy-start(s32[64]{0:T(128)} %labels_ref.1) | copy-start | bytes 772
  48.0 6.3 %collective-permute-start.7 = (bf16[256,384]{1,0:T(8,128)(2,1)S(1)}, bf16[256,384]{1,0:T(8,128)(2,1)S(1)}, u32[]{:S(2)}, u32[]{:S(2)}) collective-permute-start(bf16[256,384]{1,0:T(8,128)(2,1)S(1)} %constant_dynamic-update-slice_fusion.refs_0_), channel_id=1, source_target_pairs={{0,6},{1,7},{2,4},{3,5},{4,2},{5,3},{6,0},{7,1},{8,14},{9,15},{10,... | collective-permute-start | bytes 589832 | tf_op jit(solution)/shard_map/ppermute | solution.py:442
  48.1 9.9 %collective-permute-start.6 = (bf16[256,384]{1,0:T(8,128)(2,1)S(1)}, bf16[256,384]{1,0:T(8,128)(2,1)S(1)}, u32[]{:S(2)}, u32[]{:S(2)}) collective-permute-start(bf16[256,384]{1,0:T(8,128)(2,1)S(1)} %constant_dynamic-update-slice_fusion.refs_0_), channel_id=1, source_target_pairs={{0,2},{1,3},{2,0},{3,1},{4,6},{5,7},{6,4},{7,5},{8,10},{9,11},{10,... | collective-permute-start | bytes 589832 | tf_op jit(solution)/shard_map/ppermute | solution.py:442
  48.2 11.8 %collective-permute-start.5 = (bf16[256,384]{1,0:T(8,128)(2,1)S(1)}, bf16[256,384]{1,0:T(8,128)(2,1)S(1)}, u32[]{:S(2)}, u32[]{:S(2)}) collective-permute-start(bf16[256,384]{1,0:T(8,128)(2,1)S(1)} %constant_dynamic-update-slice_fusion.refs_0_), channel_id=1, source_target_pairs={{0,4},{1,5},{2,6},{3,7},{4,0},{5,1},{6,2},{7,3},{8,12},{9,13},{10,... | collective-permute-start | bytes 589832 | tf_op jit(solution)/shard_map/ppermute | solution.py:442
  50.7 12.0 %collective-permute-start.8 = (bf16[256,384]{1,0:T(8,128)(2,1)S(1)}, bf16[256,384]{1,0:T(8,128)(2,1)S(1)}, u32[]{:S(2)}, u32[]{:S(2)}) collective-permute-start(bf16[256,384]{1,0:T(8,128)(2,1)S(1)} %constant_dynamic-update-slice_fusion.refs_0_), channel_id=1, source_target_pairs={{0,1},{1,0},{2,3},{3,2},{4,5},{5,4},{6,7},{7,6},{8,9},{9,8},{10,11... | collective-permute-start | bytes 589832 | tf_op jit(solution)/shard_map/ppermute | solution.py:442
  54.3 8.4 %collective-permute-start.11 = (bf16[256,384]{1,0:T(8,128)(2,1)S(1)}, bf16[256,384]{1,0:T(8,128)(2,1)S(1)}, u32[]{:S(2)}, u32[]{:S(2)}) collective-permute-start(bf16[256,384]{1,0:T(8,128)(2,1)S(1)} %collective-permute-done.7.refs_3_), channel_id=1, source_target_pairs={{0,1},{1,0},{2,3},{3,2},{4,5},{5,4},{6,7},{7,6},{8,9},{9,8},{10,11... | collective-permute-start | bytes 589832 | tf_op jit(solution)/shard_map/ppermute | solution.py:442
  58.0 4.8 %collective-permute-start.10 = (bf16[256,384]{1,0:T(8,128)(2,1)S(1)}, bf16[256,384]{1,0:T(8,128)(2,1)S(1)}, u32[]{:S(2)}, u32[]{:S(2)}) collective-permute-start(bf16[256,384]{1,0:T(8,128)(2,1)S(1)} %collective-permute-done.6.refs_2_), channel_id=1, source_target_pairs={{0,1},{1,0},{2,3},{3,2},{4,5},{5,4},{6,7},{7,6},{8,9},{9,8},{10,11... | collective-permute-start | bytes 589832 | tf_op jit(solution)/shard_map/ppermute | solution.py:442
  60.0 2.7 %collective-permute-start.9 = (bf16[256,384]{1,0:T(8,128)(2,1)S(1)}, bf16[256,384]{1,0:T(8,128)(2,1)S(1)}, u32[]{:S(2)}, u32[]{:S(2)}) collective-permute-start(bf16[256,384]{1,0:T(8,128)(2,1)S(1)} %collective-permute-done.5.refs_1_), channel_id=1, source_target_pairs={{0,1},{1,0},{2,3},{3,2},{4,5},{5,4},{6,7},{7,6},{8,9},{9,8},{10,11... | collective-permute-start | bytes 589832 | tf_op jit(solution)/shard_map/ppermute | solution.py:442
  (4 other events, 19.3 us)
